TPU v7x, 32 devices: a whole 2x2x4 slice. The times are simulated.
32 devices in a mesh: groups: 2 (over y), vocab: 16 (over z, x, core).
Axes of the slice: x: 2, y: 2, z: 4, core: 2. Of those that a mesh axis runs over, the one named last changes fastest.
Arguments:
- hidden: bfloat16 [128, 4096], P(('groups', 'vocab')), parts along dimension 0, may hold values from -2048 to 2048
- embedding: bfloat16 [16384, 4096], P(('groups', 'vocab')), parts along dimension 0, may hold values from -0.28125 to 0.28125
- d_input: bfloat16 [128, 4096], P(('groups', 'vocab')), parts along dimension 0, may hold values from -6 to 6
- input_ids: int32 [128], P('groups'), parts along dimension 0, may hold values from 0 to 8191
- language: int32 [128], P('groups'), parts along dimension 0, may hold values from 0 to 15
- allowed: int32 [32, 16], P('groups'), parts along dimension 0, may hold values from 0 to 1, as said below
- target: int32 [128], P('groups'), parts along dimension 0, may hold values from 0 to 8191, as said below
- token_weight: float32 [128], P('groups'), parts along dimension 0, may hold values from 4 to 32
Outputs:
- d_hidden: bfloat16 [128, 4096], P(('groups', 'vocab')), parts along dimension 0
- d_embed: bfloat16 [16384, 4096], P(('groups', 'vocab')), parts along dimension 0
There are 2 independent parts, one for each index of `groups`. A program takes and returns all parts, laid end to end along the dimension named above; each array names one. Nothing has to cross between parts.
Inputs may be any that keep to these rules, and one draw needn't show every extreme that they name: `allowed`: every language allows at least one block. Each target lies in a block allowed for its token's language.
All inputs are finite; a program needn't handle non-finite values.
Results may differ from a plain program's by a relative error of at most 0.005.
Values may be sent and summed in bfloat16 or wider, within the bound.
No kernel may reach another device: no remote copies, remote signals or barrier semaphores. Data moves between devices by JAX's collectives and lax.ppermute only.
A program may use at most 128 MiB of HBM per device.

v0:
```python
import jax
import jax.numpy as jnp
from jax import lax
from jax.sharding import PartitionSpec as P


def per_device(hidden, embedding, d_input, input_ids, language, allowed, target, token_weight):
    block_cols = embedding.shape[0]
    rank_here = lax.axis_index("vocab")
    all_hidden, all_input = (
        lax.all_gather(hidden, "vocab", axis=0, tiled=True),
        lax.all_gather(d_input, "vocab", axis=0, tiled=True),
    )
    logits = lax.dot_general(
        all_hidden, embedding, (((1,), (1,)), ((), ())), preferred_element_type=jnp.float32
    )
    lang_allows = lax.dynamic_slice_in_dim(allowed, rank_here, 1, 1)[:, 0]
    lang_count = allowed.shape[0]
    matches = language[:, None] == jnp.arange(lang_count, dtype=jnp.int32)[None, :]
    row_ok = jnp.sum(jnp.where(matches, lang_allows[None, :], 0), axis=1) > 0
    masked = jnp.where(row_ok[:, None], logits, jnp.float32(-1e30))
    row_max = lax.pmax(jnp.max(masked, axis=1), "vocab")
    shifted = jnp.exp(masked - row_max[:, None])
    local_total = jnp.sum(jnp.where(row_ok[:, None], shifted, jnp.float32(0.0)), axis=1)
    row_total = lax.psum(local_total, "vocab")
    columns = rank_here * block_cols + jnp.arange(block_cols, dtype=jnp.int32)
    onehot = (columns[None, :] == target[:, None]).astype(jnp.float32)
    d_logits = jnp.where(
        row_ok[:, None],
        token_weight[:, None] * (shifted / row_total[:, None] - onehot),
        jnp.float32(0.0),
    ).astype(jnp.bfloat16)
    d_hidden = lax.psum_scatter(
        jnp.dot(d_logits, embedding, preferred_element_type=jnp.float32),
        "vocab",
        scatter_dimension=0,
        tiled=True,
    ).astype(jnp.bfloat16)
    head = lax.dot_general(
        d_logits, all_hidden, (((0,), (0,)), ((), ())), preferred_element_type=jnp.float32
    )
    local_rows = input_ids - rank_here * block_cols
    valid = (local_rows >= 0) & (local_rows < block_cols)
    local_rows = jnp.where(valid, local_rows, block_cols)
    head = head.at[local_rows].add(all_input.astype(jnp.float32), mode="drop")
    return (d_hidden, head.astype(jnp.bfloat16))


def solution(mesh):
    placed = (
        P(("groups", "vocab"), None),
        P(("groups", "vocab"), None),
        P(("groups", "vocab"), None),
        P("groups"),
        P("groups"),
        P("groups", None),
        P("groups"),
        P("groups"),
    )
    return jax.shard_map(
        per_device,
        mesh=mesh,
        in_specs=placed,
        out_specs=(P(("groups", "vocab"), None), P(("groups", "vocab"), None)),
        check_vma=False,
    )
```

profile of v0, /device:TPU:0, one launch (start us, length us, event | category | flops | bytes accessed | tf_op | source)
XLA Modules:
  0.0 204.9 jit_solution(8653944772240307747)
XLA Ops:
  0.6 0.0 copy-start
  0.6 0.0 copy-start.1
  0.7 1.2 dynamic-slice
  2.6 0.0 copy-done
  2.6 0.2 dynamic-slice_reduce_fusion
  2.8 0.7 select_reduce_fusion.1
  3.5 0.7 compare_select_fusion
  4.2 24.8 %all-gather = bf16[16,4,4096]{2,1,0:T(4,128)(2,1)S(1)} all-gather(bf16[1,4,4096]{2,1,0:T(4,128)(2,1)} %bitcast.7), channel_id=1, replica_groups=mesh['groups'=2,'vocab'=16] {'vocab'}, dimensions={0}, use_global_device_ids=true | all-gather | bytes 557056 | tf_op jit(solution)/shard_map/all_gather | solution.py:11
  28.9 0.0 copy-start.2
  29.0 0.0 copy-start.3
  29.0 0.1 reshape.27
  29.1 3.7 %fusion.2 = (f32[64]{0:T(128)S(1)}, f32[64,512]{1,0:T(8,128)S(1)}) fusion(bf16[64,4096]{1,0:T(8,128)(2,1)S(1)} %reshape.27, bf16[512,4096]{1,0:T(8,128)(2,1)} %param.9, pred[64]{0:T(512)(128)(4,1)S(1)} %broadcast_compare_fusion), kind=kOutput, calls=%fused_computation.15 | convolution fusion | flops 268500928 | bytes 4849984 | tf_op jit(solution)/shard_map/dot_general | solution.py:14
  32.8 29.8 %pmax.7 = f32[64]{0:T(128)S(1)} all-reduce(f32[64]{0:T(128)S(1)} %get-tuple-element.2), channel_id=1, replica_groups=mesh['groups'=2,'vocab'=16] {'vocab'}, use_global_device_ids=true, to_apply=%region_2.3 | all-reduce | flops 64 | bytes 512 | tf_op jit(solution)/shard_map/pmax | solution.py:22
  62.6 0.2 select_reduce_fusion
  62.8 29.5 %psum.7 = f32[64]{0:T(128)S(1)} all-reduce(f32[64]{0:T(128)S(1)} %select_reduce_fusion), channel_id=1, replica_groups=mesh['groups'=2,'vocab'=16] {'vocab'}, use_global_device_ids=true, to_apply=%region_4.5 | all-reduce | flops 64 | bytes 512 | tf_op jit(solution)/shard_map/psum | solution.py:25
  92.3 0.0 copy-done.1
  92.3 18.7 %all-gather.1 = bf16[16,4,4096]{2,1,0:T(4,128)(2,1)S(1)} all-gather(bf16[1,4,4096]{2,1,0:T(4,128)(2,1)S(1)} %bitcast.8), channel_id=1, replica_groups=mesh['groups'=2,'vocab'=16] {'vocab'}, dimensions={0}, use_global_device_ids=true | all-gather | bytes 557056 | tf_op jit(solution)/shard_map/all_gather | solution.py:12
  111.0 0.1 reshape.30
  111.1 0.0 copy-done.2
  111.1 0.0 copy-done.3
  111.1 3.1 %fusion.1 = f32[64,4096]{1,0:T(8,128)S(1)} fusion(bf16[512,4096]{1,0:T(8,128)(2,1)} %param.9, f32[64,512]{1,0:T(8,128)S(1)} %get-tuple-element.3, s32[512]{0:T(512)S(1)} %iota_add_fusion, f32[64]{0:T(128)S(1)} %psum.7, f32[64]{0:T(128)S(1)} %pmax.7, f32[64]{0:T(128)S(1)} %copy-done.2, s32[64]{0:T(128)S(1)} %copy-done.3, ...), kind=kOutput, calls=%fused_computation.14 | convolution fusion | flops 268697600 | bytes 5377088 | tf_op jit(solution)/shard_map/dot_general | solution.py:34
  114.2 70.9 %all-reduce.2 = bf16[64,4096]{1,0:T(8,128)(2,1)S(1)} all-reduce(f32[64,4096]{1,0:T(8,128)S(1)} %fusion.1), channel_id=2, replica_groups=mesh['groups'=2,'vocab'=16] {'vocab'}, use_global_device_ids=true, to_apply=%region_5.6.clone | all-reduce | flops 262144 | bytes 1572864
  185.1 0.6 dynamic-slice_convert_fusion
  185.8 4.6 %fusion = f32[512,4096]{1,0:T(8,128)} fusion(bf16[64,4096]{1,0:T(8,128)(2,1)S(1)} %reshape.27, f32[64,512]{1,0:T(8,128)S(1)} %get-tuple-element.3, s32[512]{0:T(512)S(1)} %iota_add_fusion, f32[64]{0:T(128)S(1)} %psum.7, f32[64]{0:T(128)S(1)} %pmax.7, f32[64]{0:T(128)S(1)} %copy-done.2, s32[64]{0:T(128)S(1)} %copy-done.3, ...), kind=kOutput, calls=%fused_computation.13 | convolution fusion | flops 268697600 | bytes 9047104 | tf_op jit(solution)/shard_map/dot_general | solution.py:39
  190.4 8.5 %scatter_fusion = f32[512,4096]{1,0:T(8,128)} fusion(f32[512,4096]{1,0:T(8,128)} %fusion, s32[64]{0:T(128)S(1)} %compare_select_fusion, f32[64,4096]{1,0:T(8,128)S(1)} %reshape.30), kind=kCustom, calls=%fused_computation | custom fusion | flops 262144 | bytes 3145984 | tf_op jit(solution)/shard_map/scatter-add | solution.py:45
  198.8 6.0 %convert_element_type.19 = bf16[512,4096]{1,0:T(8,128)(2,1)} convert(f32[512,4096]{1,0:T(8,128)} %scatter_fusion) | non-fusion elementwise | flops 2097152 | bytes 12582912 | tf_op jit(solution)/shard_map/convert_element_type | solution.py:46
  (2 shorter events, 0.0 us)
Async XLA Ops:
  0.6 1.9 copy-start
  0.6 91.6 %copy-start.1 = (bf16[4,4096]{1,0:T(4,128)(2,1)S(1)}, bf16[4,4096]{1,0:T(4,128)(2,1)}, u32[]{:S(2)}) copy-start(bf16[4,4096]{1,0:T(4,128)(2,1)} %param.10) | copy-start | bytes 98308
  28.9 82.1 %copy-start.2 = (f32[64]{0:T(128)S(1)}, f32[64]{0:T(128)}, u32[]{:S(2)}) copy-start(f32[64]{0:T(128)} %param.15) | copy-start | bytes 772
  29.0 82.1 %copy-start.3 = (s32[64]{0:T(128)S(1)}, s32[64]{0:T(128)}, u32[]{:S(2)}) copy-start(s32[64]{0:T(128)} %param.14) | copy-start | bytes 772
where the time goes:
time: 205 us
  blocking collectives  174 us (85%)
  other arithmetic  16.1 us (8%)
  matrix products  11.4 us (6%)
  local copies, waits for them, and re-layouts  2.28 us (1%)
    unnamed x1, blocking collectives  70.9 us
    pmax x1, blocking collectives, per_device(): row_max = lax.pmax(jnp.max(masked, axis=1), 'vocab')  29.8 us
    psum x1, blocking collectives, per_device(): row_total = lax.psum(local_total, 'vocab')  29.5 us
    all_gather x1, blocking collectives, per_device(): lax.all_gather(hidden, 'vocab', axis=0, tiled=True)  24.8 us
    all_gather x1, blocking collectives, per_device(): lax.all_gather(d_input, 'vocab', axis=0, tiled=True)  18.7 us
    scatter-add x1, other arithmetic, per_device(): head = head.at[local_rows].add(all_input.astype(jnp.float32), mode='drop')  8.45 us
    convert_element_type x1, other arithmetic, per_device(): return (d_hidden, head.astype(jnp.bfloat16))  6.02 us
    dot_general x1, matrix products, per_device(): lax.dot_general(d_logits, all_hidden, (((0,), (0,)), ((), ())), preferred...  4.6 us

commit v1 on v0

v1 whole, which is shorter than its diff:
```python
import jax
import jax.numpy as jnp
from jax import lax
from jax.sharding import PartitionSpec as P

NEG = -1e30


def per_device(n, hidden, embedding, d_input, input_ids, language, allowed, target, token_weight):
    f32, bf16 = jnp.float32, jnp.bfloat16
    cols, width = embedding.shape
    mine = hidden.shape[0]
    tokens = mine * n
    steps = n.bit_length() - 1
    me = lax.axis_index("vocab")

    def swap(x, k):
        return lax.ppermute(x, "vocab", [(i, i ^ k) for i in range(n)])

    def bit(k):
        return (me & k) != 0

    def order(x):
        y = x.reshape((2,) * steps + (mine,) + x.shape[1:])
        perm = tuple(range(steps))[::-1] + tuple(range(steps, y.ndim))
        return y.transpose(perm).reshape(x.shape)

    def gather(x):
        k = n // 2
        while k:
            r = swap(x, k)
            x = jnp.where(bit(k), jnp.concatenate([r, x], 0), jnp.concatenate([x, r], 0))
            k //= 2
        return x

    def halves(x, k):
        h = x.shape[0] // 2
        a, b = x[:h], x[h:]
        return jnp.where(bit(k), b, a), jnp.where(bit(k), a, b)

    target, language, input_ids, weight = order(target), order(language), order(input_ids), order(token_weight)
    lang_allows = lax.dynamic_slice_in_dim(allowed, me, 1, 1)[:, 0]
    matches = language[:, None] == jnp.arange(allowed.shape[0], dtype=jnp.int32)[None, :]
    row_ok = jnp.sum(jnp.where(matches, lang_allows[None, :], 0), axis=1) > 0
    columns = me * cols + jnp.arange(cols, dtype=jnp.int32)
    is_target = columns[None, :] == target[:, None]

    rows = jnp.dot(is_target.astype(bf16), embedding, preferred_element_type=f32).astype(bf16)
    k = 1
    while k < n:
        keep, send = halves(rows, k)
        rows = keep + swap(send, k)
        k *= 2

    all_hidden = gather(hidden)
    all_input = gather(d_input)

    logits = lax.dot_general(all_hidden, embedding, (((1,), (1,)), ((), ())), preferred_element_type=f32)
    masked = jnp.where(row_ok[:, None], logits, f32(NEG))
    m = jnp.max(masked, axis=1)
    p = jnp.where(row_ok[:, None], jnp.exp(masked - m[:, None]), f32(0.0))
    s = jnp.sum(p, axis=1)
    lt = jnp.max(jnp.where(is_target, masked, f32(NEG)), axis=1)
    part = jnp.dot(jnp.where(is_target, f32(0.0), p).astype(bf16), embedding, preferred_element_type=f32)

    lo = 0
    k = 1
    while k < n:
        got = swap(jnp.stack([m, s, lt]), k)
        m_new = jnp.maximum(m, got[0])
        a, b = jnp.exp(m - m_new), jnp.exp(got[0] - m_new)
        s = s * a + got[1] * b
        lt = jnp.maximum(lt, got[2])
        keep, send = halves(part, k)
        recv = swap(send.astype(bf16), k).astype(f32)
        size = keep.shape[0]
        lo = lo + jnp.where(bit(k), size, 0)
        part = keep * lax.dynamic_slice_in_dim(a, lo, size)[:, None] + recv * lax.dynamic_slice_in_dim(b, lo, size)[:, None]
        m = m_new
        k *= 2

    d_logits = jnp.where(
        row_ok[:, None],
        weight[:, None] * (jnp.exp(masked - m[:, None]) / s[:, None] - is_target.astype(f32)),
        f32(0.0),
    ).astype(bf16)
    coef = (weight * (jnp.exp(lt - m) / s - 1.0)).astype(bf16).astype(f32)
    scale = weight / s
    d_hidden = (
        part * lax.dynamic_slice_in_dim(scale, lo, mine)[:, None]
        + rows.astype(f32) * lax.dynamic_slice_in_dim(coef, lo, mine)[:, None]
    ).astype(bf16)
    took = (columns[None, :] == input_ids[:, None]).astype(bf16)
    d_embed = lax.dot_general(
        jnp.concatenate([d_logits, took], 0),
        jnp.concatenate([all_hidden, all_input], 0),
        (((0,), (0,)), ((), ())),
        preferred_element_type=f32,
    ).astype(bf16)
    return d_hidden, d_embed


def solution(mesh):
    n = mesh.shape["vocab"]
    placed = (
        P(("groups", "vocab"), None),
        P(("groups", "vocab"), None),
        P(("groups", "vocab"), None),
        P("groups"),
        P("groups"),
        P("groups", None),
        P("groups"),
        P("groups"),
    )
    return jax.shard_map(
        lambda *args: per_device(n, *args),
        mesh=mesh,
        in_specs=placed,
        out_specs=(P(("groups", "vocab"), None), P(("groups", "vocab"), None)),
        check_vma=False,
    )
```

time: 205 us -> 62.8 us (0.31)
  blocking collectives: 174 us -> 0 us
  waiting for transfers between devices: 0 us -> 24.6 us
  starting transfers between devices: 0 us -> 23.4 us
  other arithmetic: 16.1 us -> 2.41 us
  matrix products: 11.4 us -> 8.75 us
    unnamed x1 -> x0, blocking collectives: 70.9 us -> none
    all_gather x2 -> x0, blocking collectives: 43.5 us -> none  [the longest x1 24.8 us: per_device(): lax.all_gather(hidden, 'vocab', axis=0, tiled=True)]
    pmax x1 -> x0, blocking collectives: 29.8 us -> none  [per_device(): row_max = lax.pmax(jnp.max(masked, axis=1), 'vocab')]
    psum x1 -> x0, blocking collectives: 29.5 us -> none  [per_device(): row_total = lax.psum(local_total, 'vocab')]
    ppermute x0 -> x20, waiting for transfers between devices: none -> 24.6 us  [swap(): return lax.ppermute(x, 'vocab', [(i, i ^ k) for i in range(n)])]
    ppermute x0 -> x20, starting transfers between devices: none -> 23.4 us  [swap(): return lax.ppermute(x, 'vocab', [(i, i ^ k) for i in range(n)])]
    scatter-add x1 -> x0, other arithmetic: 8.45 us -> none  [per_device(): head = head.at[local_rows].add(all_input.astype(jnp.float32), mode='drop')]
    convert_element_type x1 -> x8, other arithmetic: 6.02 us -> 1.05 us  [the longest x1 0.72 us: per_device(): d_hidden = (part * lax.dynamic_slice_in_dim(scale, lo, mine)[:, None] + r...]
  transfers between devices with their start and end apart: 0 -> 20, of which waited for: 0 -> 10; matrix products, arithmetic and copies ran while one was open for 0% -> 20% of each run, Pallas kernels for 0% -> 0%
where the time goes in v1:
time: 62.8 us; the launch traced here: 62.6 us
  waiting for transfers between devices  24.6 us (39%)
  starting transfers between devices  23.4 us (37%)
  matrix products  8.75 us (14%)
  other arithmetic  2.41 us (4%)
  local copies, waits for them, and re-layouts  2.37 us (4%)
  between operations  1.08 us (2%)
    ppermute x20, waiting for transfers between devices, swap(): return lax.ppermute(x, 'vocab', [(i, i ^ k) for i in range(n)])  24.6 us
    ppermute x20, starting transfers between devices, swap(): return lax.ppermute(x, 'vocab', [(i, i ^ k) for i in range(n)])  23.4 us
    dot_general x1, matrix products, per_device(): lax.dot_general(jnp.concatenate([d_logits, took], 0), jnp.concatenate([al...  3.29 us
    dot_general x1, matrix products, per_device(): jnp.dot(is_target.astype(bf16), embedding, preferred_element_type=f32)  3.08 us
    dot_general x1, matrix products, per_device(): lax.dot_general(all_hidden, embedding, (((1,), (1,)), ((), ())), preferre...  1.49 us
  transfers between devices with their start and end apart: 20, of which 10 were waited for; matrix products, arithmetic and copies ran while one was open for 20% of the time, Pallas kernels for 0%

profile of v1, /device:TPU:0, one launch (start us, length us, event | category | flops | bytes accessed | tf_op | source)
XLA Modules:
  0.0 62.6 jit_solution(12472080156256121289)
XLA Ops:
  0.7 4.1 %collective-permute-start = (bf16[4,4096]{1,0:T(4,128)(2,1)}, bf16[4,4096]{1,0:T(4,128)(2,1)S(1)}, u32[]{:S(2)}, u32[]{:S(2)}) collective-permute-start(bf16[4,4096]{1,0:T(4,128)(2,1)} %param.8), channel_id=1, source_target_pairs={{0,8},{1,9},{2,10},{3,11},{4,12},{5,13},{6,14},{7,15},{8,0},{9,1},... | collective-permute-start | bytes 98312 | tf_op jit(solution)/shard_map/ppermute | solution.py:18
  4.9 0.7 %reshape.148 = s32[2,2,2,2,4]{4,3,2,1,0:T(2,128)S(1)} reshape(s32[64]{0:T(128)} %param.14) | data formatting | bytes 512 | tf_op jit(solution)/shard_map/reshape | solution.py:24
  5.6 0.1 eq.44
  5.7 3.1 %convolution_convert_fusion.1 = bf16[64,4096]{1,0:T(8,128)(2,1)S(1)} fusion(bf16[512,4096]{1,0:T(8,128)(2,1)} %param.9, s32[512]{0:T(512)S(1)} %iota_add_fusion, s32[64]{0:T(128)S(1)} %eq.44), kind=kOutput, calls=%fused_computation.1 | convolution fusion | flops 268730368 | bytes 4720896 | tf_op jit(solution)/shard_map/dot_general | solution.py:48
  8.9 0.1 reshape.152
  9.1 0.1 eq.51
  9.2 0.1 reshape.149
  9.3 0.1 eq.47
  9.4 0.1 compare_convert_fusion.1
  9.5 0.2 dynamic-slice_reduce_fusion
  9.6 0.1 select_reduce_fusion
  9.8 0.1 reshape.150
  9.9 0.1 reshape.151
  10.1 1.9 %collective-permute-start.1 = (bf16[8,4096]{1,0:T(8,128)(2,1)S(1)}, bf16[8,4096]{1,0:T(8,128)(2,1)S(1)}, u32[]{:S(2)}, u32[]{:S(2)}) collective-permute-start(bf16[8,4096]{1,0:T(8,128)(2,1)S(1)} %maximum_select_fusion.6), channel_id=1, source_target_pairs={{0,4},{1,5},{2,6},{3,7},{4,0},{5,1},{6,2},{7,3},{8,12},{9,13},{10,... | collective-permute-start | bytes 196616 | tf_op jit(solution)/shard_map/ppermute | solution.py:18
  12.1 0.3 collective-permute-start.17
  12.3 2.4 %collective-permute-done.1 = bf16[8,4096]{1,0:T(8,128)(2,1)S(1)} collective-permute-done((bf16[8,4096]{1,0:T(8,128)(2,1)S(1)}, bf16[8,4096]{1,0:T(8,128)(2,1)S(1)}, u32[]{:S(2)}, u32[]{:S(2)}) %collective-permute-start.1) | collective-permute-done | bytes 65568 | tf_op jit(solution)/shard_map/ppermute | solution.py:18
  14.8 1.7 %collective-permute-start.2 = (bf16[16,4096]{1,0:T(8,128)(2,1)S(1)}, bf16[16,4096]{1,0:T(8,128)(2,1)S(1)}, u32[]{:S(2)}, u32[]{:S(2)}) collective-permute-start(bf16[16,4096]{1,0:T(8,128)(2,1)S(1)} %maximum_select_fusion.4), channel_id=1, source_target_pairs={{0,2},{1,3},{2,0},{3,1},{4,6},{5,7},{6,4},{7,5},{8,10},{9,11},{10,... | collective-permute-start | bytes 393224 | tf_op jit(solution)/shard_map/ppermute | solution.py:18
  16.5 1.5 %collective-permute-start.18 = (bf16[16,4096]{1,0:T(8,128)(2,1)S(1)}, bf16[16,4096]{1,0:T(8,128)(2,1)S(1)}, u32[]{:S(2)}, u32[]{:S(2)}) collective-permute-start(bf16[16,4096]{1,0:T(8,128)(2,1)S(1)} %maximum_select_fusion.5), channel_id=1, source_target_pairs={{0,2},{1,3},{2,0},{3,1},{4,6},{5,7},{6,4},{7,5},{8,10},{9,11},{10,... | collective-permute-start | bytes 393224 | tf_op jit(solution)/shard_map/ppermute | solution.py:18
  18.0 0.7 %collective-permute-start.13 = (bf16[16,4096]{1,0:T(8,128)(2,1)S(1)}, bf16[16,4096]{1,0:T(8,128)(2,1)S(1)}, u32[]{:S(2)}, u32[]{:S(2)}) collective-permute-start(bf16[16,4096]{1,0:T(8,128)(2,1)S(1)} %broadcast_select_fusion.1), channel_id=1, source_target_pairs={{0,2},{1,3},{2,0},{3,1},{4,6},{5,7},{6,4},{7,5},{8,10},{9,11},{10,... | collective-permute-start | bytes 393224 | tf_op jit(solution)/shard_map/ppermute | solution.py:18
  18.7 5.3 %collective-permute-done.18 = bf16[16,4096]{1,0:T(8,128)(2,1)S(1)} collective-permute-done((bf16[16,4096]{1,0:T(8,128)(2,1)S(1)}, bf16[16,4096]{1,0:T(8,128)(2,1)S(1)}, u32[]{:S(2)}, u32[]{:S(2)}) %collective-permute-start.18) | collective-permute-done | bytes 131104 | tf_op jit(solution)/shard_map/ppermute | solution.py:18
  24.2 1.5 %collective-permute-done.13 = bf16[16,4096]{1,0:T(8,128)(2,1)S(1)} collective-permute-done((bf16[16,4096]{1,0:T(8,128)(2,1)S(1)}, bf16[16,4096]{1,0:T(8,128)(2,1)S(1)}, u32[]{:S(2)}, u32[]{:S(2)}) %collective-permute-start.13) | collective-permute-done | bytes 131104 | tf_op jit(solution)/shard_map/ppermute | solution.py:18
  25.7 1.7 %collective-permute-start.14 = (bf16[8,4096]{1,0:T(8,128)(2,1)S(1)}, bf16[8,4096]{1,0:T(8,128)(2,1)S(1)}, u32[]{:S(2)}, u32[]{:S(2)}) collective-permute-start(bf16[8,4096]{1,0:T(8,128)(2,1)S(1)} %broadcast_select_fusion.2), channel_id=1, source_target_pairs={{0,4},{1,5},{2,6},{3,7},{4,0},{5,1},{6,2},{7,3},{8,12},{9,13},{10,... | collective-permute-start | bytes 196616 | tf_op jit(solution)/shard_map/ppermute | solution.py:18
  27.5 2.5 %collective-permute-done.14 = bf16[8,4096]{1,0:T(8,128)(2,1)S(1)} collective-permute-done((bf16[8,4096]{1,0:T(8,128)(2,1)S(1)}, bf16[8,4096]{1,0:T(8,128)(2,1)S(1)}, u32[]{:S(2)}, u32[]{:S(2)}) %collective-permute-start.14) | collective-permute-done | bytes 65568 | tf_op jit(solution)/shard_map/ppermute | solution.py:18
  30.1 0.1 maximum_select_fusion
  30.2 1.5 %fusion.45 = (f32[64]{0:T(128)S(1)}, f32[64,512]{1,0:T(8,128)S(1)}) fusion(bf16[64,4096]{1,0:T(8,128)(2,1)S(1)} %maximum_select_fusion, bf16[512,4096]{1,0:T(8,128)(2,1)S(1)} %copy-done.1, pred[64]{0:T(512)(128)(4,1)S(1)} %broadcast_compare_fusion), kind=kOutput, calls=%fused_computation.109 | convolution fusion | flops 268500928 | bytes 4849984 | tf_op jit(solution)/shard_map/dot_general | solution.py:58
  31.7 0.2 fusion.13
  32.0 2.7 %collective-permute-start.15 = (bf16[4,4096]{1,0:T(4,128)(2,1)S(1)}, bf16[4,4096]{1,0:T(4,128)(2,1)S(1)}, u32[]{:S(2)}, u32[]{:S(2)}) collective-permute-start(bf16[4,4096]{1,0:T(4,128)(2,1)S(1)} %broadcast_select_fusion.3), channel_id=1, source_target_pairs={{0,8},{1,9},{2,10},{3,11},{4,12},{5,13},{6,14},{7,15},{8,0},{9,1},... | collective-permute-start | bytes 98312 | tf_op jit(solution)/shard_map/ppermute | solution.py:18
  34.8 1.6 %collective-permute-start.6 = (f32[3,64]{1,0:T(4,128)S(1)}, f32[3,64]{1,0:T(4,128)S(1)}, u32[]{:S(2)}, u32[]{:S(2)}) collective-permute-start(f32[3,64]{1,0:T(4,128)S(1)} %pad_maximum_fusion.1), channel_id=1, source_target_pairs={{0,2},{1,3},{2,0},{3,1},{4,6},{5,7},{6,4},{7,5},{8,10},{9,11},{10,... | collective-permute-start | bytes 2312 | tf_op jit(solution)/shard_map/ppermute | solution.py:18
  36.3 0.9 %fusion.14 = f32[64,4096]{1,0:T(8,128)S(1)} fusion(bf16[512,4096]{1,0:T(8,128)(2,1)S(1)} %copy-done.1, f32[64,512]{1,0:T(8,128)S(1)} %get-tuple-element.25, f32[64]{0:T(128)S(1)} %get-tuple-element.24, s32[512]{0:T(512)S(1)} %iota_add_fusion, s32[64]{0:T(128)S(1)} %eq.44, pred[64]{0:T(512)(128)(4,1)S(1)} %broadcast_compare_fusion), kind=kOutput, calls=%fused_computation.38 | convolution fusion | flops 268599296 | bytes 5376576 | tf_op jit(solution)/shard_map/dot_general | solution.py:64
  37.2 1.2 %collective-permute-done.6 = f32[3,64]{1,0:T(4,128)S(1)} collective-permute-done((f32[3,64]{1,0:T(4,128)S(1)}, f32[3,64]{1,0:T(4,128)S(1)}, u32[]{:S(2)}, u32[]{:S(2)}) %collective-permute-start.6) | collective-permute-done | bytes 800 | tf_op jit(solution)/shard_map/ppermute | solution.py:18
  38.4 1.6 %collective-permute-start.8 = (f32[3,64]{1,0:T(4,128)S(1)}, f32[3,64]{1,0:T(4,128)S(1)}, u32[]{:S(2)}, u32[]{:S(2)}) collective-permute-start(f32[3,64]{1,0:T(4,128)S(1)} %pad_maximum_fusion.2), channel_id=1, source_target_pairs={{0,4},{1,5},{2,6},{3,7},{4,0},{5,1},{6,2},{7,3},{8,12},{9,13},{10,... | collective-permute-start | bytes 2312 | tf_op jit(solution)/shard_map/ppermute | solution.py:18
  40.2 1.9 %collective-permute-done.8 = f32[3,64]{1,0:T(4,128)S(1)} collective-permute-done((f32[3,64]{1,0:T(4,128)S(1)}, f32[3,64]{1,0:T(4,128)S(1)}, u32[]{:S(2)}, u32[]{:S(2)}) %collective-permute-start.8) | collective-permute-done | bytes 800 | tf_op jit(solution)/shard_map/ppermute | solution.py:18
  42.1 1.1 %collective-permute-start.10 = (f32[3,64]{1,0:T(4,128)S(1)}, f32[3,64]{1,0:T(4,128)S(1)}, u32[]{:S(2)}, u32[]{:S(2)}) collective-permute-start(f32[3,64]{1,0:T(4,128)S(1)} %pad_maximum_fusion.3), channel_id=1, source_target_pairs={{0,8},{1,9},{2,10},{3,11},{4,12},{5,13},{6,14},{7,15},{8,0},{9,1},... | collective-permute-start | bytes 2312 | tf_op jit(solution)/shard_map/ppermute | solution.py:18
  43.2 0.1 maximum_select_fusion.1
  43.3 3.4 %collective-permute-done.10 = f32[3,64]{1,0:T(4,128)S(1)} collective-permute-done((f32[3,64]{1,0:T(4,128)S(1)}, f32[3,64]{1,0:T(4,128)S(1)}, u32[]{:S(2)}, u32[]{:S(2)}) %collective-permute-start.10) | collective-permute-done | bytes 800 | tf_op jit(solution)/shard_map/ppermute | solution.py:18
  46.7 0.1 dynamic_slice.36
  47.0 0.2 multiply_add_fusion
  47.2 1.6 %collective-permute-start.7 = (bf16[16,4096]{1,0:T(8,128)(2,1)S(1)}, bf16[16,4096]{1,0:T(8,128)(2,1)S(1)}, u32[]{:S(2)}, u32[]{:S(2)}) collective-permute-start(bf16[16,4096]{1,0:T(8,128)(2,1)S(1)} %select_convert_fusion.1), channel_id=1, source_target_pairs={{0,2},{1,3},{2,0},{3,1},{4,6},{5,7},{6,4},{7,5},{8,10},{9,11},{10,... | collective-permute-start | bytes 393224 | tf_op jit(solution)/shard_map/ppermute | solution.py:18
  48.7 0.1 fusion.9
  48.9 3.4 %collective-permute-done.7 = bf16[16,4096]{1,0:T(8,128)(2,1)S(1)} collective-permute-done((bf16[16,4096]{1,0:T(8,128)(2,1)S(1)}, bf16[16,4096]{1,0:T(8,128)(2,1)S(1)}, u32[]{:S(2)}, u32[]{:S(2)}) %collective-permute-start.7) | collective-permute-done | bytes 131104 | tf_op jit(solution)/shard_map/ppermute | solution.py:18
  52.2 0.1 multiply_add_fusion.1
  52.4 1.6 %collective-permute-start.9 = (bf16[8,4096]{1,0:T(8,128)(2,1)S(1)}, bf16[8,4096]{1,0:T(8,128)(2,1)S(1)}, u32[]{:S(2)}, u32[]{:S(2)}) collective-permute-start(bf16[8,4096]{1,0:T(8,128)(2,1)S(1)} %select_convert_fusion.2), channel_id=1, source_target_pairs={{0,4},{1,5},{2,6},{3,7},{4,0},{5,1},{6,2},{7,3},{8,12},{9,13},{10,... | collective-permute-start | bytes 196616 | tf_op jit(solution)/shard_map/ppermute | solution.py:18
  54.2 2.7 %collective-permute-done.9 = bf16[8,4096]{1,0:T(8,128)(2,1)S(1)} collective-permute-done((bf16[8,4096]{1,0:T(8,128)(2,1)S(1)}, bf16[8,4096]{1,0:T(8,128)(2,1)S(1)}, u32[]{:S(2)}, u32[]{:S(2)}) %collective-permute-start.9) | collective-permute-done | bytes 65568 | tf_op jit(solution)/shard_map/ppermute | solution.py:18
  56.9 0.1 multiply_add_fusion.2
  57.0 0.9 %collective-permute-start.11 = (bf16[4,4096]{1,0:T(4,128)(2,1)S(1)}, bf16[4,4096]{1,0:T(4,128)(2,1)S(1)}, u32[]{:S(2)}, u32[]{:S(2)}) collective-permute-start(bf16[4,4096]{1,0:T(4,128)(2,1)S(1)} %select_convert_fusion.3), channel_id=1, source_target_pairs={{0,8},{1,9},{2,10},{3,11},{4,12},{5,13},{6,14},{7,15},{8,0},{9,1},... | collective-permute-start | bytes 98312 | tf_op jit(solution)/shard_map/ppermute | solution.py:18
  57.9 3.3 %convolution_convert_fusion = bf16[512,4096]{1,0:T(8,128)(2,1)} fusion(bf16[64,4096]{1,0:T(8,128)(2,1)S(1)} %maximum_select_fusion.1, bf16[64,4096]{1,0:T(8,128)(2,1)S(1)} %maximum_select_fusion, bf16[64,512]{1,0:T(8,128)(2,1)S(1)} %compare_convert_fusion.1, bf16[64,512]{1,0:T(8,128)(2,1)S(1)} %fusion.9), kind=kOutput, calls=%fused_computation | convolution fusion | flops 541327360 | bytes 5373952 | tf_op jit(solution)/shard_map/dot_general | solution.py:94
  61.5 0.4 collective-permute-done.11
  61.9 0.7 %add_convert_fusion = bf16[4,4096]{1,0:T(4,128)(2,1)} fusion(bf16[4,4096]{1,0:T(4,128)(2,1)S(1)} %collective-permute-done.11, f32[8,4096]{1,0:T(8,128)S(1)} %multiply_add_fusion.2, f32[4]{0:T(128)S(1)} %dynamic_slice.43, bf16[4,4096]{1,0:T(4,128)(2,1)S(1)} %collective-permute-done.15, f32[4]{0:T(128)S(1)} %dynamic_slice.42, f32[4]{0:T(128)S(1)} %dynamic_slice.41, ...), kind=kLoop, calls=%fused_computation.41 | loop fusion | flops 196608 | bytes 294977 | tf_op jit(solution)/shard_map/convert_element_type | solution.py:92
  (71 shorter events, 1.9 us)
Async XLA Ops:
  0.6 8.8 %copy-start = (s32[16,16]{1,0:T(8,128)S(1)}, s32[16,16]{1,0:T(8,128)}, u32[]{:S(2)}) copy-start(s32[16,16]{1,0:T(8,128)} %param.13) | copy-start | bytes 3076
  0.6 9.4 %copy-start.2 = (bf16[4,4096]{1,0:T(4,128)(2,1)S(1)}, bf16[4,4096]{1,0:T(4,128)(2,1)}, u32[]{:S(2)}) copy-start(bf16[4,4096]{1,0:T(4,128)(2,1)} %param.8) | copy-start | bytes 98308
  0.7 11.3 %copy-start.3 = (bf16[4,4096]{1,0:T(4,128)(2,1)S(1)}, bf16[4,4096]{1,0:T(4,128)(2,1)}, u32[]{:S(2)}) copy-start(bf16[4,4096]{1,0:T(4,128)(2,1)} %param.10) | copy-start | bytes 98308
  0.7 8.3 %copy-start.4 = (s32[64]{0:T(128)S(1)}, s32[64]{0:T(128)}, u32[]{:S(2)}) copy-start(s32[64]{0:T(128)} %param.11) | copy-start | bytes 772
  0.7 8.5 %copy-start.5 = (s32[64]{0:T(128)S(1)}, s32[64]{0:T(128)}, u32[]{:S(2)}) copy-start(s32[64]{0:T(128)} %param.12) | copy-start | bytes 772
  0.7 9.1 %copy-start.6 = (f32[64]{0:T(128)S(1)}, f32[64]{0:T(128)}, u32[]{:S(2)}) copy-start(f32[64]{0:T(128)} %param.15) | copy-start | bytes 772
  0.7 9.3 %collective-permute-start = (bf16[4,4096]{1,0:T(4,128)(2,1)}, bf16[4,4096]{1,0:T(4,128)(2,1)S(1)}, u32[]{:S(2)}, u32[]{:S(2)}) collective-permute-start(bf16[4,4096]{1,0:T(4,128)(2,1)} %param.8), channel_id=1, source_target_pairs={{0,8},{1,9},{2,10},{3,11},{4,12},{5,13},{6,14},{7,15},{8,0},{9,1},... | collective-permute-start | bytes 98312 | tf_op jit(solution)/shard_map/ppermute | solution.py:18
  4.8 7.2 %collective-permute-start.16 = (bf16[4,4096]{1,0:T(4,128)(2,1)}, bf16[4,4096]{1,0:T(4,128)(2,1)S(1)}, u32[]{:S(2)}, u32[]{:S(2)}) collective-permute-start(bf16[4,4096]{1,0:T(4,128)(2,1)} %param.10), channel_id=1, source_target_pairs={{0,8},{1,9},{2,10},{3,11},{4,12},{5,13},{6,14},{7,15},{8,0},{9,1},... | collective-permute-start | bytes 98312 | tf_op jit(solution)/shard_map/ppermute | solution.py:18
  8.9 9.1 %collective-permute-start.12 = (bf16[32,4096]{1,0:T(8,128)(2,1)S(1)}, bf16[32,4096]{1,0:T(8,128)(2,1)S(1)}, u32[]{:S(2)}, u32[]{:S(2)}) collective-permute-start(bf16[32,4096]{1,0:T(8,128)(2,1)S(1)} %broadcast_select_fusion), channel_id=1, source_target_pairs={{0,1},{1,0},{2,3},{3,2},{4,5},{5,4},{6,7},{7,6},{8,9},{9,8},{10,11... | collective-permute-start | bytes 786440 | tf_op jit(solution)/shard_map/ppermute | solution.py:18
  10.0 20.2 %copy-start.1 = (bf16[512,4096]{1,0:T(8,128)(2,1)S(1)}, bf16[512,4096]{1,0:T(8,128)(2,1)}, u32[]{:S(2)}) copy-start(bf16[512,4096]{1,0:T(8,128)(2,1)} %param.9) | copy-start | bytes 12582916
  10.1 4.6 %collective-permute-start.1 = (bf16[8,4096]{1,0:T(8,128)(2,1)S(1)}, bf16[8,4096]{1,0:T(8,128)(2,1)S(1)}, u32[]{:S(2)}, u32[]{:S(2)}) collective-permute-start(bf16[8,4096]{1,0:T(8,128)(2,1)S(1)} %maximum_select_fusion.6), channel_id=1, source_target_pairs={{0,4},{1,5},{2,6},{3,7},{4,0},{5,1},{6,2},{7,3},{8,12},{9,13},{10,... | collective-permute-start | bytes 196616 | tf_op jit(solution)/shard_map/ppermute | solution.py:18
  12.1 4.4 %collective-permute-start.17 = (bf16[8,4096]{1,0:T(8,128)(2,1)S(1)}, bf16[8,4096]{1,0:T(8,128)(2,1)S(1)}, u32[]{:S(2)}, u32[]{:S(2)}) collective-permute-start(bf16[8,4096]{1,0:T(8,128)(2,1)S(1)} %maximum_select_fusion.7), channel_id=1, source_target_pairs={{0,4},{1,5},{2,6},{3,7},{4,0},{5,1},{6,2},{7,3},{8,12},{9,13},{10,... | collective-permute-start | bytes 196616 | tf_op jit(solution)/shard_map/ppermute | solution.py:18
  14.8 12.6 %collective-permute-start.2 = (bf16[16,4096]{1,0:T(8,128)(2,1)S(1)}, bf16[16,4096]{1,0:T(8,128)(2,1)S(1)}, u32[]{:S(2)}, u32[]{:S(2)}) collective-permute-start(bf16[16,4096]{1,0:T(8,128)(2,1)S(1)} %maximum_select_fusion.4), channel_id=1, source_target_pairs={{0,2},{1,3},{2,0},{3,1},{4,6},{5,7},{6,4},{7,5},{8,10},{9,11},{10,... | collective-permute-start | bytes 393224 | tf_op jit(solution)/shard_map/ppermute | solution.py:18
  16.5 7.5 %collective-permute-start.18 = (bf16[16,4096]{1,0:T(8,128)(2,1)S(1)}, bf16[16,4096]{1,0:T(8,128)(2,1)S(1)}, u32[]{:S(2)}, u32[]{:S(2)}) collective-permute-start(bf16[16,4096]{1,0:T(8,128)(2,1)S(1)} %maximum_select_fusion.5), channel_id=1, source_target_pairs={{0,2},{1,3},{2,0},{3,1},{4,6},{5,7},{6,4},{7,5},{8,10},{9,11},{10,... | collective-permute-start | bytes 393224 | tf_op jit(solution)/shard_map/ppermute | solution.py:18
  18.0 7.6 %collective-permute-start.13 = (bf16[16,4096]{1,0:T(8,128)(2,1)S(1)}, bf16[16,4096]{1,0:T(8,128)(2,1)S(1)}, u32[]{:S(2)}, u32[]{:S(2)}) collective-permute-start(bf16[16,4096]{1,0:T(8,128)(2,1)S(1)} %broadcast_select_fusion.1), channel_id=1, source_target_pairs={{0,2},{1,3},{2,0},{3,1},{4,6},{5,7},{6,4},{7,5},{8,10},{9,11},{10,... | collective-permute-start | bytes 393224 | tf_op jit(solution)/shard_map/ppermute | solution.py:18
  24.1 19.1 %collective-permute-start.19 = (bf16[32,4096]{1,0:T(8,128)(2,1)S(1)}, bf16[32,4096]{1,0:T(8,128)(2,1)S(1)}, u32[]{:S(2)}, u32[]{:S(2)}) collective-permute-start(bf16[32,4096]{1,0:T(8,128)(2,1)S(1)} %maximum_select_fusion.3), channel_id=1, source_target_pairs={{0,1},{1,0},{2,3},{3,2},{4,5},{5,4},{6,7},{7,6},{8,9},{9,8},{10,11... | collective-permute-start | bytes 786440 | tf_op jit(solution)/shard_map/ppermute | solution.py:18
  25.7 4.3 %collective-permute-start.14 = (bf16[8,4096]{1,0:T(8,128)(2,1)S(1)}, bf16[8,4096]{1,0:T(8,128)(2,1)S(1)}, u32[]{:S(2)}, u32[]{:S(2)}) collective-permute-start(bf16[8,4096]{1,0:T(8,128)(2,1)S(1)} %broadcast_select_fusion.2), channel_id=1, source_target_pairs={{0,4},{1,5},{2,6},{3,7},{4,0},{5,1},{6,2},{7,3},{8,12},{9,13},{10,... | collective-permute-start | bytes 196616 | tf_op jit(solution)/shard_map/ppermute | solution.py:18
  27.5 2.6 %collective-permute-start.3 = (bf16[32,4096]{1,0:T(8,128)(2,1)S(1)}, bf16[32,4096]{1,0:T(8,128)(2,1)S(1)}, u32[]{:S(2)}, u32[]{:S(2)}) collective-permute-start(bf16[32,4096]{1,0:T(8,128)(2,1)S(1)} %maximum_select_fusion.2), channel_id=1, source_target_pairs={{0,1},{1,0},{2,3},{3,2},{4,5},{5,4},{6,7},{7,6},{8,9},{9,8},{10,11... | collective-permute-start | bytes 786440 | tf_op jit(solution)/shard_map/ppermute | solution.py:18
  31.9 2.8 %collective-permute-start.4 = (f32[3,64]{1,0:T(4,128)S(1)}, f32[3,64]{1,0:T(4,128)S(1)}, u32[]{:S(2)}, u32[]{:S(2)}) collective-permute-start(f32[3,64]{1,0:T(4,128)S(1)} %pad_maximum_fusion), channel_id=1, source_target_pairs={{0,1},{1,0},{2,3},{3,2},{4,5},{5,4},{6,7},{7,6},{8,9},{9,8},{10,11... | collective-permute-start | bytes 2312 | tf_op jit(solution)/shard_map/ppermute | solution.py:18
  32.0 29.5 %collective-permute-start.15 = (bf16[4,4096]{1,0:T(4,128)(2,1)S(1)}, bf16[4,4096]{1,0:T(4,128)(2,1)S(1)}, u32[]{:S(2)}, u32[]{:S(2)}) collective-permute-start(bf16[4,4096]{1,0:T(4,128)(2,1)S(1)} %broadcast_select_fusion.3), channel_id=1, source_target_pairs={{0,8},{1,9},{2,10},{3,11},{4,12},{5,13},{6,14},{7,15},{8,0},{9,1},... | collective-permute-start | bytes 98312 | tf_op jit(solution)/shard_map/ppermute | solution.py:18
  34.8 3.7 %collective-permute-start.6 = (f32[3,64]{1,0:T(4,128)S(1)}, f32[3,64]{1,0:T(4,128)S(1)}, u32[]{:S(2)}, u32[]{:S(2)}) collective-permute-start(f32[3,64]{1,0:T(4,128)S(1)} %pad_maximum_fusion.1), channel_id=1, source_target_pairs={{0,2},{1,3},{2,0},{3,1},{4,6},{5,7},{6,4},{7,5},{8,10},{9,11},{10,... | collective-permute-start | bytes 2312 | tf_op jit(solution)/shard_map/ppermute | solution.py:18
  38.4 3.7 %collective-permute-start.8 = (f32[3,64]{1,0:T(4,128)S(1)}, f32[3,64]{1,0:T(4,128)S(1)}, u32[]{:S(2)}, u32[]{:S(2)}) collective-permute-start(f32[3,64]{1,0:T(4,128)S(1)} %pad_maximum_fusion.2), channel_id=1, source_target_pairs={{0,4},{1,5},{2,6},{3,7},{4,0},{5,1},{6,2},{7,3},{8,12},{9,13},{10,... | collective-permute-start | bytes 2312 | tf_op jit(solution)/shard_map/ppermute | solution.py:18
  40.1 6.9 %collective-permute-start.5 = (bf16[32,4096]{1,0:T(8,128)(2,1)S(1)}, bf16[32,4096]{1,0:T(8,128)(2,1)S(1)}, u32[]{:S(2)}, u32[]{:S(2)}) collective-permute-start(bf16[32,4096]{1,0:T(8,128)(2,1)S(1)} %select_convert_fusion), channel_id=1, source_target_pairs={{0,1},{1,0},{2,3},{3,2},{4,5},{5,4},{6,7},{7,6},{8,9},{9,8},{10,11... | collective-permute-start | bytes 786440 | tf_op jit(solution)/shard_map/ppermute | solution.py:18
  42.1 4.5 %collective-permute-start.10 = (f32[3,64]{1,0:T(4,128)S(1)}, f32[3,64]{1,0:T(4,128)S(1)}, u32[]{:S(2)}, u32[]{:S(2)}) collective-permute-start(f32[3,64]{1,0:T(4,128)S(1)} %pad_maximum_fusion.3), channel_id=1, source_target_pairs={{0,8},{1,9},{2,10},{3,11},{4,12},{5,13},{6,14},{7,15},{8,0},{9,1},... | collective-permute-start | bytes 2312 | tf_op jit(solution)/shard_map/ppermute | solution.py:18
  47.2 5.0 %collective-permute-start.7 = (bf16[16,4096]{1,0:T(8,128)(2,1)S(1)}, bf16[16,4096]{1,0:T(8,128)(2,1)S(1)}, u32[]{:S(2)}, u32[]{:S(2)}) collective-permute-start(bf16[16,4096]{1,0:T(8,128)(2,1)S(1)} %select_convert_fusion.1), channel_id=1, source_target_pairs={{0,2},{1,3},{2,0},{3,1},{4,6},{5,7},{6,4},{7,5},{8,10},{9,11},{10,... | collective-permute-start | bytes 393224 | tf_op jit(solution)/shard_map/ppermute | solution.py:18
  52.4 4.5 %collective-permute-start.9 = (bf16[8,4096]{1,0:T(8,128)(2,1)S(1)}, bf16[8,4096]{1,0:T(8,128)(2,1)S(1)}, u32[]{:S(2)}, u32[]{:S(2)}) collective-permute-start(bf16[8,4096]{1,0:T(8,128)(2,1)S(1)} %select_convert_fusion.2), channel_id=1, source_target_pairs={{0,4},{1,5},{2,6},{3,7},{4,0},{5,1},{6,2},{7,3},{8,12},{9,13},{10,... | collective-permute-start | bytes 196616 | tf_op jit(solution)/shard_map/ppermute | solution.py:18
  57.0 4.9 %collective-permute-start.11 = (bf16[4,4096]{1,0:T(4,128)(2,1)S(1)}, bf16[4,4096]{1,0:T(4,128)(2,1)S(1)}, u32[]{:S(2)}, u32[]{:S(2)}) collective-permute-start(bf16[4,4096]{1,0:T(4,128)(2,1)S(1)} %select_convert_fusion.3), channel_id=1, source_target_pairs={{0,8},{1,9},{2,10},{3,11},{4,12},{5,13},{6,14},{7,15},{8,0},{9,1},... | collective-permute-start | bytes 98312 | tf_op jit(solution)/shard_map/ppermute | solution.py:18

commit v2 on v1

v2 whole, which is shorter than its diff:
```python
import functools

import jax
import jax.numpy as jnp
from jax import lax
from jax.experimental import pallas as pl
from jax.experimental.pallas import tpu as pltpu
from jax.sharding import PartitionSpec as P

NEG = -1e30
f32, bf16, i32 = jnp.float32, jnp.bfloat16, jnp.int32


def prepare(mine, steps, me, hidden, d_input, ids, language, allowed, target, weight,
            hidden_o, input_o, pick_o, took_o, ok_o, weight_o):
    rank = me[0, 0]
    n = 1 << steps
    tokens = mine * n
    cols = pick_o.shape[1]
    hidden_o[...] = hidden[...]
    input_o[...] = d_input[...]
    place = lax.broadcasted_iota(i32, (tokens, 1), 0)
    block = lax.div(place, mine)
    source = place - block * mine
    for i in range(steps):
        source = source + mine * (n >> (i + 1)) * (lax.shift_right_logical(block, i) & 1)
    here = source == lax.broadcasted_iota(i32, (tokens, tokens), 1)

    def column(ref):
        return jnp.sum(jnp.where(here, ref[...], jnp.zeros_like(ref[...])), axis=1, keepdims=True)

    vocab = rank * cols + lax.broadcasted_iota(i32, (1, cols), 1)
    pick_o[...] = (column(target) == vocab).astype(f32).astype(bf16)
    took_o[...] = (column(ids) == vocab).astype(f32).astype(bf16)
    weight_o[...] = column(weight)
    langs, blocks = allowed.shape
    speaks = (column(language) == lax.broadcasted_iota(i32, (1, langs), 1)).astype(f32)
    may = jnp.dot(speaks, allowed[...].astype(f32), preferred_element_type=f32)
    column_here = lax.broadcasted_iota(i32, (1, blocks), 1) == rank
    ok_o[...] = jnp.sum(jnp.where(column_here, may, 0.0), axis=1, keepdims=True)


def per_device(n, hidden, embedding, d_input, input_ids, language, allowed, target, token_weight):
    cols, width = embedding.shape
    mine = hidden.shape[0]
    tokens = mine * n
    steps = n.bit_length() - 1
    me = lax.axis_index("vocab")

    def swap(x, k):
        return lax.ppermute(x, "vocab", [(i, i ^ k) for i in range(n)])

    def bit(k):
        return (me & k) != 0

    def after(x, *deps):
        return lax.optimization_barrier((x,) + deps)[0]

    def join(x, r, k):
        return jnp.where(bit(k), jnp.concatenate([r, x], 0), jnp.concatenate([x, r], 0))

    def halves(x, k):
        h = x.shape[0] // 2
        a, b = x[:h], x[h:]
        return jnp.where(bit(k), b, a), jnp.where(bit(k), a, b)

    first = swap(hidden, n // 2)
    first_input = swap(d_input, n // 2)
    vmem = pl.BlockSpec(memory_space=pltpu.VMEM)
    hidden_c, input_c, pick, took, ok, weight = pl.pallas_call(
        functools.partial(prepare, mine, steps),
        out_shape=(
            jax.ShapeDtypeStruct(hidden.shape, bf16),
            jax.ShapeDtypeStruct(d_input.shape, bf16),
            jax.ShapeDtypeStruct((tokens, cols), bf16),
            jax.ShapeDtypeStruct((tokens, cols), bf16),
            jax.ShapeDtypeStruct((tokens, 1), f32),
            jax.ShapeDtypeStruct((tokens, 1), f32),
        ),
        in_specs=[pl.BlockSpec(memory_space=pltpu.SMEM)] + [vmem] * 7,
        out_specs=(vmem,) * 6,
        name="prepare",
    )(
        me.reshape(1, 1), hidden, d_input, input_ids.reshape(1, tokens), language.reshape(1, tokens),
        allowed, target.reshape(1, tokens), token_weight.reshape(1, tokens),
    )
    usable = ok > 0.0
    is_target = pick > 0

    all_hidden, all_input = join(hidden_c, first, n // 2), join(input_c, first_input, n // 2)
    k = n // 4
    while k:
        if k == 2:
            all_input = after(all_input, all_hidden)
            pick_late = after(pick, all_hidden)
        got = swap(all_hidden, k)
        if k > 1:
            got_input = swap(all_input, k)
        all_hidden = join(all_hidden, got, k)
        if k > 2:
            all_input = join(all_input, got_input, k)
        k //= 2
    all_input = join(all_input, after(got_input, all_hidden), 2)
    all_input = join(all_input, swap(all_input, 1), 1)
    rows = jnp.dot(pick_late, embedding, preferred_element_type=f32).astype(bf16)
    keep, send = halves(rows, 1)
    rows = keep + swap(send, 1)

    logits = lax.dot_general(all_hidden, embedding, (((1,), (1,)), ((), ())), preferred_element_type=f32)
    masked = jnp.where(usable, logits, f32(NEG))
    m = jnp.max(masked, axis=1)
    p = jnp.where(usable, jnp.exp(masked - m[:, None]), f32(0.0))
    s = jnp.sum(p, axis=1)
    lt = jnp.max(jnp.where(is_target, masked, f32(NEG)), axis=1)
    part = jnp.dot(jnp.where(is_target, f32(0.0), p).astype(bf16), embedding, preferred_element_type=f32)

    lo = 0
    k = 1
    while k < n:
        keep, send = halves(part, k)
        send = send.astype(bf16)
        packed = jnp.stack([m, s, lt])
        if k > 1:
            packed, send = lax.optimization_barrier((packed, send))
            keep_rows, send_rows = halves(after(rows, packed), k)
        got = swap(packed, k)
        recv = swap(send, k)
        if k > 1:
            rows = keep_rows + swap(send_rows, k)
        m_new = jnp.maximum(m, got[0])
        a, b = jnp.exp(m - m_new), jnp.exp(got[0] - m_new)
        s = s * a + got[1] * b
        lt = jnp.maximum(lt, got[2])
        m, s, lt, a, b = lax.optimization_barrier((m_new, s, lt, a, b))
        size = keep.shape[0]
        lo = lo + jnp.where(bit(k), size, 0)
        part = keep * lax.dynamic_slice_in_dim(a, lo, size)[:, None] + recv.astype(f32) * lax.dynamic_slice_in_dim(b, lo, size)[:, None]
        k *= 2

    hot = is_target.astype(f32)
    d_logits = jnp.where(
        usable, weight * (jnp.exp(masked - m[:, None]) / s[:, None] - hot), f32(0.0)
    ).astype(bf16)
    w = weight[:, 0]
    coef = (w * (jnp.exp(lt - m) / s - 1.0)).astype(bf16).astype(f32)
    scale = w / s
    d_hidden = (
        part * lax.dynamic_slice_in_dim(scale, lo, mine)[:, None]
        + rows.astype(f32) * lax.dynamic_slice_in_dim(coef, lo, mine)[:, None]
    ).astype(bf16)
    d_embed = lax.dot_general(
        jnp.concatenate([d_logits, took], 0),
        jnp.concatenate([all_hidden, all_input], 0),
        (((0,), (0,)), ((), ())),
        preferred_element_type=f32,
    ).astype(bf16)
    return d_hidden, d_embed


def solution(mesh):
    n = mesh.shape["vocab"]
    placed = (
        P(("groups", "vocab"), None),
        P(("groups", "vocab"), None),
        P(("groups", "vocab"), None),
        P("groups"),
        P("groups"),
        P("groups", None),
        P("groups"),
        P("groups"),
    )
    return jax.shard_map(
        functools.partial(per_device, n),
        mesh=mesh,
        in_specs=placed,
        out_specs=(P(("groups", "vocab"), None), P(("groups", "vocab"), None)),
        check_vma=False,
    )
```

time: 62.8 us -> 54.6 us (0.87)
  waiting for transfers between devices: 24.6 us -> 13.6 us
  other arithmetic: 2.41 us -> 5.62 us
  Pallas kernels: 0 us -> 1.74 us
  local copies, waits for them, and re-layouts: 2.37 us -> 0.77 us
  starting transfers between devices: 23.4 us -> 22.7 us
    ppermute x20, waiting for transfers between devices: 24.6 us -> 13.6 us  [swap(): return lax.ppermute(x, 'vocab', [(i, i ^ k) for i in range(n)])]
    pallas_call x0 -> x1, Pallas kernels: none -> 1.74 us  [per_device(): pl.pallas_call(functools.partial(prepare, mine, steps), out_shape=(jax.Sh...]
    select_n x8, other arithmetic: 0.44 us -> 2.12 us  [join(): jnp.where(bit(k), jnp.concatenate([r, x], 0), jnp.concatenate([x, r], 0))]
    reshape x5 -> x0, local copies, waits for them, and re-layouts: 1.1 us -> none  [the longest x4 1.01 us: order(): y = x.reshape((2,) * steps + (mine,) + x.shape[1:])]
    pallas_call x0 -> x1, other arithmetic: none -> 0.87 us  [per_device(): pl.pallas_call(functools.partial(prepare, mine, steps), out_shape=(jax.Sh...]
    gt x1, other arithmetic: 0.01 us -> 0.86 us  [per_device(): usable = ok > 0.0]
    ppermute x20, starting transfers between devices: 23.4 us -> 22.7 us  [swap(): return lax.ppermute(x, 'vocab', [(i, i ^ k) for i in range(n)])]
  transfers between devices with their start and end apart: 20 -> 20, of which waited for: 10 -> 10; matrix products, arithmetic and copies ran while one was open for 20% -> 27% of each run, Pallas kernels for 0% -> 3%
where the time goes in v2:
time: 54.6 us; the launch traced here: 54.1 us
  starting transfers between devices  22.7 us (42%)
  waiting for transfers between devices  13.6 us (25%)
  matrix products  8.75 us (16%)
  other arithmetic  5.62 us (10%)
  Pallas kernels  1.74 us (3%)
  between operations  0.9 us (2%)
  local copies, waits for them, and re-layouts  0.77 us (1%)
    ppermute x20, starting transfers between devices, swap(): return lax.ppermute(x, 'vocab', [(i, i ^ k) for i in range(n)])  22.7 us
    ppermute x20, waiting for transfers between devices, swap(): return lax.ppermute(x, 'vocab', [(i, i ^ k) for i in range(n)])  13.6 us
    dot_general x1, matrix products, per_device(): lax.dot_general(jnp.concatenate([d_logits, took], 0), jnp.concatenate([al...  3.29 us
    dot_general x1, matrix products, per_device(): jnp.dot(pick_late, embedding, preferred_element_type=f32).astype(bf16)  3.07 us
    select_n x8, other arithmetic, join(): jnp.where(bit(k), jnp.concatenate([r, x], 0), jnp.concatenate([x, r], 0))  2.12 us
    pallas_call x1, Pallas kernels, per_device(): pl.pallas_call(functools.partial(prepare, mine, steps), out_shape=(jax.Sh...  1.74 us
    dot_general x1, matrix products, per_device(): lax.dot_general(all_hidden, embedding, (((1,), (1,)), ((), ())), preferre...  1.49 us
  transfers between devices with their start and end apart: 20, of which 10 were waited for; matrix products, arithmetic and copies ran while one was open for 27% of the time, Pallas kernels for 3%

profile of v2, /device:TPU:0, one launch (start us, length us, event | category | flops | bytes accessed | tf_op | source)
XLA Modules:
  0.0 54.1 jit_solution(3208647588154397488)
XLA Ops:
  0.6 4.1 %collective-permute-start = (bf16[4,4096]{1,0:T(4,128)(2,1)}, bf16[4,4096]{1,0:T(4,128)(2,1)S(1)}, u32[]{:S(2)}, u32[]{:S(2)}) collective-permute-start(bf16[4,4096]{1,0:T(4,128)(2,1)} %hidden.1), channel_id=1, source_target_pairs={{0,8},{1,9},{2,10},{3,11},{4,12},{5,13},{6,14},{7,15},{8,0},{9,1},... | collective-permute-start | bytes 98312 | tf_op jit(solution)/shard_map/ppermute | solution.py:51
  4.8 1.7 %prepare.1 = (bf16[4,4096]{1,0:T(4,128)(2,1)}, bf16[4,4096]{1,0:T(4,128)(2,1)}, bf16[64,512]{1,0:T(8,128)(2,1)}, bf16[64,512]{1,0:T(8,128)(2,1)}, f32[64,1]{1,0:T(8,128)}, /*index=5*/f32[64,1]{1,0:T(8,128)}) custom-call(s32[1,1]{1,0:T(1,128)} %bitcast.me, bf16[4,4096]{1,0:T(4,128)(2,1)} %hidden.1, bf16[4,4096]{1,0:T(4,128)(2,1)} %d_input.1, ...), custom_call_target="tpu_custom_call" | custom-call | tf_op jit(solution)/shard_map/prepare/pallas_call | solution.py:70
  6.6 0.9 %compare_reduce_fusion = pred[64]{0:T(512)(128)(4,1)S(1)} fusion(f32[64,1]{1,0:T(8,128)} %get-tuple-element.41), kind=kLoop, calls=%fused_computation.41 | loop fusion | flops 64 | bytes 320 | tf_op jit(solution)/shard_map/gt | solution.py:87
  7.4 0.9 %reduce.1 = f32[64]{0:T(128)S(1)} reduce(f32[64,1]{1,0:T(8,128)} %get-tuple-element.66, f32[]{:T(128)} %constant.36), dimensions={1}, to_apply=%get-tuple-element.66.reduce_sub_computation | reduce | bytes 516 | tf_op jit(solution)/shard_map/prepare/pallas_call | solution.py:70
  8.3 0.9 %maximum_select_fusion.6 = bf16[8,4096]{1,0:T(8,128)(2,1)S(1)} fusion(bf16[4,4096]{1,0:T(4,128)(2,1)} %get-tuple-element.42, bf16[4,4096]{1,0:T(4,128)(2,1)S(1)} %collective-permute-done, pred[]{:T(512)S(6)} %ne.8), kind=kLoop, calls=%fused_computation.31 | loop fusion | flops 294912 | bytes 131073 | tf_op jit(solution)/shard_map/jit(_where)/select_n | solution.py:60
  9.2 1.9 %collective-permute-start.1 = (bf16[8,4096]{1,0:T(8,128)(2,1)S(1)}, bf16[8,4096]{1,0:T(8,128)(2,1)S(1)}, u32[]{:S(2)}, u32[]{:S(2)}) collective-permute-start(bf16[8,4096]{1,0:T(8,128)(2,1)S(1)} %maximum_select_fusion.6), channel_id=1, source_target_pairs={{0,4},{1,5},{2,6},{3,7},{4,0},{5,1},{6,2},{7,3},{8,12},{9,13},{10,... | collective-permute-start | bytes 196616 | tf_op jit(solution)/shard_map/ppermute | solution.py:51
  11.1 0.9 %maximum_select_fusion.7 = bf16[8,4096]{1,0:T(8,128)(2,1)S(1)} fusion(bf16[4,4096]{1,0:T(4,128)(2,1)} %get-tuple-element.75, bf16[4,4096]{1,0:T(4,128)(2,1)S(1)} %collective-permute-done.16, pred[]{:T(512)S(6)} %ne.8), kind=kLoop, calls=%fused_computation.32 | loop fusion | flops 294912 | bytes 131073 | tf_op jit(solution)/shard_map/jit(_where)/select_n | solution.py:60
  12.0 0.3 collective-permute-start.17
  12.3 1.3 %collective-permute-done.1 = bf16[8,4096]{1,0:T(8,128)(2,1)S(1)} collective-permute-done((bf16[8,4096]{1,0:T(8,128)(2,1)S(1)}, bf16[8,4096]{1,0:T(8,128)(2,1)S(1)}, u32[]{:S(2)}, u32[]{:S(2)}) %collective-permute-start.1) | collective-permute-done | bytes 65568 | tf_op jit(solution)/shard_map/ppermute | solution.py:51
  13.6 2.0 %collective-permute-start.2 = (bf16[16,4096]{1,0:T(8,128)(2,1)S(1)}, bf16[16,4096]{1,0:T(8,128)(2,1)S(1)}, u32[]{:S(2)}, u32[]{:S(2)}) collective-permute-start(bf16[16,4096]{1,0:T(8,128)(2,1)S(1)} %maximum_select_fusion.4), channel_id=1, source_target_pairs={{0,2},{1,3},{2,0},{3,1},{4,6},{5,7},{6,4},{7,5},{8,10},{9,11},{10,... | collective-permute-start | bytes 393224 | tf_op jit(solution)/shard_map/ppermute | solution.py:51
  15.6 0.8 %collective-permute-done.17 = bf16[8,4096]{1,0:T(8,128)(2,1)S(1)} collective-permute-done((bf16[8,4096]{1,0:T(8,128)(2,1)S(1)}, bf16[8,4096]{1,0:T(8,128)(2,1)S(1)}, u32[]{:S(2)}, u32[]{:S(2)}) %collective-permute-start.17) | collective-permute-done | bytes 65568 | tf_op jit(solution)/shard_map/ppermute | solution.py:51
  16.4 1.6 %collective-permute-start.18 = (bf16[16,4096]{1,0:T(8,128)(2,1)S(1)}, bf16[16,4096]{1,0:T(8,128)(2,1)S(1)}, u32[]{:S(2)}, u32[]{:S(2)}) collective-permute-start(bf16[16,4096]{1,0:T(8,128)(2,1)S(1)} %maximum_select_fusion.5), channel_id=1, source_target_pairs={{0,2},{1,3},{2,0},{3,1},{4,6},{5,7},{6,4},{7,5},{8,10},{9,11},{10,... | collective-permute-start | bytes 393224 | tf_op jit(solution)/shard_map/ppermute | solution.py:51
  18.0 3.1 %convolution_convert_fusion.1 = bf16[64,4096]{1,0:T(8,128)(2,1)S(1)} fusion(bf16[64,512]{1,0:T(8,128)(2,1)} %get-tuple-element.68, bf16[512,4096]{1,0:T(8,128)(2,1)} %param.9), kind=kOutput, calls=%fused_computation.1 | convolution fusion | flops 268697600 | bytes 4784128 | tf_op jit(solution)/shard_map/dot_general | solution.py:105
  21.2 0.5 %collective-permute-start.3 = (bf16[32,4096]{1,0:T(8,128)(2,1)S(1)}, bf16[32,4096]{1,0:T(8,128)(2,1)S(1)}, u32[]{:S(2)}, u32[]{:S(2)}) collective-permute-start(bf16[32,4096]{1,0:T(8,128)(2,1)S(1)} %maximum_select_fusion.2), channel_id=1, source_target_pairs={{0,1},{1,0},{2,3},{3,2},{4,5},{5,4},{6,7},{7,6},{8,9},{9,8},{10,11... | collective-permute-start | bytes 786440 | tf_op jit(solution)/shard_map/ppermute | solution.py:51
  21.8 0.9 %collective-permute-done.12 = bf16[32,4096]{1,0:T(8,128)(2,1)S(1)} collective-permute-done((bf16[32,4096]{1,0:T(8,128)(2,1)S(1)}, bf16[32,4096]{1,0:T(8,128)(2,1)S(1)}, u32[]{:S(2)}, u32[]{:S(2)}) %collective-permute-start.12) | collective-permute-done | bytes 262176 | tf_op jit(solution)/shard_map/ppermute | solution.py:51
  22.7 0.3 collective-permute-done.3
  23.1 0.1 maximum_select_fusion
  23.2 1.5 %fusion.26 = (f32[64]{0:T(128)S(1)}, f32[64,512]{1,0:T(8,128)S(1)}) fusion(bf16[64,4096]{1,0:T(8,128)(2,1)S(1)} %maximum_select_fusion, bf16[512,4096]{1,0:T(8,128)(2,1)S(1)} %copy-done, pred[64]{0:T(512)(128)(4,1)S(1)} %compare_reduce_fusion), kind=kOutput, calls=%fused_computation.80 | convolution fusion | flops 268500928 | bytes 4849984 | tf_op jit(solution)/shard_map/dot_general | solution.py:109
  24.7 0.9 %fusion.7 = f32[64,4096]{1,0:T(8,128)S(1)} fusion(bf16[512,4096]{1,0:T(8,128)(2,1)S(1)} %copy-done, f32[64,512]{1,0:T(8,128)S(1)} %get-tuple-element.103, f32[64]{0:T(128)S(1)} %get-tuple-element.102, pred[64]{0:T(512)(128)(4,1)S(1)} %compare_reduce_fusion, bf16[64,512]{1,0:T(8,128)(2,1)S(1)} %copy-done.1), kind=kOutput, calls=%fused_computation.30 | convolution fusion | flops 268599296 | bytes 5439808 | tf_op jit(solution)/shard_map/dot_general | solution.py:115
  25.6 0.2 fusion.6
  25.8 0.3 collective-permute-start.4
  26.2 0.3 collective-permute-start.19
  26.5 0.3 collective-permute-start.5
  26.8 0.3 collective-permute-done.4
  27.1 0.1 dynamic_slice.30
  27.2 0.8 %collective-permute-done.5 = bf16[32,4096]{1,0:T(8,128)(2,1)S(1)} collective-permute-done((bf16[32,4096]{1,0:T(8,128)(2,1)S(1)}, bf16[32,4096]{1,0:T(8,128)(2,1)S(1)}, u32[]{:S(2)}, u32[]{:S(2)}) %collective-permute-start.5) | collective-permute-done | bytes 262176 | tf_op jit(solution)/shard_map/ppermute | solution.py:51
  28.1 0.2 multiply_add_fusion
  28.3 0.6 %collective-permute-start.6 = (f32[3,64]{1,0:T(4,128)S(1)}, f32[3,64]{1,0:T(4,128)S(1)}, u32[]{:S(2)}, u32[]{:S(2)}) collective-permute-start(f32[3,64]{1,0:T(4,128)S(1)} %pad_maximum_fusion.1), channel_id=1, source_target_pairs={{0,2},{1,3},{2,0},{3,1},{4,6},{5,7},{6,4},{7,5},{8,10},{9,11},{10,... | collective-permute-start | bytes 2312 | tf_op jit(solution)/shard_map/ppermute | solution.py:51
  28.9 1.6 %collective-permute-start.13 = (bf16[16,4096]{1,0:T(8,128)(2,1)S(1)}, bf16[16,4096]{1,0:T(8,128)(2,1)S(1)}, u32[]{:S(2)}, u32[]{:S(2)}) collective-permute-start(bf16[16,4096]{1,0:T(8,128)(2,1)S(1)} %broadcast_select_fusion.1), channel_id=1, source_target_pairs={{0,2},{1,3},{2,0},{3,1},{4,6},{5,7},{6,4},{7,5},{8,10},{9,11},{10,... | collective-permute-start | bytes 393224 | tf_op jit(solution)/shard_map/ppermute | solution.py:51
  30.4 0.5 collective-permute-start.7
  31.0 0.1 maximum_select_fusion.1
  31.1 0.8 %collective-permute-done.6 = f32[3,64]{1,0:T(4,128)S(1)} collective-permute-done((f32[3,64]{1,0:T(4,128)S(1)}, f32[3,64]{1,0:T(4,128)S(1)}, u32[]{:S(2)}, u32[]{:S(2)}) %collective-permute-start.6) | collective-permute-done | bytes 800 | tf_op jit(solution)/shard_map/ppermute | solution.py:51
  31.9 0.1 dynamic_slice.32
  32.1 5.1 %collective-permute-done.7 = bf16[16,4096]{1,0:T(8,128)(2,1)S(1)} collective-permute-done((bf16[16,4096]{1,0:T(8,128)(2,1)S(1)}, bf16[16,4096]{1,0:T(8,128)(2,1)S(1)}, u32[]{:S(2)}, u32[]{:S(2)}) %collective-permute-start.7) | collective-permute-done | bytes 131104 | tf_op jit(solution)/shard_map/ppermute | solution.py:51
  37.2 0.1 multiply_add_fusion.1
  37.3 0.9 %collective-permute-start.8 = (f32[3,64]{1,0:T(4,128)S(1)}, f32[3,64]{1,0:T(4,128)S(1)}, u32[]{:S(2)}, u32[]{:S(2)}) collective-permute-start(f32[3,64]{1,0:T(4,128)S(1)} %pad_maximum_fusion.2), channel_id=1, source_target_pairs={{0,4},{1,5},{2,6},{3,7},{4,0},{5,1},{6,2},{7,3},{8,12},{9,13},{10,... | collective-permute-start | bytes 2312 | tf_op jit(solution)/shard_map/ppermute | solution.py:51
  38.2 1.3 %collective-permute-start.14 = (bf16[8,4096]{1,0:T(8,128)(2,1)S(1)}, bf16[8,4096]{1,0:T(8,128)(2,1)S(1)}, u32[]{:S(2)}, u32[]{:S(2)}) collective-permute-start(bf16[8,4096]{1,0:T(8,128)(2,1)S(1)} %broadcast_select_fusion.2), channel_id=1, source_target_pairs={{0,4},{1,5},{2,6},{3,7},{4,0},{5,1},{6,2},{7,3},{8,12},{9,13},{10,... | collective-permute-start | bytes 196616 | tf_op jit(solution)/shard_map/ppermute | solution.py:51
  39.5 0.8 %collective-permute-start.9 = (bf16[8,4096]{1,0:T(8,128)(2,1)S(1)}, bf16[8,4096]{1,0:T(8,128)(2,1)S(1)}, u32[]{:S(2)}, u32[]{:S(2)}) collective-permute-start(bf16[8,4096]{1,0:T(8,128)(2,1)S(1)} %select_convert_fusion.3), channel_id=1, source_target_pairs={{0,4},{1,5},{2,6},{3,7},{4,0},{5,1},{6,2},{7,3},{8,12},{9,13},{10,... | collective-permute-start | bytes 196616 | tf_op jit(solution)/shard_map/ppermute | solution.py:51
  40.3 0.7 %collective-permute-done.8 = f32[3,64]{1,0:T(4,128)S(1)} collective-permute-done((f32[3,64]{1,0:T(4,128)S(1)}, f32[3,64]{1,0:T(4,128)S(1)}, u32[]{:S(2)}, u32[]{:S(2)}) %collective-permute-start.8) | collective-permute-done | bytes 800 | tf_op jit(solution)/shard_map/ppermute | solution.py:51
  41.0 0.1 dynamic_slice.34
  41.1 2.6 %collective-permute-done.9 = bf16[8,4096]{1,0:T(8,128)(2,1)S(1)} collective-permute-done((bf16[8,4096]{1,0:T(8,128)(2,1)S(1)}, bf16[8,4096]{1,0:T(8,128)(2,1)S(1)}, u32[]{:S(2)}, u32[]{:S(2)}) %collective-permute-start.9) | collective-permute-done | bytes 65568 | tf_op jit(solution)/shard_map/ppermute | solution.py:51
  43.8 0.1 multiply_add_fusion.2
  43.9 2.7 %collective-permute-start.10 = (f32[3,64]{1,0:T(4,128)S(1)}, f32[3,64]{1,0:T(4,128)S(1)}, u32[]{:S(2)}, u32[]{:S(2)}) collective-permute-start(f32[3,64]{1,0:T(4,128)S(1)} %pad_maximum_fusion.3), channel_id=1, source_target_pairs={{0,8},{1,9},{2,10},{3,11},{4,12},{5,13},{6,14},{7,15},{8,0},{9,1},... | collective-permute-start | bytes 2312 | tf_op jit(solution)/shard_map/ppermute | solution.py:51
  46.6 0.4 collective-permute-start.15
  47.0 2.6 %collective-permute-start.11 = (bf16[4,4096]{1,0:T(4,128)(2,1)S(1)}, bf16[4,4096]{1,0:T(4,128)(2,1)S(1)}, u32[]{:S(2)}, u32[]{:S(2)}) collective-permute-start(bf16[4,4096]{1,0:T(4,128)(2,1)S(1)} %select_convert_fusion.6), channel_id=1, source_target_pairs={{0,8},{1,9},{2,10},{3,11},{4,12},{5,13},{6,14},{7,15},{8,0},{9,1},... | collective-permute-start | bytes 98312 | tf_op jit(solution)/shard_map/ppermute | solution.py:51
  49.6 0.1 select_convert_fusion.2
  49.8 3.3 %convolution_convert_fusion = bf16[512,4096]{1,0:T(8,128)(2,1)} fusion(bf16[64,4096]{1,0:T(8,128)(2,1)S(1)} %maximum_select_fusion.1, bf16[64,4096]{1,0:T(8,128)(2,1)S(1)} %maximum_select_fusion, bf16[64,512]{1,0:T(8,128)(2,1)S(1)} %copy-done.2, bf16[64,512]{1,0:T(8,128)(2,1)S(1)} %select_convert_fusion.2), kind=kOutput, calls=%fused_computation | convolution fusion | flops 541327360 | bytes 5373952 | tf_op jit(solution)/shard_map/dot_general | solution.py:151
  53.4 0.7 %add_convert_fusion = bf16[4,4096]{1,0:T(4,128)(2,1)} fusion(bf16[4,4096]{1,0:T(4,128)(2,1)S(1)} %collective-permute-done.11, f32[8,4096]{1,0:T(8,128)S(1)} %multiply_add_fusion.2, f32[4]{0:T(128)S(1)} %dynamic_slice.39, bf16[4,4096]{1,0:T(4,128)(2,1)S(1)} %collective-permute-done.15, f32[4]{0:T(128)S(1)} %dynamic_slice.38, f32[4]{0:T(128)S(1)} %dynamic_slice.37, ...), kind=kLoop, calls=%fused_computation.33 | loop fusion | flops 196608 | bytes 294977 | tf_op jit(solution)/shard_map/convert_element_type | solution.py:150
  (49 shorter events, 1.2 us)
Async XLA Ops:
  0.6 7.7 %collective-permute-start = (bf16[4,4096]{1,0:T(4,128)(2,1)}, bf16[4,4096]{1,0:T(4,128)(2,1)S(1)}, u32[]{:S(2)}, u32[]{:S(2)}) collective-permute-start(bf16[4,4096]{1,0:T(4,128)(2,1)} %hidden.1), channel_id=1, source_target_pairs={{0,8},{1,9},{2,10},{3,11},{4,12},{5,13},{6,14},{7,15},{8,0},{9,1},... | collective-permute-start | bytes 98312 | tf_op jit(solution)/shard_map/ppermute | solution.py:51
  4.7 6.4 %collective-permute-start.16 = (bf16[4,4096]{1,0:T(4,128)(2,1)}, bf16[4,4096]{1,0:T(4,128)(2,1)S(1)}, u32[]{:S(2)}, u32[]{:S(2)}) collective-permute-start(bf16[4,4096]{1,0:T(4,128)(2,1)} %d_input.1), channel_id=1, source_target_pairs={{0,8},{1,9},{2,10},{3,11},{4,12},{5,13},{6,14},{7,15},{8,0},{9,1},... | collective-permute-start | bytes 98312 | tf_op jit(solution)/shard_map/ppermute | solution.py:51
  9.2 4.3 %collective-permute-start.1 = (bf16[8,4096]{1,0:T(8,128)(2,1)S(1)}, bf16[8,4096]{1,0:T(8,128)(2,1)S(1)}, u32[]{:S(2)}, u32[]{:S(2)}) collective-permute-start(bf16[8,4096]{1,0:T(8,128)(2,1)S(1)} %maximum_select_fusion.6), channel_id=1, source_target_pairs={{0,4},{1,5},{2,6},{3,7},{4,0},{5,1},{6,2},{7,3},{8,12},{9,13},{10,... | collective-permute-start | bytes 196616 | tf_op jit(solution)/shard_map/ppermute | solution.py:51
  12.0 4.3 %collective-permute-start.17 = (bf16[8,4096]{1,0:T(8,128)(2,1)S(1)}, bf16[8,4096]{1,0:T(8,128)(2,1)S(1)}, u32[]{:S(2)}, u32[]{:S(2)}) collective-permute-start(bf16[8,4096]{1,0:T(8,128)(2,1)S(1)} %maximum_select_fusion.7), channel_id=1, source_target_pairs={{0,4},{1,5},{2,6},{3,7},{4,0},{5,1},{6,2},{7,3},{8,12},{9,13},{10,... | collective-permute-start | bytes 196616 | tf_op jit(solution)/shard_map/ppermute | solution.py:51
  13.6 7.6 %collective-permute-start.2 = (bf16[16,4096]{1,0:T(8,128)(2,1)S(1)}, bf16[16,4096]{1,0:T(8,128)(2,1)S(1)}, u32[]{:S(2)}, u32[]{:S(2)}) collective-permute-start(bf16[16,4096]{1,0:T(8,128)(2,1)S(1)} %maximum_select_fusion.4), channel_id=1, source_target_pairs={{0,2},{1,3},{2,0},{3,1},{4,6},{5,7},{6,4},{7,5},{8,10},{9,11},{10,... | collective-permute-start | bytes 393224 | tf_op jit(solution)/shard_map/ppermute | solution.py:51
  15.6 7.6 %copy-start = (bf16[512,4096]{1,0:T(8,128)(2,1)S(1)}, bf16[512,4096]{1,0:T(8,128)(2,1)}, u32[]{:S(2)}) copy-start(bf16[512,4096]{1,0:T(8,128)(2,1)} %param.9) | copy-start | bytes 12582916
  16.4 9.4 %collective-permute-start.18 = (bf16[16,4096]{1,0:T(8,128)(2,1)S(1)}, bf16[16,4096]{1,0:T(8,128)(2,1)S(1)}, u32[]{:S(2)}, u32[]{:S(2)}) collective-permute-start(bf16[16,4096]{1,0:T(8,128)(2,1)S(1)} %maximum_select_fusion.5), channel_id=1, source_target_pairs={{0,2},{1,3},{2,0},{3,1},{4,6},{5,7},{6,4},{7,5},{8,10},{9,11},{10,... | collective-permute-start | bytes 393224 | tf_op jit(solution)/shard_map/ppermute | solution.py:51
  21.0 3.6 %copy-start.1 = (bf16[64,512]{1,0:T(8,128)(2,1)S(1)}, bf16[64,512]{1,0:T(8,128)(2,1)}, u32[]{:S(2)}) copy-start(bf16[64,512]{1,0:T(8,128)(2,1)} %get-tuple-element.68) | copy-start | bytes 196612
  21.1 1.6 %collective-permute-start.12 = (bf16[32,4096]{1,0:T(8,128)(2,1)S(1)}, bf16[32,4096]{1,0:T(8,128)(2,1)S(1)}, u32[]{:S(2)}, u32[]{:S(2)}) collective-permute-start(bf16[32,4096]{1,0:T(8,128)(2,1)S(1)} %broadcast_select_fusion), channel_id=1, source_target_pairs={{0,1},{1,0},{2,3},{3,2},{4,5},{5,4},{6,7},{7,6},{8,9},{9,8},{10,11... | collective-permute-start | bytes 786440 | tf_op jit(solution)/shard_map/ppermute | solution.py:51
  21.2 1.8 %collective-permute-start.3 = (bf16[32,4096]{1,0:T(8,128)(2,1)S(1)}, bf16[32,4096]{1,0:T(8,128)(2,1)S(1)}, u32[]{:S(2)}, u32[]{:S(2)}) collective-permute-start(bf16[32,4096]{1,0:T(8,128)(2,1)S(1)} %maximum_select_fusion.2), channel_id=1, source_target_pairs={{0,1},{1,0},{2,3},{3,2},{4,5},{5,4},{6,7},{7,6},{8,9},{9,8},{10,11... | collective-permute-start | bytes 786440 | tf_op jit(solution)/shard_map/ppermute | solution.py:51
  25.6 24.2 %copy-start.2 = (bf16[64,512]{1,0:T(8,128)(2,1)S(1)}, bf16[64,512]{1,0:T(8,128)(2,1)}, u32[]{:S(2)}) copy-start(bf16[64,512]{1,0:T(8,128)(2,1)} %get-tuple-element.74) | copy-start | bytes 196612
  25.8 1.2 %collective-permute-start.4 = (f32[3,64]{1,0:T(4,128)S(1)}, f32[3,64]{1,0:T(4,128)S(1)}, u32[]{:S(2)}, u32[]{:S(2)}) collective-permute-start(f32[3,64]{1,0:T(4,128)S(1)} %pad_maximum_fusion), channel_id=1, source_target_pairs={{0,1},{1,0},{2,3},{3,2},{4,5},{5,4},{6,7},{7,6},{8,9},{9,8},{10,11... | collective-permute-start | bytes 2312 | tf_op jit(solution)/shard_map/ppermute | solution.py:51
  26.2 4.8 %collective-permute-start.19 = (bf16[32,4096]{1,0:T(8,128)(2,1)S(1)}, bf16[32,4096]{1,0:T(8,128)(2,1)S(1)}, u32[]{:S(2)}, u32[]{:S(2)}) collective-permute-start(bf16[32,4096]{1,0:T(8,128)(2,1)S(1)} %maximum_select_fusion.3), channel_id=1, source_target_pairs={{0,1},{1,0},{2,3},{3,2},{4,5},{5,4},{6,7},{7,6},{8,9},{9,8},{10,11... | collective-permute-start | bytes 786440 | tf_op jit(solution)/shard_map/ppermute | solution.py:51
  26.5 1.6 %collective-permute-start.5 = (bf16[32,4096]{1,0:T(8,128)(2,1)S(1)}, bf16[32,4096]{1,0:T(8,128)(2,1)S(1)}, u32[]{:S(2)}, u32[]{:S(2)}) collective-permute-start(bf16[32,4096]{1,0:T(8,128)(2,1)S(1)} %select_convert_fusion), channel_id=1, source_target_pairs={{0,1},{1,0},{2,3},{3,2},{4,5},{5,4},{6,7},{7,6},{8,9},{9,8},{10,11... | collective-permute-start | bytes 786440 | tf_op jit(solution)/shard_map/ppermute | solution.py:51
  28.3 3.7 %collective-permute-start.6 = (f32[3,64]{1,0:T(4,128)S(1)}, f32[3,64]{1,0:T(4,128)S(1)}, u32[]{:S(2)}, u32[]{:S(2)}) collective-permute-start(f32[3,64]{1,0:T(4,128)S(1)} %pad_maximum_fusion.1), channel_id=1, source_target_pairs={{0,2},{1,3},{2,0},{3,1},{4,6},{5,7},{6,4},{7,5},{8,10},{9,11},{10,... | collective-permute-start | bytes 2312 | tf_op jit(solution)/shard_map/ppermute | solution.py:51
  28.9 9.3 %collective-permute-start.13 = (bf16[16,4096]{1,0:T(8,128)(2,1)S(1)}, bf16[16,4096]{1,0:T(8,128)(2,1)S(1)}, u32[]{:S(2)}, u32[]{:S(2)}) collective-permute-start(bf16[16,4096]{1,0:T(8,128)(2,1)S(1)} %broadcast_select_fusion.1), channel_id=1, source_target_pairs={{0,2},{1,3},{2,0},{3,1},{4,6},{5,7},{6,4},{7,5},{8,10},{9,11},{10,... | collective-permute-start | bytes 393224 | tf_op jit(solution)/shard_map/ppermute | solution.py:51
  30.4 6.7 %collective-permute-start.7 = (bf16[16,4096]{1,0:T(8,128)(2,1)S(1)}, bf16[16,4096]{1,0:T(8,128)(2,1)S(1)}, u32[]{:S(2)}, u32[]{:S(2)}) collective-permute-start(bf16[16,4096]{1,0:T(8,128)(2,1)S(1)} %select_convert_fusion.1), channel_id=1, source_target_pairs={{0,2},{1,3},{2,0},{3,1},{4,6},{5,7},{6,4},{7,5},{8,10},{9,11},{10,... | collective-permute-start | bytes 393224 | tf_op jit(solution)/shard_map/ppermute | solution.py:51
  37.3 3.7 %collective-permute-start.8 = (f32[3,64]{1,0:T(4,128)S(1)}, f32[3,64]{1,0:T(4,128)S(1)}, u32[]{:S(2)}, u32[]{:S(2)}) collective-permute-start(f32[3,64]{1,0:T(4,128)S(1)} %pad_maximum_fusion.2), channel_id=1, source_target_pairs={{0,4},{1,5},{2,6},{3,7},{4,0},{5,1},{6,2},{7,3},{8,12},{9,13},{10,... | collective-permute-start | bytes 2312 | tf_op jit(solution)/shard_map/ppermute | solution.py:51
  38.2 8.4 %collective-permute-start.14 = (bf16[8,4096]{1,0:T(8,128)(2,1)S(1)}, bf16[8,4096]{1,0:T(8,128)(2,1)S(1)}, u32[]{:S(2)}, u32[]{:S(2)}) collective-permute-start(bf16[8,4096]{1,0:T(8,128)(2,1)S(1)} %broadcast_select_fusion.2), channel_id=1, source_target_pairs={{0,4},{1,5},{2,6},{3,7},{4,0},{5,1},{6,2},{7,3},{8,12},{9,13},{10,... | collective-permute-start | bytes 196616 | tf_op jit(solution)/shard_map/ppermute | solution.py:51
  39.5 4.3 %collective-permute-start.9 = (bf16[8,4096]{1,0:T(8,128)(2,1)S(1)}, bf16[8,4096]{1,0:T(8,128)(2,1)S(1)}, u32[]{:S(2)}, u32[]{:S(2)}) collective-permute-start(bf16[8,4096]{1,0:T(8,128)(2,1)S(1)} %select_convert_fusion.3), channel_id=1, source_target_pairs={{0,4},{1,5},{2,6},{3,7},{4,0},{5,1},{6,2},{7,3},{8,12},{9,13},{10,... | collective-permute-start | bytes 196616 | tf_op jit(solution)/shard_map/ppermute | solution.py:51
  43.9 5.7 %collective-permute-start.10 = (f32[3,64]{1,0:T(4,128)S(1)}, f32[3,64]{1,0:T(4,128)S(1)}, u32[]{:S(2)}, u32[]{:S(2)}) collective-permute-start(f32[3,64]{1,0:T(4,128)S(1)} %pad_maximum_fusion.3), channel_id=1, source_target_pairs={{0,8},{1,9},{2,10},{3,11},{4,12},{5,13},{6,14},{7,15},{8,0},{9,1},... | collective-permute-start | bytes 2312 | tf_op jit(solution)/shard_map/ppermute | solution.py:51
  46.6 6.8 %collective-permute-start.15 = (bf16[4,4096]{1,0:T(4,128)(2,1)S(1)}, bf16[4,4096]{1,0:T(4,128)(2,1)S(1)}, u32[]{:S(2)}, u32[]{:S(2)}) collective-permute-start(bf16[4,4096]{1,0:T(4,128)(2,1)S(1)} %broadcast_select_fusion.3), channel_id=1, source_target_pairs={{0,8},{1,9},{2,10},{3,11},{4,12},{5,13},{6,14},{7,15},{8,0},{9,1},... | collective-permute-start | bytes 98312 | tf_op jit(solution)/shard_map/ppermute | solution.py:51
  47.0 6.4 %collective-permute-start.11 = (bf16[4,4096]{1,0:T(4,128)(2,1)S(1)}, bf16[4,4096]{1,0:T(4,128)(2,1)S(1)}, u32[]{:S(2)}, u32[]{:S(2)}) collective-permute-start(bf16[4,4096]{1,0:T(4,128)(2,1)S(1)} %select_convert_fusion.6), channel_id=1, source_target_pairs={{0,8},{1,9},{2,10},{3,11},{4,12},{5,13},{6,14},{7,15},{8,0},{9,1},... | collective-permute-start | bytes 98312 | tf_op jit(solution)/shard_map/ppermute | solution.py:51

commit v3 on v2

v3 whole, which is shorter than its diff:
```python
import functools

import jax
import jax.numpy as jnp
from jax import lax
from jax.experimental import pallas as pl
from jax.experimental.pallas import tpu as pltpu
from jax.sharding import PartitionSpec as P

NEG = -1e30
f32, bf16, i32 = jnp.float32, jnp.bfloat16, jnp.int32


def prepare(mine, steps, me, table_h, ids_h, language_h, allowed_h, target_h, weight_h,
            code_o, took_o, weight_o, pick_o,
            ids, language, allowed, target, weight, sem):
    del table_h
    small = [
        pltpu.make_async_copy(src, dst, sem.at[i])
        for i, (src, dst) in enumerate((
            (target_h, target), (ids_h, ids), (language_h, language), (weight_h, weight), (allowed_h, allowed)))
    ]
    for copy in small:
        copy.start()
    for copy in small:
        copy.wait()
    rank = me[0, 0]
    n = 1 << steps
    tokens = mine * n
    half = tokens // 2
    cols = took_o.shape[1]
    place = lax.broadcasted_iota(i32, (tokens, 1), 0)
    block = lax.div(place, mine)
    source = place - block * mine
    for i in range(steps):
        source = source + mine * (n >> (i + 1)) * (lax.shift_right_logical(block, i) & 1)
    here = source == lax.broadcasted_iota(i32, (tokens, tokens), 1)

    def column(ref):
        return jnp.sum(jnp.where(here, ref[...], jnp.zeros_like(ref[...])), axis=1, keepdims=True)

    vocab = rank * cols + lax.broadcasted_iota(i32, (1, cols), 1)
    pick = (column(target) == vocab).astype(f32)
    took_o[...] = (column(ids) == vocab).astype(f32).astype(bf16)
    langs, blocks = allowed.shape
    speaks = (column(language) == lax.broadcasted_iota(i32, (1, langs), 1)).astype(f32)
    may = jnp.dot(speaks, allowed[...].astype(f32), preferred_element_type=f32)
    column_here = lax.broadcasted_iota(i32, (1, blocks), 1) == rank
    ok = jnp.sum(jnp.where(column_here, may, 0.0), axis=1, keepdims=True)
    code_o[...] = (jnp.where(ok > 0.0, 1.0, 0.0) * (1.0 + pick)).astype(bf16)
    weight_o[...] = jnp.broadcast_to(column(weight), weight_o.shape)
    upper = (rank & 1) == 1
    pick_o[...] = jnp.where(upper, jnp.concatenate([pick[half:], pick[:half]], 0), pick).astype(bf16)


def per_device(n, hidden, embedding, d_input, input_ids, language, allowed, target, token_weight):
    cols, width = embedding.shape
    mine = hidden.shape[0]
    tokens = mine * n
    steps = n.bit_length() - 1
    me = lax.axis_index("vocab")

    def swap(x, k):
        return lax.ppermute(x, "vocab", [(i, i ^ k) for i in range(n)])

    def bit(k):
        return (me & k) != 0

    def after(x, *deps):
        return lax.optimization_barrier((x,) + deps)[0]

    def join(x, r, k):
        return jnp.where(bit(k), jnp.concatenate([r, x], 0), jnp.concatenate([x, r], 0))

    def halves(x, k):
        h = x.shape[0] // 2
        a, b = x[:h], x[h:]
        return jnp.where(bit(k), b, a), jnp.where(bit(k), a, b)

    first = swap(hidden, n // 2)
    first_input = swap(d_input, n // 2)
    vmem, hbm = pl.BlockSpec(memory_space=pltpu.VMEM), pl.BlockSpec(memory_space=pltpu.HBM)
    code, took, weight, pick = pl.pallas_call(
        functools.partial(prepare, mine, steps),
        out_shape=(
            jax.ShapeDtypeStruct((tokens, cols), bf16),
            jax.ShapeDtypeStruct((tokens, cols), bf16),
            jax.ShapeDtypeStruct((tokens, cols), f32),
            jax.ShapeDtypeStruct((tokens, cols), bf16),
        ),
        in_specs=[pl.BlockSpec(memory_space=pltpu.SMEM)] + [hbm] * 6,
        out_specs=(vmem,) * 4,
        scratch_shapes=[
            pltpu.VMEM((1, tokens), i32),
            pltpu.VMEM((1, tokens), i32),
            pltpu.VMEM(allowed.shape, i32),
            pltpu.VMEM((1, tokens), i32),
            pltpu.VMEM((1, tokens), f32),
            pltpu.SemaphoreType.DMA((5,)),
        ],
        compiler_params=pltpu.CompilerParams(vmem_limit_bytes=60 * 1024 * 1024),
        name="prepare",
    )(
        me.reshape(1, 1), embedding, input_ids.reshape(1, tokens), language.reshape(1, tokens),
        allowed, target.reshape(1, tokens), token_weight.reshape(1, tokens),
    )
    usable = code > 0
    is_target = code > 1

    k = n // 2
    all_hidden, all_input = join(hidden, first, k), join(d_input, first_input, k)
    k //= 2
    while k > 2:
        got, got_input = swap(all_hidden, k), swap(all_input, k)
        all_hidden, all_input = join(all_hidden, got, k), join(all_input, got_input, k)
        k //= 2
    got = swap(all_hidden, 2)
    half = tokens // 2
    rows = jnp.dot(after(pick, all_hidden), embedding, preferred_element_type=f32).astype(bf16)
    rows = rows[:half] + swap(rows[half:], 1)
    rows_keep, rows_send = halves(rows, 2)
    rows_got = swap(rows_send, 2)
    input_got = swap(after(all_input, all_hidden), 2)
    all_hidden = join(all_hidden, got, 2)
    all_hidden = join(all_hidden, swap(all_hidden, 1), 1)

    logits = lax.dot_general(all_hidden, embedding, (((1,), (1,)), ((), ())), preferred_element_type=f32)
    masked = jnp.where(usable, logits, f32(NEG))
    m = jnp.max(masked, axis=1)
    p = jnp.where(usable, jnp.exp(masked - m[:, None]), f32(0.0))
    s = jnp.sum(p, axis=1)
    lt = jnp.max(jnp.where(is_target, masked, f32(NEG)), axis=1)
    p = after(jnp.where(is_target, f32(0.0), p).astype(bf16), m, s, lt)
    part = jnp.dot(p, embedding, preferred_element_type=f32)

    lo = 0
    k = 1
    while k < n:
        last = k == n // 2
        keep, send = halves(part, k)
        send = send.astype(bf16)
        if last:
            rows_keep, rows_send = halves(rows, k)
            send = jnp.concatenate([send, rows_send], 0)
        packed = jnp.stack([m, s, lt])
        if k > 1:
            packed, send = lax.optimization_barrier((packed, send))
        got = swap(packed, k)
        recv = swap(send, k)
        size = keep.shape[0]
        if last:
            rows = rows_keep + recv[size:]
        m_new = jnp.maximum(m, got[0])
        a, b = jnp.exp(m - m_new), jnp.exp(got[0] - m_new)
        s = s * a + got[1] * b
        lt = jnp.maximum(lt, got[2])
        m, s, lt, a, b = lax.optimization_barrier((m_new, s, lt, a, b))
        if k == 1:
            rows = rows_keep + after(rows_got, m)
            all_input = join(all_input, after(input_got, m), 2)
            all_input = join(all_input, swap(all_input, 1), 1)
        elif 2 < k < n // 2:
            rows = rows_keep + after(rows_got, m)
        if 1 < k < n // 4:
            rows_keep, rows_send = halves(after(rows, m), 2 * k)
            rows_got = swap(rows_send, 2 * k)
        lo = lo + jnp.where(bit(k), size, 0)
        part = keep * lax.dynamic_slice_in_dim(a, lo, size)[:, None] + recv[:size].astype(f32) * lax.dynamic_slice_in_dim(b, lo, size)[:, None]
        k *= 2

    hot = is_target.astype(f32)
    d_logits = jnp.where(
        usable, weight * (jnp.exp(masked - m[:, None]) / s[:, None] - hot), f32(0.0)
    ).astype(bf16)
    w = lax.dynamic_slice_in_dim(token_weight, me * mine, mine)
    m_own, s_own, lt_own = (lax.dynamic_slice_in_dim(x, lo, mine) for x in (m, s, lt))
    coef = (w * (jnp.exp(lt_own - m_own) / s_own - 1.0)).astype(bf16).astype(f32)
    d_hidden = (part * (w / s_own)[:, None] + rows.astype(f32) * coef[:, None]).astype(bf16)
    d_embed = lax.dot_general(
        jnp.concatenate([d_logits, took], 0),
        jnp.concatenate([all_hidden, all_input], 0),
        (((0,), (0,)), ((), ())),
        preferred_element_type=f32,
    ).astype(bf16)
    return d_hidden, d_embed


def solution(mesh):
    n = mesh.shape["vocab"]
    placed = (
        P(("groups", "vocab"), None),
        P(("groups", "vocab"), None),
        P(("groups", "vocab"), None),
        P("groups"),
        P("groups"),
        P("groups", None),
        P("groups"),
        P("groups"),
    )
    return jax.shard_map(
        functools.partial(per_device, n),
        mesh=mesh,
        in_specs=placed,
        out_specs=(P(("groups", "vocab"), None), P(("groups", "vocab"), None)),
        check_vma=False,
    )
```

time: 54.6 us -> 49.4 us (0.905)
  other arithmetic: 5.62 us -> 2.29 us
  starting transfers between devices: 22.7 us -> 21.7 us
    select_n x8, other arithmetic: 2.12 us -> 0.44 us  [join(): jnp.where(bit(k), jnp.concatenate([r, x], 0), jnp.concatenate([x, r], 0))]
    ppermute x20 -> x19, starting transfers between devices: 22.7 us -> 21.7 us  [swap(): return lax.ppermute(x, 'vocab', [(i, i ^ k) for i in range(n)])]
    pallas_call x1 -> x0, other arithmetic: 0.87 us -> none  [per_device(): pl.pallas_call(functools.partial(prepare, mine, steps), out_shape=(jax.Sh...]
    gt x1 -> x0, other arithmetic: 0.86 us -> none  [per_device(): usable = ok > 0.0]
    ppermute x20 -> x19, waiting for transfers between devices: 13.6 us -> 13.1 us  [swap(): return lax.ppermute(x, 'vocab', [(i, i ^ k) for i in range(n)])]
  transfers between devices with their start and end apart: 20 -> 19, of which waited for: 10 -> 12; matrix products, arithmetic and copies ran while one was open for 27% -> 22% of each run, Pallas kernels for 3% -> 4%
where the time goes in v3:
time: 49.4 us; the launch traced here: 49.2 us
  starting transfers between devices  21.7 us (44%)
  waiting for transfers between devices  13.1 us (27%)
  matrix products  8.69 us (18%)
  other arithmetic  2.29 us (5%)
  Pallas kernels  1.79 us (4%)
  between operations  0.94 us (2%)
  local copies, waits for them, and re-layouts  0.67 us (1%)
    ppermute x19, starting transfers between devices, swap(): return lax.ppermute(x, 'vocab', [(i, i ^ k) for i in range(n)])  21.7 us
    ppermute x19, waiting for transfers between devices, swap(): return lax.ppermute(x, 'vocab', [(i, i ^ k) for i in range(n)])  13.1 us
    dot_general x1, matrix products, per_device(): lax.dot_general(jnp.concatenate([d_logits, took], 0), jnp.concatenate([al...  3.29 us
    dot_general x1, matrix products, per_device(): jnp.dot(after(pick, all_hidden), embedding, preferred_element_type=f32)  3.07 us
    pallas_call x1, Pallas kernels, per_device(): pl.pallas_call(functools.partial(prepare, mine, steps), out_shape=(jax.Sh...  1.79 us
    dot_general x1, matrix products, per_device(): lax.dot_general(all_hidden, embedding, (((1,), (1,)), ((), ())), preferre...  1.49 us
  transfers between devices with their start and end apart: 19, of which 12 were waited for; matrix products, arithmetic and copies ran while one was open for 22% of the time, Pallas kernels for 4%

profile of v3, /device:TPU:0, one launch (start us, length us, event | category | flops | bytes accessed | tf_op | source)
XLA Modules:
  0.0 49.2 jit_solution(9958167155092538153)
XLA Ops:
  0.7 4.1 %collective-permute-start = (bf16[4,4096]{1,0:T(4,128)(2,1)}, bf16[4,4096]{1,0:T(4,128)(2,1)S(1)}, u32[]{:S(2)}, u32[]{:S(2)}) collective-permute-start(bf16[4,4096]{1,0:T(4,128)(2,1)} %param.8), channel_id=1, source_target_pairs={{0,8},{1,9},{2,10},{3,11},{4,12},{5,13},{6,14},{7,15},{8,0},{9,1},... | collective-permute-start | bytes 98312 | tf_op jit(solution)/shard_map/ppermute | solution.py:64
  4.8 0.1 collective-permute-start.15
  4.8 1.8 %prepare.1 = (bf16[64,512]{1,0:T(8,128)(2,1)}, bf16[64,512]{1,0:T(8,128)(2,1)}, f32[64,512]{1,0:T(8,128)}, bf16[64,512]{1,0:T(8,128)(2,1)}) custom-call(s32[1,1]{1,0:T(1,128)} %bitcast.me, bf16[512,4096]{1,0:T(8,128)(2,1)} %table_h.1, s32[1,64]{1,0:T(1,128)} %bitcast.88, s32[1,64]{1,0:T(1,128)} %bitcast.89, s32[16,16]{1,0:T(8,128)} %allowed_h.1, ...), custom_call_target="tpu_custom_call" | custom-call | tf_op jit(solution)/shard_map/prepare/pallas_call | solution.py:83
  6.6 0.6 %collective-permute-done = bf16[4,4096]{1,0:T(4,128)(2,1)S(1)} collective-permute-done((bf16[4,4096]{1,0:T(4,128)(2,1)}, bf16[4,4096]{1,0:T(4,128)(2,1)S(1)}, u32[]{:S(2)}, u32[]{:S(2)}) %collective-permute-start) | collective-permute-done | bytes 32800 | tf_op jit(solution)/shard_map/ppermute | solution.py:64
  7.3 1.8 %collective-permute-start.1 = (bf16[8,4096]{1,0:T(8,128)(2,1)S(1)}, bf16[8,4096]{1,0:T(8,128)(2,1)S(1)}, u32[]{:S(2)}, u32[]{:S(2)}) collective-permute-start(bf16[8,4096]{1,0:T(8,128)(2,1)S(1)} %maximum_select_fusion.6), channel_id=1, source_target_pairs={{0,4},{1,5},{2,6},{3,7},{4,0},{5,1},{6,2},{7,3},{8,12},{9,13},{10,... | collective-permute-start | bytes 196616 | tf_op jit(solution)/shard_map/ppermute | solution.py:64
  9.1 0.8 %collective-permute-done.15 = bf16[4,4096]{1,0:T(4,128)(2,1)S(1)} collective-permute-done((bf16[4,4096]{1,0:T(4,128)(2,1)}, bf16[4,4096]{1,0:T(4,128)(2,1)S(1)}, u32[]{:S(2)}, u32[]{:S(2)}) %collective-permute-start.15) | collective-permute-done | bytes 32800 | tf_op jit(solution)/shard_map/ppermute | solution.py:64
  10.0 1.5 %collective-permute-start.16 = (bf16[8,4096]{1,0:T(8,128)(2,1)S(1)}, bf16[8,4096]{1,0:T(8,128)(2,1)S(1)}, u32[]{:S(2)}, u32[]{:S(2)}) collective-permute-start(bf16[8,4096]{1,0:T(8,128)(2,1)S(1)} %maximum_select_fusion.7), channel_id=1, source_target_pairs={{0,4},{1,5},{2,6},{3,7},{4,0},{5,1},{6,2},{7,3},{8,12},{9,13},{10,... | collective-permute-start | bytes 196616 | tf_op jit(solution)/shard_map/ppermute | solution.py:64
  11.5 0.6 %collective-permute-done.1 = bf16[8,4096]{1,0:T(8,128)(2,1)S(1)} collective-permute-done((bf16[8,4096]{1,0:T(8,128)(2,1)S(1)}, bf16[8,4096]{1,0:T(8,128)(2,1)S(1)}, u32[]{:S(2)}, u32[]{:S(2)}) %collective-permute-start.1) | collective-permute-done | bytes 65568 | tf_op jit(solution)/shard_map/ppermute | solution.py:64
  12.2 1.9 %collective-permute-start.2 = (bf16[16,4096]{1,0:T(8,128)(2,1)S(1)}, bf16[16,4096]{1,0:T(8,128)(2,1)S(1)}, u32[]{:S(2)}, u32[]{:S(2)}) collective-permute-start(bf16[16,4096]{1,0:T(8,128)(2,1)S(1)} %maximum_select_fusion.4), channel_id=1, source_target_pairs={{0,2},{1,3},{2,0},{3,1},{4,6},{5,7},{6,4},{7,5},{8,10},{9,11},{10,... | collective-permute-start | bytes 393224 | tf_op jit(solution)/shard_map/ppermute | solution.py:64
  14.1 0.2 collective-permute-done.16
  14.3 1.6 %collective-permute-start.17 = (bf16[16,4096]{1,0:T(8,128)(2,1)S(1)}, bf16[16,4096]{1,0:T(8,128)(2,1)S(1)}, u32[]{:S(2)}, u32[]{:S(2)}) collective-permute-start(bf16[16,4096]{1,0:T(8,128)(2,1)S(1)} %maximum_select_fusion.5), channel_id=1, source_target_pairs={{0,2},{1,3},{2,0},{3,1},{4,6},{5,7},{6,4},{7,5},{8,10},{9,11},{10,... | collective-permute-start | bytes 393224 | tf_op jit(solution)/shard_map/ppermute | solution.py:64
  15.9 3.1 %convolution_convert_fusion.1 = bf16[64,4096]{1,0:T(8,128)(2,1)S(1)} fusion(bf16[64,512]{1,0:T(8,128)(2,1)} %get-tuple-element.61, bf16[512,4096]{1,0:T(8,128)(2,1)} %table_h.1), kind=kOutput, calls=%fused_computation.1 | convolution fusion | flops 268697600 | bytes 4784128 | tf_op jit(solution)/shard_map/dot_general | solution.py:119
  19.1 0.5 %collective-permute-start.3 = (bf16[32,4096]{1,0:T(8,128)(2,1)S(1)}, bf16[32,4096]{1,0:T(8,128)(2,1)S(1)}, u32[]{:S(2)}, u32[]{:S(2)}) collective-permute-start(bf16[32,4096]{1,0:T(8,128)(2,1)S(1)} %maximum_select_fusion.2), channel_id=1, source_target_pairs={{0,1},{1,0},{2,3},{3,2},{4,5},{5,4},{6,7},{7,6},{8,9},{9,8},{10,11... | collective-permute-start | bytes 786440 | tf_op jit(solution)/shard_map/ppermute | solution.py:64
  19.7 0.9 %collective-permute-done.10 = bf16[32,4096]{1,0:T(8,128)(2,1)S(1)} collective-permute-done((bf16[32,4096]{1,0:T(8,128)(2,1)S(1)}, bf16[32,4096]{1,0:T(8,128)(2,1)S(1)}, u32[]{:S(2)}, u32[]{:S(2)}) %collective-permute-start.10) | collective-permute-done | bytes 262176 | tf_op jit(solution)/shard_map/ppermute | solution.py:64
  20.6 0.6 %collective-permute-start.11 = (bf16[16,4096]{1,0:T(8,128)(2,1)S(1)}, bf16[16,4096]{1,0:T(8,128)(2,1)S(1)}, u32[]{:S(2)}, u32[]{:S(2)}) collective-permute-start(bf16[16,4096]{1,0:T(8,128)(2,1)S(1)} %broadcast_select_fusion), channel_id=1, source_target_pairs={{0,2},{1,3},{2,0},{3,1},{4,6},{5,7},{6,4},{7,5},{8,10},{9,11},{10,... | collective-permute-start | bytes 393224 | tf_op jit(solution)/shard_map/ppermute | solution.py:64
  21.2 0.1 maximum_select_fusion
  21.3 1.5 %fusion.20 = (f32[64]{0:T(128)S(1)}, f32[64,512]{1,0:T(8,128)S(1)}) fusion(bf16[64,4096]{1,0:T(8,128)(2,1)S(1)} %maximum_select_fusion, bf16[512,4096]{1,0:T(8,128)(2,1)S(1)} %copy-done, bf16[64,512]{1,0:T(8,128)(2,1)S(1)} %copy-done.1), kind=kOutput, calls=%fused_computation.76 | convolution fusion | flops 268533696 | bytes 4915456 | tf_op jit(solution)/shard_map/dot_general | solution.py:127
  22.8 0.2 fusion.6
  23.1 0.8 %fusion.21 = f32[64,4096]{1,0:T(8,128)S(1)} fusion(bf16[64,512]{1,0:T(8,128)(2,1)S(1)} %get-tuple-element.40, bf16[512,4096]{1,0:T(8,128)(2,1)S(1)} %copy-done), kind=kOutput, calls=%fused_computation.77 | convolution fusion | flops 268435456 | bytes 5308416 | tf_op jit(solution)/shard_map/dot_general | solution.py:134
  24.1 0.6 %collective-permute-start.5 = (bf16[32,4096]{1,0:T(8,128)(2,1)S(1)}, bf16[32,4096]{1,0:T(8,128)(2,1)S(1)}, u32[]{:S(2)}, u32[]{:S(2)}) collective-permute-start(bf16[32,4096]{1,0:T(8,128)(2,1)S(1)} %select_convert_fusion), channel_id=1, source_target_pairs={{0,1},{1,0},{2,3},{3,2},{4,5},{5,4},{6,7},{7,6},{8,9},{9,8},{10,11... | collective-permute-start | bytes 786440 | tf_op jit(solution)/shard_map/ppermute | solution.py:64
  24.7 0.1 dynamic_slice.36
  24.8 0.1 dynamic_slice.37
  24.9 1.3 %collective-permute-done.11 = bf16[16,4096]{1,0:T(8,128)(2,1)S(1)} collective-permute-done((bf16[16,4096]{1,0:T(8,128)(2,1)S(1)}, bf16[16,4096]{1,0:T(8,128)(2,1)S(1)}, u32[]{:S(2)}, u32[]{:S(2)}) %collective-permute-start.11) | collective-permute-done | bytes 131104 | tf_op jit(solution)/shard_map/ppermute | solution.py:64
  26.3 0.2 multiply_add_fusion
  26.5 1.1 %collective-permute-start.6 = (f32[3,64]{1,0:T(4,128)S(1)}, f32[3,64]{1,0:T(4,128)S(1)}, u32[]{:S(2)}, u32[]{:S(2)}) collective-permute-start(f32[3,64]{1,0:T(4,128)S(1)} %pad_maximum_fusion.2), channel_id=1, source_target_pairs={{0,2},{1,3},{2,0},{3,1},{4,6},{5,7},{6,4},{7,5},{8,10},{9,11},{10,... | collective-permute-start | bytes 2312 | tf_op jit(solution)/shard_map/ppermute | solution.py:64
  27.6 1.1 %collective-permute-start.7 = (bf16[16,4096]{1,0:T(8,128)(2,1)S(1)}, bf16[16,4096]{1,0:T(8,128)(2,1)S(1)}, u32[]{:S(2)}, u32[]{:S(2)}) collective-permute-start(bf16[16,4096]{1,0:T(8,128)(2,1)S(1)} %select_convert_fusion.1), channel_id=1, source_target_pairs={{0,2},{1,3},{2,0},{3,1},{4,6},{5,7},{6,4},{7,5},{8,10},{9,11},{10,... | collective-permute-start | bytes 393224 | tf_op jit(solution)/shard_map/ppermute | solution.py:64
  28.6 1.5 %collective-permute-done.6 = f32[3,64]{1,0:T(4,128)S(1)} collective-permute-done((f32[3,64]{1,0:T(4,128)S(1)}, f32[3,64]{1,0:T(4,128)S(1)}, u32[]{:S(2)}, u32[]{:S(2)}) %collective-permute-start.6) | collective-permute-done | bytes 800 | tf_op jit(solution)/shard_map/ppermute | solution.py:64
  30.1 0.1 dynamic_slice.38
  30.2 0.1 dynamic_slice.39
  30.3 2.8 %collective-permute-done.7 = bf16[16,4096]{1,0:T(8,128)(2,1)S(1)} collective-permute-done((bf16[16,4096]{1,0:T(8,128)(2,1)S(1)}, bf16[16,4096]{1,0:T(8,128)(2,1)S(1)}, u32[]{:S(2)}, u32[]{:S(2)}) %collective-permute-start.7) | collective-permute-done | bytes 131104 | tf_op jit(solution)/shard_map/ppermute | solution.py:64
  33.1 0.1 multiply_add_fusion.1
  33.3 1.5 %collective-permute-start.8 = (f32[3,64]{1,0:T(4,128)S(1)}, f32[3,64]{1,0:T(4,128)S(1)}, u32[]{:S(2)}, u32[]{:S(2)}) collective-permute-start(f32[3,64]{1,0:T(4,128)S(1)} %pad_maximum_fusion.3), channel_id=1, source_target_pairs={{0,4},{1,5},{2,6},{3,7},{4,0},{5,1},{6,2},{7,3},{8,12},{9,13},{10,... | collective-permute-start | bytes 2312 | tf_op jit(solution)/shard_map/ppermute | solution.py:64
  34.8 0.6 %collective-permute-start.12 = (bf16[8,4096]{1,0:T(8,128)(2,1)S(1)}, bf16[8,4096]{1,0:T(8,128)(2,1)S(1)}, u32[]{:S(2)}, u32[]{:S(2)}) collective-permute-start(bf16[8,4096]{1,0:T(8,128)(2,1)S(1)} %broadcast_select_fusion.1), channel_id=1, source_target_pairs={{0,4},{1,5},{2,6},{3,7},{4,0},{5,1},{6,2},{7,3},{8,12},{9,13},{10,... | collective-permute-start | bytes 196616 | tf_op jit(solution)/shard_map/ppermute | solution.py:64
  35.4 1.5 %collective-permute-start.9 = (bf16[8,4096]{1,0:T(8,128)(2,1)S(1)}, bf16[8,4096]{1,0:T(8,128)(2,1)S(1)}, u32[]{:S(2)}, u32[]{:S(2)}) collective-permute-start(bf16[8,4096]{1,0:T(8,128)(2,1)S(1)} %select_convert_fusion.3), channel_id=1, source_target_pairs={{0,4},{1,5},{2,6},{3,7},{4,0},{5,1},{6,2},{7,3},{8,12},{9,13},{10,... | collective-permute-start | bytes 196616 | tf_op jit(solution)/shard_map/ppermute | solution.py:64
  36.9 0.1 dynamic_slice.40
  37.1 2.1 %collective-permute-done.12 = bf16[8,4096]{1,0:T(8,128)(2,1)S(1)} collective-permute-done((bf16[8,4096]{1,0:T(8,128)(2,1)S(1)}, bf16[8,4096]{1,0:T(8,128)(2,1)S(1)}, u32[]{:S(2)}, u32[]{:S(2)}) %collective-permute-start.12) | collective-permute-done | bytes 65568 | tf_op jit(solution)/shard_map/ppermute | solution.py:64
  39.2 0.6 %collective-permute-done.9 = bf16[8,4096]{1,0:T(8,128)(2,1)S(1)} collective-permute-done((bf16[8,4096]{1,0:T(8,128)(2,1)S(1)}, bf16[8,4096]{1,0:T(8,128)(2,1)S(1)}, u32[]{:S(2)}, u32[]{:S(2)}) %collective-permute-start.9) | collective-permute-done | bytes 65568 | tf_op jit(solution)/shard_map/ppermute | solution.py:64
  39.8 0.1 multiply_add_fusion.2
  40.0 2.4 %collective-permute-start.13 = (f32[3,64]{1,0:T(4,128)S(1)}, f32[3,64]{1,0:T(4,128)S(1)}, u32[]{:S(2)}, u32[]{:S(2)}) collective-permute-start(f32[3,64]{1,0:T(4,128)S(1)} %pad_maximum_fusion.4), channel_id=1, source_target_pairs={{0,8},{1,9},{2,10},{3,11},{4,12},{5,13},{6,14},{7,15},{8,0},{9,1},... | collective-permute-start | bytes 2312 | tf_op jit(solution)/shard_map/ppermute | solution.py:64
  42.4 0.1 maximum_select_fusion.1
  42.5 0.7 %collective-permute-start.14 = (bf16[8,4096]{1,0:T(8,128)(2,1)S(1)}, bf16[8,4096]{1,0:T(8,128)(2,1)S(1)}, u32[]{:S(2)}, u32[]{:S(2)}) collective-permute-start(bf16[8,4096]{1,0:T(8,128)(2,1)S(1)} %pad_maximum_fusion), channel_id=1, source_target_pairs={{0,8},{1,9},{2,10},{3,11},{4,12},{5,13},{6,14},{7,15},{8,0},{9,1},... | collective-permute-start | bytes 196616 | tf_op jit(solution)/shard_map/ppermute | solution.py:64
  43.2 1.4 %collective-permute-done.13 = f32[3,64]{1,0:T(4,128)S(1)} collective-permute-done((f32[3,64]{1,0:T(4,128)S(1)}, f32[3,64]{1,0:T(4,128)S(1)}, u32[]{:S(2)}, u32[]{:S(2)}) %collective-permute-start.13) | collective-permute-done | bytes 800 | tf_op jit(solution)/shard_map/ppermute | solution.py:64
  44.6 0.1 dynamic_slice.42
  44.8 0.1 select_convert_fusion.2
  44.9 3.3 %convolution_convert_fusion = bf16[512,4096]{1,0:T(8,128)(2,1)} fusion(bf16[64,4096]{1,0:T(8,128)(2,1)S(1)} %maximum_select_fusion.1, bf16[64,4096]{1,0:T(8,128)(2,1)S(1)} %maximum_select_fusion, bf16[64,512]{1,0:T(8,128)(2,1)S(1)} %copy-done.3, bf16[64,512]{1,0:T(8,128)(2,1)S(1)} %select_convert_fusion.2), kind=kOutput, calls=%fused_computation | convolution fusion | flops 541327360 | bytes 5373952 | tf_op jit(solution)/shard_map/dot_general | solution.py:179
  48.2 0.1 dynamic-slice_divide_fusion
  48.3 0.1 collective-permute-done.14
  48.4 0.7 %add_convert_fusion = bf16[4,4096]{1,0:T(4,128)(2,1)} fusion(f32[8,4096]{1,0:T(8,128)S(1)} %multiply_add_fusion.2, bf16[8,4096]{1,0:T(8,128)(2,1)S(1)} %collective-permute-done.14, f32[4]{0:T(128)S(1)} %get-tuple-element.100, f32[4]{0:T(128)S(1)} %get-tuple-element.99, f32[4]{0:T(128)S(1)} %dynamic_slice.43, f32[4]{0:T(128)S(1)} %dynamic_slice.42, ...), kind=kLoop, calls=%fused_computation.32 | loop fusion | flops 196608 | bytes 294977 | tf_op jit(solution)/shard_map/convert_element_type | solution.py:178
  (52 shorter events, 1.0 us)
Async XLA Ops:
  0.6 6.6 %copy-start.4 = (bf16[4,4096]{1,0:T(4,128)(2,1)S(1)}, bf16[4,4096]{1,0:T(4,128)(2,1)}, u32[]{:S(2)}) copy-start(bf16[4,4096]{1,0:T(4,128)(2,1)} %param.8) | copy-start | bytes 98308
  0.6 9.2 %copy-start.5 = (bf16[4,4096]{1,0:T(4,128)(2,1)S(1)}, bf16[4,4096]{1,0:T(4,128)(2,1)}, u32[]{:S(2)}) copy-start(bf16[4,4096]{1,0:T(4,128)(2,1)} %param.10) | copy-start | bytes 98308
  0.7 6.6 %collective-permute-start = (bf16[4,4096]{1,0:T(4,128)(2,1)}, bf16[4,4096]{1,0:T(4,128)(2,1)S(1)}, u32[]{:S(2)}, u32[]{:S(2)}) collective-permute-start(bf16[4,4096]{1,0:T(4,128)(2,1)} %param.8), channel_id=1, source_target_pairs={{0,8},{1,9},{2,10},{3,11},{4,12},{5,13},{6,14},{7,15},{8,0},{9,1},... | collective-permute-start | bytes 98312 | tf_op jit(solution)/shard_map/ppermute | solution.py:64
  4.8 5.1 %collective-permute-start.15 = (bf16[4,4096]{1,0:T(4,128)(2,1)}, bf16[4,4096]{1,0:T(4,128)(2,1)S(1)}, u32[]{:S(2)}, u32[]{:S(2)}) collective-permute-start(bf16[4,4096]{1,0:T(4,128)(2,1)} %param.10), channel_id=1, source_target_pairs={{0,8},{1,9},{2,10},{3,11},{4,12},{5,13},{6,14},{7,15},{8,0},{9,1},... | collective-permute-start | bytes 98312 | tf_op jit(solution)/shard_map/ppermute | solution.py:64
  7.3 4.8 %collective-permute-start.1 = (bf16[8,4096]{1,0:T(8,128)(2,1)S(1)}, bf16[8,4096]{1,0:T(8,128)(2,1)S(1)}, u32[]{:S(2)}, u32[]{:S(2)}) collective-permute-start(bf16[8,4096]{1,0:T(8,128)(2,1)S(1)} %maximum_select_fusion.6), channel_id=1, source_target_pairs={{0,4},{1,5},{2,6},{3,7},{4,0},{5,1},{6,2},{7,3},{8,12},{9,13},{10,... | collective-permute-start | bytes 196616 | tf_op jit(solution)/shard_map/ppermute | solution.py:64
  10.0 4.3 %collective-permute-start.16 = (bf16[8,4096]{1,0:T(8,128)(2,1)S(1)}, bf16[8,4096]{1,0:T(8,128)(2,1)S(1)}, u32[]{:S(2)}, u32[]{:S(2)}) collective-permute-start(bf16[8,4096]{1,0:T(8,128)(2,1)S(1)} %maximum_select_fusion.7), channel_id=1, source_target_pairs={{0,4},{1,5},{2,6},{3,7},{4,0},{5,1},{6,2},{7,3},{8,12},{9,13},{10,... | collective-permute-start | bytes 196616 | tf_op jit(solution)/shard_map/ppermute | solution.py:64
  12.1 9.2 %copy-start = (bf16[512,4096]{1,0:T(8,128)(2,1)S(1)}, bf16[512,4096]{1,0:T(8,128)(2,1)}, u32[]{:S(2)}) copy-start(bf16[512,4096]{1,0:T(8,128)(2,1)} %table_h.1) | copy-start | bytes 12582916
  12.2 9.2 %copy-start.1 = (bf16[64,512]{1,0:T(8,128)(2,1)S(1)}, bf16[64,512]{1,0:T(8,128)(2,1)}, u32[]{:S(2)}) copy-start(bf16[64,512]{1,0:T(8,128)(2,1)} %get-tuple-element.39) | copy-start | bytes 196612
  12.2 6.9 %collective-permute-start.2 = (bf16[16,4096]{1,0:T(8,128)(2,1)S(1)}, bf16[16,4096]{1,0:T(8,128)(2,1)S(1)}, u32[]{:S(2)}, u32[]{:S(2)}) collective-permute-start(bf16[16,4096]{1,0:T(8,128)(2,1)S(1)} %maximum_select_fusion.4), channel_id=1, source_target_pairs={{0,2},{1,3},{2,0},{3,1},{4,6},{5,7},{6,4},{7,5},{8,10},{9,11},{10,... | collective-permute-start | bytes 393224 | tf_op jit(solution)/shard_map/ppermute | solution.py:64
  14.3 10.3 %collective-permute-start.17 = (bf16[16,4096]{1,0:T(8,128)(2,1)S(1)}, bf16[16,4096]{1,0:T(8,128)(2,1)S(1)}, u32[]{:S(2)}, u32[]{:S(2)}) collective-permute-start(bf16[16,4096]{1,0:T(8,128)(2,1)S(1)} %maximum_select_fusion.5), channel_id=1, source_target_pairs={{0,2},{1,3},{2,0},{3,1},{4,6},{5,7},{6,4},{7,5},{8,10},{9,11},{10,... | collective-permute-start | bytes 393224 | tf_op jit(solution)/shard_map/ppermute | solution.py:64
  19.0 1.6 %collective-permute-start.10 = (bf16[32,4096]{1,0:T(8,128)(2,1)S(1)}, bf16[32,4096]{1,0:T(8,128)(2,1)S(1)}, u32[]{:S(2)}, u32[]{:S(2)}) collective-permute-start(bf16[32,4096]{1,0:T(8,128)(2,1)S(1)} %slice.133), channel_id=1, source_target_pairs={{0,1},{1,0},{2,3},{3,2},{4,5},{5,4},{6,7},{7,6},{8,9},{9,8},{10,11... | collective-permute-start | bytes 786440 | tf_op jit(solution)/shard_map/ppermute | solution.py:64
  19.1 2.1 %collective-permute-start.3 = (bf16[32,4096]{1,0:T(8,128)(2,1)S(1)}, bf16[32,4096]{1,0:T(8,128)(2,1)S(1)}, u32[]{:S(2)}, u32[]{:S(2)}) collective-permute-start(bf16[32,4096]{1,0:T(8,128)(2,1)S(1)} %maximum_select_fusion.2), channel_id=1, source_target_pairs={{0,1},{1,0},{2,3},{3,2},{4,5},{5,4},{6,7},{7,6},{8,9},{9,8},{10,11... | collective-permute-start | bytes 786440 | tf_op jit(solution)/shard_map/ppermute | solution.py:64
  20.6 5.6 %collective-permute-start.11 = (bf16[16,4096]{1,0:T(8,128)(2,1)S(1)}, bf16[16,4096]{1,0:T(8,128)(2,1)S(1)}, u32[]{:S(2)}, u32[]{:S(2)}) collective-permute-start(bf16[16,4096]{1,0:T(8,128)(2,1)S(1)} %broadcast_select_fusion), channel_id=1, source_target_pairs={{0,2},{1,3},{2,0},{3,1},{4,6},{5,7},{6,4},{7,5},{8,10},{9,11},{10,... | collective-permute-start | bytes 393224 | tf_op jit(solution)/shard_map/ppermute | solution.py:64
  23.1 1.6 %collective-permute-start.4 = (f32[3,64]{1,0:T(4,128)S(1)}, f32[3,64]{1,0:T(4,128)S(1)}, u32[]{:S(2)}, u32[]{:S(2)}) collective-permute-start(f32[3,64]{1,0:T(4,128)S(1)} %pad_maximum_fusion.1), channel_id=1, source_target_pairs={{0,1},{1,0},{2,3},{3,2},{4,5},{5,4},{6,7},{7,6},{8,9},{9,8},{10,11... | collective-permute-start | bytes 2312 | tf_op jit(solution)/shard_map/ppermute | solution.py:64
  24.0 20.8 %copy-start.2 = (f32[64,512]{1,0:T(8,128)S(1)}, f32[64,512]{1,0:T(8,128)}, u32[]{:S(2)}) copy-start(f32[64,512]{1,0:T(8,128)} %get-tuple-element.72) | copy-start | bytes 393220
  24.0 20.9 %copy-start.3 = (bf16[64,512]{1,0:T(8,128)(2,1)S(1)}, bf16[64,512]{1,0:T(8,128)(2,1)}, u32[]{:S(2)}) copy-start(bf16[64,512]{1,0:T(8,128)(2,1)} %get-tuple-element.73) | copy-start | bytes 196612
  24.1 2.2 %collective-permute-start.5 = (bf16[32,4096]{1,0:T(8,128)(2,1)S(1)}, bf16[32,4096]{1,0:T(8,128)(2,1)S(1)}, u32[]{:S(2)}, u32[]{:S(2)}) collective-permute-start(bf16[32,4096]{1,0:T(8,128)(2,1)S(1)} %select_convert_fusion), channel_id=1, source_target_pairs={{0,1},{1,0},{2,3},{3,2},{4,5},{5,4},{6,7},{7,6},{8,9},{9,8},{10,11... | collective-permute-start | bytes 786440 | tf_op jit(solution)/shard_map/ppermute | solution.py:64
  24.9 17.5 %collective-permute-start.18 = (bf16[32,4096]{1,0:T(8,128)(2,1)S(1)}, bf16[32,4096]{1,0:T(8,128)(2,1)S(1)}, u32[]{:S(2)}, u32[]{:S(2)}) collective-permute-start(bf16[32,4096]{1,0:T(8,128)(2,1)S(1)} %maximum_select_fusion.3), channel_id=1, source_target_pairs={{0,1},{1,0},{2,3},{3,2},{4,5},{5,4},{6,7},{7,6},{8,9},{9,8},{10,11... | collective-permute-start | bytes 786440 | tf_op jit(solution)/shard_map/ppermute | solution.py:64
  26.5 3.7 %collective-permute-start.6 = (f32[3,64]{1,0:T(4,128)S(1)}, f32[3,64]{1,0:T(4,128)S(1)}, u32[]{:S(2)}, u32[]{:S(2)}) collective-permute-start(f32[3,64]{1,0:T(4,128)S(1)} %pad_maximum_fusion.2), channel_id=1, source_target_pairs={{0,2},{1,3},{2,0},{3,1},{4,6},{5,7},{6,4},{7,5},{8,10},{9,11},{10,... | collective-permute-start | bytes 2312 | tf_op jit(solution)/shard_map/ppermute | solution.py:64
  27.6 5.5 %collective-permute-start.7 = (bf16[16,4096]{1,0:T(8,128)(2,1)S(1)}, bf16[16,4096]{1,0:T(8,128)(2,1)S(1)}, u32[]{:S(2)}, u32[]{:S(2)}) collective-permute-start(bf16[16,4096]{1,0:T(8,128)(2,1)S(1)} %select_convert_fusion.1), channel_id=1, source_target_pairs={{0,2},{1,3},{2,0},{3,1},{4,6},{5,7},{6,4},{7,5},{8,10},{9,11},{10,... | collective-permute-start | bytes 393224 | tf_op jit(solution)/shard_map/ppermute | solution.py:64
  33.3 3.7 %collective-permute-start.8 = (f32[3,64]{1,0:T(4,128)S(1)}, f32[3,64]{1,0:T(4,128)S(1)}, u32[]{:S(2)}, u32[]{:S(2)}) collective-permute-start(f32[3,64]{1,0:T(4,128)S(1)} %pad_maximum_fusion.3), channel_id=1, source_target_pairs={{0,4},{1,5},{2,6},{3,7},{4,0},{5,1},{6,2},{7,3},{8,12},{9,13},{10,... | collective-permute-start | bytes 2312 | tf_op jit(solution)/shard_map/ppermute | solution.py:64
  34.8 4.3 %collective-permute-start.12 = (bf16[8,4096]{1,0:T(8,128)(2,1)S(1)}, bf16[8,4096]{1,0:T(8,128)(2,1)S(1)}, u32[]{:S(2)}, u32[]{:S(2)}) collective-permute-start(bf16[8,4096]{1,0:T(8,128)(2,1)S(1)} %broadcast_select_fusion.1), channel_id=1, source_target_pairs={{0,4},{1,5},{2,6},{3,7},{4,0},{5,1},{6,2},{7,3},{8,12},{9,13},{10,... | collective-permute-start | bytes 196616 | tf_op jit(solution)/shard_map/ppermute | solution.py:64
  35.4 4.4 %collective-permute-start.9 = (bf16[8,4096]{1,0:T(8,128)(2,1)S(1)}, bf16[8,4096]{1,0:T(8,128)(2,1)S(1)}, u32[]{:S(2)}, u32[]{:S(2)}) collective-permute-start(bf16[8,4096]{1,0:T(8,128)(2,1)S(1)} %select_convert_fusion.3), channel_id=1, source_target_pairs={{0,4},{1,5},{2,6},{3,7},{4,0},{5,1},{6,2},{7,3},{8,12},{9,13},{10,... | collective-permute-start | bytes 196616 | tf_op jit(solution)/shard_map/ppermute | solution.py:64
  40.0 4.6 %collective-permute-start.13 = (f32[3,64]{1,0:T(4,128)S(1)}, f32[3,64]{1,0:T(4,128)S(1)}, u32[]{:S(2)}, u32[]{:S(2)}) collective-permute-start(f32[3,64]{1,0:T(4,128)S(1)} %pad_maximum_fusion.4), channel_id=1, source_target_pairs={{0,8},{1,9},{2,10},{3,11},{4,12},{5,13},{6,14},{7,15},{8,0},{9,1},... | collective-permute-start | bytes 2312 | tf_op jit(solution)/shard_map/ppermute | solution.py:64
  42.5 5.7 %copy-start.6 = (f32[64]{0:T(128)S(1)}, f32[64]{0:T(128)}, u32[]{:S(2)}) copy-start(f32[64]{0:T(128)} %param.15) | copy-start | bytes 772
  42.5 5.9 %collective-permute-start.14 = (bf16[8,4096]{1,0:T(8,128)(2,1)S(1)}, bf16[8,4096]{1,0:T(8,128)(2,1)S(1)}, u32[]{:S(2)}, u32[]{:S(2)}) collective-permute-start(bf16[8,4096]{1,0:T(8,128)(2,1)S(1)} %pad_maximum_fusion), channel_id=1, source_target_pairs={{0,8},{1,9},{2,10},{3,11},{4,12},{5,13},{6,14},{7,15},{8,0},{9,1},... | collective-permute-start | bytes 196616 | tf_op jit(solution)/shard_map/ppermute | solution.py:64

commit v4 on v3

--- a/solution.py
+++ b/solution.py
@@ -51,6 +51,20 @@
     weight_o[...] = jnp.broadcast_to(column(weight), weight_o.shape)
     upper = (rank & 1) == 1
     pick_o[...] = jnp.where(upper, jnp.concatenate([pick[half:], pick[:half]], 0), pick).astype(bf16)
+
+
+def table_grad(tiles, dl, took, hid, inp, out, held, sem):
+    lhs = jnp.concatenate([dl[...], took[...]], 0).T
+    step = out.shape[1] // tiles
+    leaving = []
+    for i in range(tiles):
+        at = pl.ds(i * step, step)
+        rhs = jnp.concatenate([hid[:, at], inp[:, at]], 0)
+        held[:, at] = jnp.dot(lhs, rhs, preferred_element_type=f32).astype(bf16)
+        leaving.append(pltpu.make_async_copy(held.at[:, at], out.at[:, at], sem.at[i]))
+        leaving[-1].start()
+    for copy in leaving:
+        copy.wait()
 
 
 def per_device(n, hidden, embedding, d_input, input_ids, language, allowed, target, token_weight):
@@ -120,8 +134,8 @@
     rows = rows[:half] + swap(rows[half:], 1)
     rows_keep, rows_send = halves(rows, 2)
     rows_got = swap(rows_send, 2)
+    all_hidden = join(all_hidden, got, 2)
     input_got = swap(after(all_input, all_hidden), 2)
-    all_hidden = join(all_hidden, got, 2)
     all_hidden = join(all_hidden, swap(all_hidden, 1), 1)
 
     logits = lax.dot_general(all_hidden, embedding, (((1,), (1,)), ((), ())), preferred_element_type=f32)
@@ -156,7 +170,6 @@
         lt = jnp.maximum(lt, got[2])
         m, s, lt, a, b = lax.optimization_barrier((m_new, s, lt, a, b))
         if k == 1:
-            rows = rows_keep + after(rows_got, m)
             all_input = join(all_input, after(input_got, m), 2)
             all_input = join(all_input, swap(all_input, 1), 1)
         elif 2 < k < n // 2:
@@ -166,6 +179,8 @@
             rows_got = swap(rows_send, 2 * k)
         lo = lo + jnp.where(bit(k), size, 0)
         part = keep * lax.dynamic_slice_in_dim(a, lo, size)[:, None] + recv[:size].astype(f32) * lax.dynamic_slice_in_dim(b, lo, size)[:, None]
+        if k == 1:
+            rows = rows_keep + after(rows_got, part)
         k *= 2
 
     hot = is_target.astype(f32)
@@ -176,12 +191,18 @@
     m_own, s_own, lt_own = (lax.dynamic_slice_in_dim(x, lo, mine) for x in (m, s, lt))
     coef = (w * (jnp.exp(lt_own - m_own) / s_own - 1.0)).astype(bf16).astype(f32)
     d_hidden = (part * (w / s_own)[:, None] + rows.astype(f32) * coef[:, None]).astype(bf16)
-    d_embed = lax.dot_general(
-        jnp.concatenate([d_logits, took], 0),
-        jnp.concatenate([all_hidden, all_input], 0),
-        (((0,), (0,)), ((), ())),
-        preferred_element_type=f32,
-    ).astype(bf16)
+    tiles = 8
+    d_embed = pl.pallas_call(
+        functools.partial(table_grad, tiles),
+        out_shape=jax.ShapeDtypeStruct((cols, width), bf16),
+        in_specs=[vmem] * 4,
+        out_specs=hbm,
+        scratch_shapes=[pltpu.VMEM((cols, width), bf16), pltpu.SemaphoreType.DMA((tiles,))],
+        compiler_params=pltpu.CompilerParams(vmem_limit_bytes=24 * 1024 * 1024),
+        cost_estimate=pl.CostEstimate(
+            flops=4 * tokens * cols * width, bytes_accessed=2 * cols * width, transcendentals=0),
+        name="table_grad",
+    )(d_logits, took, all_hidden, all_input)
     return d_hidden, d_embed
 
 

time: 49.4 us -> 48.9 us (0.990)
  matrix products: 8.69 us -> 5.43 us
  Pallas kernels: 1.79 us -> 4.19 us
  waiting for transfers between devices: 13.1 us -> 13.6 us
    dot_general x1 -> x0, matrix products: 3.29 us -> none  [per_device(): lax.dot_general(jnp.concatenate([d_logits, took], 0), jnp.concatenate([al...]
    pallas_call x0 -> x1, Pallas kernels: none -> 2.4 us  [per_device(): pl.pallas_call(functools.partial(table_grad, tiles), out_shape=jax.ShapeD...]
    ppermute x19, waiting for transfers between devices: 13.1 us -> 13.6 us  [swap(): return lax.ppermute(x, 'vocab', [(i, i ^ k) for i in range(n)])]
  transfers between devices with their start and end apart: 19 -> 19, of which waited for: 12 -> 13; matrix products, arithmetic and copies ran while one was open for 22% -> 16% of each run, Pallas kernels for 4% -> 9%
where the time goes in v4:
time: 48.9 us; the launch traced here: 48.6 us
  starting transfers between devices  21.5 us (44%)
  waiting for transfers between devices  13.6 us (28%)
  matrix products  5.43 us (11%)
  Pallas kernels  4.19 us (9%)
  other arithmetic  2.3 us (5%)
  between operations  0.95 us (2%)
  local copies, waits for them, and re-layouts  0.66 us (1%)
    ppermute x19, starting transfers between devices, swap(): return lax.ppermute(x, 'vocab', [(i, i ^ k) for i in range(n)])  21.5 us
    ppermute x19, waiting for transfers between devices, swap(): return lax.ppermute(x, 'vocab', [(i, i ^ k) for i in range(n)])  13.6 us
    dot_general x1, matrix products, per_device(): jnp.dot(after(pick, all_hidden), embedding, preferred_element_type=f32)  3.07 us
    pallas_call x1, Pallas kernels, per_device(): pl.pallas_call(functools.partial(table_grad, tiles), out_shape=jax.ShapeD...  2.4 us
    pallas_call x1, Pallas kernels, per_device(): pl.pallas_call(functools.partial(prepare, mine, steps), out_shape=(jax.Sh...  1.79 us
    dot_general x1, matrix products, per_device(): lax.dot_general(all_hidden, embedding, (((1,), (1,)), ((), ())), preferre...  1.49 us
  transfers between devices with their start and end apart: 19, of which 13 were waited for; matrix products, arithmetic and copies ran while one was open for 16% of the time, Pallas kernels for 9%

profile of v4, /device:TPU:0, one launch (start us, length us, event | category | flops | bytes accessed | tf_op | source)
XLA Modules:
  0.0 48.6 jit_solution(10746912791865831152)
XLA Ops:
  0.7 4.1 %collective-permute-start = (bf16[4,4096]{1,0:T(4,128)(2,1)}, bf16[4,4096]{1,0:T(4,128)(2,1)S(1)}, u32[]{:S(2)}, u32[]{:S(2)}) collective-permute-start(bf16[4,4096]{1,0:T(4,128)(2,1)} %param.8), channel_id=1, source_target_pairs={{0,8},{1,9},{2,10},{3,11},{4,12},{5,13},{6,14},{7,15},{8,0},{9,1},... | collective-permute-start | bytes 98312 | tf_op jit(solution)/shard_map/ppermute | solution.py:78
  4.8 0.1 collective-permute-start.15
  4.8 1.8 %prepare.1 = (bf16[64,512]{1,0:T(8,128)(2,1)}, bf16[64,512]{1,0:T(8,128)(2,1)}, f32[64,512]{1,0:T(8,128)}, bf16[64,512]{1,0:T(8,128)(2,1)}) custom-call(s32[1,1]{1,0:T(1,128)} %bitcast.me, bf16[512,4096]{1,0:T(8,128)(2,1)} %table_h.1, s32[1,64]{1,0:T(1,128)} %bitcast.88, s32[1,64]{1,0:T(1,128)} %bitcast.89, s32[16,16]{1,0:T(8,128)} %allowed_h.1, ...), custom_call_target="tpu_custom_call" | custom-call | tf_op jit(solution)/shard_map/prepare/pallas_call | solution.py:97
  6.6 0.6 %collective-permute-done = bf16[4,4096]{1,0:T(4,128)(2,1)S(1)} collective-permute-done((bf16[4,4096]{1,0:T(4,128)(2,1)}, bf16[4,4096]{1,0:T(4,128)(2,1)S(1)}, u32[]{:S(2)}, u32[]{:S(2)}) %collective-permute-start) | collective-permute-done | bytes 32800 | tf_op jit(solution)/shard_map/ppermute | solution.py:78
  7.3 1.8 %collective-permute-start.1 = (bf16[8,4096]{1,0:T(8,128)(2,1)S(1)}, bf16[8,4096]{1,0:T(8,128)(2,1)S(1)}, u32[]{:S(2)}, u32[]{:S(2)}) collective-permute-start(bf16[8,4096]{1,0:T(8,128)(2,1)S(1)} %maximum_select_fusion.6), channel_id=1, source_target_pairs={{0,4},{1,5},{2,6},{3,7},{4,0},{5,1},{6,2},{7,3},{8,12},{9,13},{10,... | collective-permute-start | bytes 196616 | tf_op jit(solution)/shard_map/ppermute | solution.py:78
  9.1 0.8 %collective-permute-done.15 = bf16[4,4096]{1,0:T(4,128)(2,1)S(1)} collective-permute-done((bf16[4,4096]{1,0:T(4,128)(2,1)}, bf16[4,4096]{1,0:T(4,128)(2,1)S(1)}, u32[]{:S(2)}, u32[]{:S(2)}) %collective-permute-start.15) | collective-permute-done | bytes 32800 | tf_op jit(solution)/shard_map/ppermute | solution.py:78
  10.0 1.5 %collective-permute-start.16 = (bf16[8,4096]{1,0:T(8,128)(2,1)S(1)}, bf16[8,4096]{1,0:T(8,128)(2,1)S(1)}, u32[]{:S(2)}, u32[]{:S(2)}) collective-permute-start(bf16[8,4096]{1,0:T(8,128)(2,1)S(1)} %maximum_select_fusion.7), channel_id=1, source_target_pairs={{0,4},{1,5},{2,6},{3,7},{4,0},{5,1},{6,2},{7,3},{8,12},{9,13},{10,... | collective-permute-start | bytes 196616 | tf_op jit(solution)/shard_map/ppermute | solution.py:78
  11.5 0.6 %collective-permute-done.1 = bf16[8,4096]{1,0:T(8,128)(2,1)S(1)} collective-permute-done((bf16[8,4096]{1,0:T(8,128)(2,1)S(1)}, bf16[8,4096]{1,0:T(8,128)(2,1)S(1)}, u32[]{:S(2)}, u32[]{:S(2)}) %collective-permute-start.1) | collective-permute-done | bytes 65568 | tf_op jit(solution)/shard_map/ppermute | solution.py:78
  12.2 1.9 %collective-permute-start.2 = (bf16[16,4096]{1,0:T(8,128)(2,1)S(1)}, bf16[16,4096]{1,0:T(8,128)(2,1)S(1)}, u32[]{:S(2)}, u32[]{:S(2)}) collective-permute-start(bf16[16,4096]{1,0:T(8,128)(2,1)S(1)} %maximum_select_fusion.4), channel_id=1, source_target_pairs={{0,2},{1,3},{2,0},{3,1},{4,6},{5,7},{6,4},{7,5},{8,10},{9,11},{10,... | collective-permute-start | bytes 393224 | tf_op jit(solution)/shard_map/ppermute | solution.py:78
  14.1 3.1 %convolution_convert_fusion = bf16[64,4096]{1,0:T(8,128)(2,1)S(1)} fusion(bf16[64,512]{1,0:T(8,128)(2,1)} %get-tuple-element.61, bf16[512,4096]{1,0:T(8,128)(2,1)} %table_h.1), kind=kOutput, calls=%fused_computation | convolution fusion | flops 268697600 | bytes 4784128 | tf_op jit(solution)/shard_map/dot_general | solution.py:133
  17.4 0.5 %collective-permute-start.3 = (bf16[32,4096]{1,0:T(8,128)(2,1)S(1)}, bf16[32,4096]{1,0:T(8,128)(2,1)S(1)}, u32[]{:S(2)}, u32[]{:S(2)}) collective-permute-start(bf16[32,4096]{1,0:T(8,128)(2,1)S(1)} %maximum_select_fusion.2), channel_id=1, source_target_pairs={{0,1},{1,0},{2,3},{3,2},{4,5},{5,4},{6,7},{7,6},{8,9},{9,8},{10,11... | collective-permute-start | bytes 786440 | tf_op jit(solution)/shard_map/ppermute | solution.py:78
  18.0 1.3 %collective-permute-start.17 = (bf16[16,4096]{1,0:T(8,128)(2,1)S(1)}, bf16[16,4096]{1,0:T(8,128)(2,1)S(1)}, u32[]{:S(2)}, u32[]{:S(2)}) collective-permute-start(bf16[16,4096]{1,0:T(8,128)(2,1)S(1)} %maximum_select_fusion.5), channel_id=1, source_target_pairs={{0,2},{1,3},{2,0},{3,1},{4,6},{5,7},{6,4},{7,5},{8,10},{9,11},{10,... | collective-permute-start | bytes 393224 | tf_op jit(solution)/shard_map/ppermute | solution.py:78
  19.3 0.8 %collective-permute-start.11 = (bf16[16,4096]{1,0:T(8,128)(2,1)S(1)}, bf16[16,4096]{1,0:T(8,128)(2,1)S(1)}, u32[]{:S(2)}, u32[]{:S(2)}) collective-permute-start(bf16[16,4096]{1,0:T(8,128)(2,1)S(1)} %broadcast_select_fusion), channel_id=1, source_target_pairs={{0,2},{1,3},{2,0},{3,1},{4,6},{5,7},{6,4},{7,5},{8,10},{9,11},{10,... | collective-permute-start | bytes 393224 | tf_op jit(solution)/shard_map/ppermute | solution.py:78
  20.1 0.1 maximum_select_fusion.hid
  20.2 1.5 %fusion.13 = (f32[64]{0:T(128)S(1)}, f32[64,512]{1,0:T(8,128)S(1)}) fusion(bf16[64,4096]{1,0:T(8,128)(2,1)S(1)} %maximum_select_fusion.hid, bf16[512,4096]{1,0:T(8,128)(2,1)S(1)} %copy-done.1, bf16[64,512]{1,0:T(8,128)(2,1)S(1)} %copy-done.2), kind=kOutput, calls=%fused_computation.68 | convolution fusion | flops 268533696 | bytes 4915456 | tf_op jit(solution)/shard_map/dot_general | solution.py:141
  21.7 0.2 fusion
  22.0 0.9 %fusion.14 = f32[64,4096]{1,0:T(8,128)S(1)} fusion(bf16[64,512]{1,0:T(8,128)(2,1)S(1)} %get-tuple-element.40, bf16[512,4096]{1,0:T(8,128)(2,1)S(1)} %copy-done.1), kind=kOutput, calls=%fused_computation.69 | convolution fusion | flops 268435456 | bytes 5308416 | tf_op jit(solution)/shard_map/dot_general | solution.py:148
  23.0 0.6 %collective-permute-start.5 = (bf16[32,4096]{1,0:T(8,128)(2,1)S(1)}, bf16[32,4096]{1,0:T(8,128)(2,1)S(1)}, u32[]{:S(2)}, u32[]{:S(2)}) collective-permute-start(bf16[32,4096]{1,0:T(8,128)(2,1)S(1)} %select_convert_fusion), channel_id=1, source_target_pairs={{0,1},{1,0},{2,3},{3,2},{4,5},{5,4},{6,7},{7,6},{8,9},{9,8},{10,11... | collective-permute-start | bytes 786440 | tf_op jit(solution)/shard_map/ppermute | solution.py:78
  23.6 0.7 %collective-permute-done.17 = bf16[16,4096]{1,0:T(8,128)(2,1)S(1)} collective-permute-done((bf16[16,4096]{1,0:T(8,128)(2,1)S(1)}, bf16[16,4096]{1,0:T(8,128)(2,1)S(1)}, u32[]{:S(2)}, u32[]{:S(2)}) %collective-permute-start.17) | collective-permute-done | bytes 131104 | tf_op jit(solution)/shard_map/ppermute | solution.py:78
  24.4 0.1 dynamic_slice.36
  24.4 0.1 dynamic_slice.37
  24.5 0.2 collective-permute-done.5
  24.7 0.2 multiply_add_fusion
  24.9 1.3 %collective-permute-done.11 = bf16[16,4096]{1,0:T(8,128)(2,1)S(1)} collective-permute-done((bf16[16,4096]{1,0:T(8,128)(2,1)S(1)}, bf16[16,4096]{1,0:T(8,128)(2,1)S(1)}, u32[]{:S(2)}, u32[]{:S(2)}) %collective-permute-start.11) | collective-permute-done | bytes 131104 | tf_op jit(solution)/shard_map/ppermute | solution.py:78
  26.2 1.7 %collective-permute-start.6 = (f32[3,64]{1,0:T(4,128)S(1)}, f32[3,64]{1,0:T(4,128)S(1)}, u32[]{:S(2)}, u32[]{:S(2)}) collective-permute-start(f32[3,64]{1,0:T(4,128)S(1)} %pad_maximum_fusion.2), channel_id=1, source_target_pairs={{0,2},{1,3},{2,0},{3,1},{4,6},{5,7},{6,4},{7,5},{8,10},{9,11},{10,... | collective-permute-start | bytes 2312 | tf_op jit(solution)/shard_map/ppermute | solution.py:78
  28.0 0.4 collective-permute-start.7
  28.4 1.5 %collective-permute-done.6 = f32[3,64]{1,0:T(4,128)S(1)} collective-permute-done((f32[3,64]{1,0:T(4,128)S(1)}, f32[3,64]{1,0:T(4,128)S(1)}, u32[]{:S(2)}, u32[]{:S(2)}) %collective-permute-start.6) | collective-permute-done | bytes 800 | tf_op jit(solution)/shard_map/ppermute | solution.py:78
  29.8 0.1 dynamic_slice.38
  29.9 0.1 dynamic_slice.39
  30.0 3.0 %collective-permute-done.7 = bf16[16,4096]{1,0:T(8,128)(2,1)S(1)} collective-permute-done((bf16[16,4096]{1,0:T(8,128)(2,1)S(1)}, bf16[16,4096]{1,0:T(8,128)(2,1)S(1)}, u32[]{:S(2)}, u32[]{:S(2)}) %collective-permute-start.7) | collective-permute-done | bytes 131104 | tf_op jit(solution)/shard_map/ppermute | solution.py:78
  33.0 0.1 multiply_add_fusion.1
  33.1 1.5 %collective-permute-start.8 = (f32[3,64]{1,0:T(4,128)S(1)}, f32[3,64]{1,0:T(4,128)S(1)}, u32[]{:S(2)}, u32[]{:S(2)}) collective-permute-start(f32[3,64]{1,0:T(4,128)S(1)} %pad_maximum_fusion.3), channel_id=1, source_target_pairs={{0,4},{1,5},{2,6},{3,7},{4,0},{5,1},{6,2},{7,3},{8,12},{9,13},{10,... | collective-permute-start | bytes 2312 | tf_op jit(solution)/shard_map/ppermute | solution.py:78
  34.6 0.7 %collective-permute-start.12 = (bf16[8,4096]{1,0:T(8,128)(2,1)S(1)}, bf16[8,4096]{1,0:T(8,128)(2,1)S(1)}, u32[]{:S(2)}, u32[]{:S(2)}) collective-permute-start(bf16[8,4096]{1,0:T(8,128)(2,1)S(1)} %broadcast_select_fusion.1), channel_id=1, source_target_pairs={{0,4},{1,5},{2,6},{3,7},{4,0},{5,1},{6,2},{7,3},{8,12},{9,13},{10,... | collective-permute-start | bytes 196616 | tf_op jit(solution)/shard_map/ppermute | solution.py:78
  35.3 1.4 %collective-permute-start.9 = (bf16[8,4096]{1,0:T(8,128)(2,1)S(1)}, bf16[8,4096]{1,0:T(8,128)(2,1)S(1)}, u32[]{:S(2)}, u32[]{:S(2)}) collective-permute-start(bf16[8,4096]{1,0:T(8,128)(2,1)S(1)} %select_convert_fusion.3), channel_id=1, source_target_pairs={{0,4},{1,5},{2,6},{3,7},{4,0},{5,1},{6,2},{7,3},{8,12},{9,13},{10,... | collective-permute-start | bytes 196616 | tf_op jit(solution)/shard_map/ppermute | solution.py:78
  36.7 0.1 collective-permute-done.8
  36.8 0.1 dynamic_slice.40
  36.9 2.0 %collective-permute-done.12 = bf16[8,4096]{1,0:T(8,128)(2,1)S(1)} collective-permute-done((bf16[8,4096]{1,0:T(8,128)(2,1)S(1)}, bf16[8,4096]{1,0:T(8,128)(2,1)S(1)}, u32[]{:S(2)}, u32[]{:S(2)}) %collective-permute-start.12) | collective-permute-done | bytes 65568 | tf_op jit(solution)/shard_map/ppermute | solution.py:78
  39.0 0.6 %collective-permute-done.9 = bf16[8,4096]{1,0:T(8,128)(2,1)S(1)} collective-permute-done((bf16[8,4096]{1,0:T(8,128)(2,1)S(1)}, bf16[8,4096]{1,0:T(8,128)(2,1)S(1)}, u32[]{:S(2)}, u32[]{:S(2)}) %collective-permute-start.9) | collective-permute-done | bytes 65568 | tf_op jit(solution)/shard_map/ppermute | solution.py:78
  39.6 0.1 multiply_add_fusion.2
  39.8 2.8 %collective-permute-start.13 = (f32[3,64]{1,0:T(4,128)S(1)}, f32[3,64]{1,0:T(4,128)S(1)}, u32[]{:S(2)}, u32[]{:S(2)}) collective-permute-start(f32[3,64]{1,0:T(4,128)S(1)} %pad_maximum_fusion.4), channel_id=1, source_target_pairs={{0,8},{1,9},{2,10},{3,11},{4,12},{5,13},{6,14},{7,15},{8,0},{9,1},... | collective-permute-start | bytes 2312 | tf_op jit(solution)/shard_map/ppermute | solution.py:78
  42.6 0.1 maximum_select_fusion.1.inp
  42.7 0.2 collective-permute-start.14
  42.9 1.4 %collective-permute-done.13 = f32[3,64]{1,0:T(4,128)S(1)} collective-permute-done((f32[3,64]{1,0:T(4,128)S(1)}, f32[3,64]{1,0:T(4,128)S(1)}, u32[]{:S(2)}, u32[]{:S(2)}) %collective-permute-start.13) | collective-permute-done | bytes 800 | tf_op jit(solution)/shard_map/ppermute | solution.py:78
  44.4 0.1 select_convert_fusion.2.dl
  44.5 0.1 dynamic-slice_divide_fusion
  44.7 2.4 %table_grad.1 = bf16[512,4096]{1,0:T(8,128)(2,1)} custom-call(bf16[64,512]{1,0:T(8,128)(2,1)S(1)} %select_convert_fusion.2.dl, bf16[64,512]{1,0:T(8,128)(2,1)S(1)} %copy-done, bf16[64,4096]{1,0:T(8,128)(2,1)S(1)} %maximum_select_fusion.hid, bf16[64,4096]{1,0:T(8,128)(2,1)S(1)} %maximum_select_fusion.1.inp), custom_call_target="tpu_custom_call" | custom-call | flops 536870912 | bytes 4194304 | tf_op jit(solution)/shard_map/table_grad/pallas_call | solution.py:195
  47.1 0.8 %collective-permute-done.14 = bf16[8,4096]{1,0:T(8,128)(2,1)S(1)} collective-permute-done((bf16[8,4096]{1,0:T(8,128)(2,1)S(1)}, bf16[8,4096]{1,0:T(8,128)(2,1)S(1)}, u32[]{:S(2)}, u32[]{:S(2)}) %collective-permute-start.14) | collective-permute-done | bytes 65568 | tf_op jit(solution)/shard_map/ppermute | solution.py:78
  47.9 0.7 %add_convert_fusion = bf16[4,4096]{1,0:T(4,128)(2,1)} fusion(f32[8,4096]{1,0:T(8,128)S(1)} %multiply_add_fusion.2, bf16[8,4096]{1,0:T(8,128)(2,1)S(1)} %collective-permute-done.14, f32[4]{0:T(128)S(1)} %get-tuple-element.100, f32[4]{0:T(128)S(1)} %get-tuple-element.99, f32[4]{0:T(128)S(1)} %dynamic_slice.43, f32[4]{0:T(128)S(1)} %dynamic_slice.42, ...), kind=kLoop, calls=%fused_computation.25 | loop fusion | flops 196608 | bytes 294977 | tf_op jit(solution)/shard_map/convert_element_type | solution.py:193
  (52 shorter events, 1.1 us)
Async XLA Ops:
  0.6 6.6 %copy-start.4 = (bf16[4,4096]{1,0:T(4,128)(2,1)S(1)}, bf16[4,4096]{1,0:T(4,128)(2,1)}, u32[]{:S(2)}) copy-start(bf16[4,4096]{1,0:T(4,128)(2,1)} %param.8) | copy-start | bytes 98308
  0.6 9.2 %copy-start.5 = (bf16[4,4096]{1,0:T(4,128)(2,1)S(1)}, bf16[4,4096]{1,0:T(4,128)(2,1)}, u32[]{:S(2)}) copy-start(bf16[4,4096]{1,0:T(4,128)(2,1)} %param.10) | copy-start | bytes 98308
  0.7 6.6 %collective-permute-start = (bf16[4,4096]{1,0:T(4,128)(2,1)}, bf16[4,4096]{1,0:T(4,128)(2,1)S(1)}, u32[]{:S(2)}, u32[]{:S(2)}) collective-permute-start(bf16[4,4096]{1,0:T(4,128)(2,1)} %param.8), channel_id=1, source_target_pairs={{0,8},{1,9},{2,10},{3,11},{4,12},{5,13},{6,14},{7,15},{8,0},{9,1},... | collective-permute-start | bytes 98312 | tf_op jit(solution)/shard_map/ppermute | solution.py:78
  4.8 5.1 %collective-permute-start.15 = (bf16[4,4096]{1,0:T(4,128)(2,1)}, bf16[4,4096]{1,0:T(4,128)(2,1)S(1)}, u32[]{:S(2)}, u32[]{:S(2)}) collective-permute-start(bf16[4,4096]{1,0:T(4,128)(2,1)} %param.10), channel_id=1, source_target_pairs={{0,8},{1,9},{2,10},{3,11},{4,12},{5,13},{6,14},{7,15},{8,0},{9,1},... | collective-permute-start | bytes 98312 | tf_op jit(solution)/shard_map/ppermute | solution.py:78
  7.3 4.8 %collective-permute-start.1 = (bf16[8,4096]{1,0:T(8,128)(2,1)S(1)}, bf16[8,4096]{1,0:T(8,128)(2,1)S(1)}, u32[]{:S(2)}, u32[]{:S(2)}) collective-permute-start(bf16[8,4096]{1,0:T(8,128)(2,1)S(1)} %maximum_select_fusion.6), channel_id=1, source_target_pairs={{0,4},{1,5},{2,6},{3,7},{4,0},{5,1},{6,2},{7,3},{8,12},{9,13},{10,... | collective-permute-start | bytes 196616 | tf_op jit(solution)/shard_map/ppermute | solution.py:78
  10.0 7.3 %collective-permute-start.16 = (bf16[8,4096]{1,0:T(8,128)(2,1)S(1)}, bf16[8,4096]{1,0:T(8,128)(2,1)S(1)}, u32[]{:S(2)}, u32[]{:S(2)}) collective-permute-start(bf16[8,4096]{1,0:T(8,128)(2,1)S(1)} %maximum_select_fusion.7), channel_id=1, source_target_pairs={{0,4},{1,5},{2,6},{3,7},{4,0},{5,1},{6,2},{7,3},{8,12},{9,13},{10,... | collective-permute-start | bytes 196616 | tf_op jit(solution)/shard_map/ppermute | solution.py:78
  12.1 8.1 %copy-start.1 = (bf16[512,4096]{1,0:T(8,128)(2,1)S(1)}, bf16[512,4096]{1,0:T(8,128)(2,1)}, u32[]{:S(2)}) copy-start(bf16[512,4096]{1,0:T(8,128)(2,1)} %table_h.1) | copy-start | bytes 12582916
  12.2 8.1 %copy-start.2 = (bf16[64,512]{1,0:T(8,128)(2,1)S(1)}, bf16[64,512]{1,0:T(8,128)(2,1)}, u32[]{:S(2)}) copy-start(bf16[64,512]{1,0:T(8,128)(2,1)} %get-tuple-element.39) | copy-start | bytes 196612
  12.2 5.2 %collective-permute-start.2 = (bf16[16,4096]{1,0:T(8,128)(2,1)S(1)}, bf16[16,4096]{1,0:T(8,128)(2,1)S(1)}, u32[]{:S(2)}, u32[]{:S(2)}) collective-permute-start(bf16[16,4096]{1,0:T(8,128)(2,1)S(1)} %maximum_select_fusion.4), channel_id=1, source_target_pairs={{0,2},{1,3},{2,0},{3,1},{4,6},{5,7},{6,4},{7,5},{8,10},{9,11},{10,... | collective-permute-start | bytes 393224 | tf_op jit(solution)/shard_map/ppermute | solution.py:78
  17.2 2.1 %collective-permute-start.10 = (bf16[32,4096]{1,0:T(8,128)(2,1)S(1)}, bf16[32,4096]{1,0:T(8,128)(2,1)S(1)}, u32[]{:S(2)}, u32[]{:S(2)}) collective-permute-start(bf16[32,4096]{1,0:T(8,128)(2,1)S(1)} %slice.133), channel_id=1, source_target_pairs={{0,1},{1,0},{2,3},{3,2},{4,5},{5,4},{6,7},{7,6},{8,9},{9,8},{10,11... | collective-permute-start | bytes 786440 | tf_op jit(solution)/shard_map/ppermute | solution.py:78
  17.4 2.7 %collective-permute-start.3 = (bf16[32,4096]{1,0:T(8,128)(2,1)S(1)}, bf16[32,4096]{1,0:T(8,128)(2,1)S(1)}, u32[]{:S(2)}, u32[]{:S(2)}) collective-permute-start(bf16[32,4096]{1,0:T(8,128)(2,1)S(1)} %maximum_select_fusion.2), channel_id=1, source_target_pairs={{0,1},{1,0},{2,3},{3,2},{4,5},{5,4},{6,7},{7,6},{8,9},{9,8},{10,11... | collective-permute-start | bytes 786440 | tf_op jit(solution)/shard_map/ppermute | solution.py:78
  18.0 6.4 %collective-permute-start.17 = (bf16[16,4096]{1,0:T(8,128)(2,1)S(1)}, bf16[16,4096]{1,0:T(8,128)(2,1)S(1)}, u32[]{:S(2)}, u32[]{:S(2)}) collective-permute-start(bf16[16,4096]{1,0:T(8,128)(2,1)S(1)} %maximum_select_fusion.5), channel_id=1, source_target_pairs={{0,2},{1,3},{2,0},{3,1},{4,6},{5,7},{6,4},{7,5},{8,10},{9,11},{10,... | collective-permute-start | bytes 393224 | tf_op jit(solution)/shard_map/ppermute | solution.py:78
  19.3 6.9 %collective-permute-start.11 = (bf16[16,4096]{1,0:T(8,128)(2,1)S(1)}, bf16[16,4096]{1,0:T(8,128)(2,1)S(1)}, u32[]{:S(2)}, u32[]{:S(2)}) collective-permute-start(bf16[16,4096]{1,0:T(8,128)(2,1)S(1)} %broadcast_select_fusion), channel_id=1, source_target_pairs={{0,2},{1,3},{2,0},{3,1},{4,6},{5,7},{6,4},{7,5},{8,10},{9,11},{10,... | collective-permute-start | bytes 393224 | tf_op jit(solution)/shard_map/ppermute | solution.py:78
  21.9 1.6 %collective-permute-start.4 = (f32[3,64]{1,0:T(4,128)S(1)}, f32[3,64]{1,0:T(4,128)S(1)}, u32[]{:S(2)}, u32[]{:S(2)}) collective-permute-start(f32[3,64]{1,0:T(4,128)S(1)} %pad_maximum_fusion.1), channel_id=1, source_target_pairs={{0,1},{1,0},{2,3},{3,2},{4,5},{5,4},{6,7},{7,6},{8,9},{9,8},{10,11... | collective-permute-start | bytes 2312 | tf_op jit(solution)/shard_map/ppermute | solution.py:78
  22.9 21.5 %copy-start.3 = (f32[64,512]{1,0:T(8,128)S(1)}, f32[64,512]{1,0:T(8,128)}, u32[]{:S(2)}) copy-start(f32[64,512]{1,0:T(8,128)} %get-tuple-element.72) | copy-start | bytes 393220
  22.9 21.6 %copy-start.6 = (f32[64]{0:T(128)S(1)}, f32[64]{0:T(128)}, u32[]{:S(2)}) copy-start(f32[64]{0:T(128)} %param.15) | copy-start | bytes 772
  22.9 21.8 %copy-start = (bf16[64,512]{1,0:T(8,128)(2,1)S(1)}, bf16[64,512]{1,0:T(8,128)(2,1)}, u32[]{:S(2)}) copy-start(bf16[64,512]{1,0:T(8,128)(2,1)} %get-tuple-element.73.took) | copy-start | bytes 196612
  23.0 1.7 %collective-permute-start.5 = (bf16[32,4096]{1,0:T(8,128)(2,1)S(1)}, bf16[32,4096]{1,0:T(8,128)(2,1)S(1)}, u32[]{:S(2)}, u32[]{:S(2)}) collective-permute-start(bf16[32,4096]{1,0:T(8,128)(2,1)S(1)} %select_convert_fusion), channel_id=1, source_target_pairs={{0,1},{1,0},{2,3},{3,2},{4,5},{5,4},{6,7},{7,6},{8,9},{9,8},{10,11... | collective-permute-start | bytes 786440 | tf_op jit(solution)/shard_map/ppermute | solution.py:78
  24.5 18.1 %collective-permute-start.18 = (bf16[32,4096]{1,0:T(8,128)(2,1)S(1)}, bf16[32,4096]{1,0:T(8,128)(2,1)S(1)}, u32[]{:S(2)}, u32[]{:S(2)}) collective-permute-start(bf16[32,4096]{1,0:T(8,128)(2,1)S(1)} %maximum_select_fusion.3), channel_id=1, source_target_pairs={{0,1},{1,0},{2,3},{3,2},{4,5},{5,4},{6,7},{7,6},{8,9},{9,8},{10,11... | collective-permute-start | bytes 786440 | tf_op jit(solution)/shard_map/ppermute | solution.py:78
  26.2 3.6 %collective-permute-start.6 = (f32[3,64]{1,0:T(4,128)S(1)}, f32[3,64]{1,0:T(4,128)S(1)}, u32[]{:S(2)}, u32[]{:S(2)}) collective-permute-start(f32[3,64]{1,0:T(4,128)S(1)} %pad_maximum_fusion.2), channel_id=1, source_target_pairs={{0,2},{1,3},{2,0},{3,1},{4,6},{5,7},{6,4},{7,5},{8,10},{9,11},{10,... | collective-permute-start | bytes 2312 | tf_op jit(solution)/shard_map/ppermute | solution.py:78
  28.0 5.0 %collective-permute-start.7 = (bf16[16,4096]{1,0:T(8,128)(2,1)S(1)}, bf16[16,4096]{1,0:T(8,128)(2,1)S(1)}, u32[]{:S(2)}, u32[]{:S(2)}) collective-permute-start(bf16[16,4096]{1,0:T(8,128)(2,1)S(1)} %select_convert_fusion.1), channel_id=1, source_target_pairs={{0,2},{1,3},{2,0},{3,1},{4,6},{5,7},{6,4},{7,5},{8,10},{9,11},{10,... | collective-permute-start | bytes 393224 | tf_op jit(solution)/shard_map/ppermute | solution.py:78
  33.1 3.7 %collective-permute-start.8 = (f32[3,64]{1,0:T(4,128)S(1)}, f32[3,64]{1,0:T(4,128)S(1)}, u32[]{:S(2)}, u32[]{:S(2)}) collective-permute-start(f32[3,64]{1,0:T(4,128)S(1)} %pad_maximum_fusion.3), channel_id=1, source_target_pairs={{0,4},{1,5},{2,6},{3,7},{4,0},{5,1},{6,2},{7,3},{8,12},{9,13},{10,... | collective-permute-start | bytes 2312 | tf_op jit(solution)/shard_map/ppermute | solution.py:78
  34.6 4.3 %collective-permute-start.12 = (bf16[8,4096]{1,0:T(8,128)(2,1)S(1)}, bf16[8,4096]{1,0:T(8,128)(2,1)S(1)}, u32[]{:S(2)}, u32[]{:S(2)}) collective-permute-start(bf16[8,4096]{1,0:T(8,128)(2,1)S(1)} %broadcast_select_fusion.1), channel_id=1, source_target_pairs={{0,4},{1,5},{2,6},{3,7},{4,0},{5,1},{6,2},{7,3},{8,12},{9,13},{10,... | collective-permute-start | bytes 196616 | tf_op jit(solution)/shard_map/ppermute | solution.py:78
  35.3 4.3 %collective-permute-start.9 = (bf16[8,4096]{1,0:T(8,128)(2,1)S(1)}, bf16[8,4096]{1,0:T(8,128)(2,1)S(1)}, u32[]{:S(2)}, u32[]{:S(2)}) collective-permute-start(bf16[8,4096]{1,0:T(8,128)(2,1)S(1)} %select_convert_fusion.3), channel_id=1, source_target_pairs={{0,4},{1,5},{2,6},{3,7},{4,0},{5,1},{6,2},{7,3},{8,12},{9,13},{10,... | collective-permute-start | bytes 196616 | tf_op jit(solution)/shard_map/ppermute | solution.py:78
  39.8 4.5 %collective-permute-start.13 = (f32[3,64]{1,0:T(4,128)S(1)}, f32[3,64]{1,0:T(4,128)S(1)}, u32[]{:S(2)}, u32[]{:S(2)}) collective-permute-start(f32[3,64]{1,0:T(4,128)S(1)} %pad_maximum_fusion.4), channel_id=1, source_target_pairs={{0,8},{1,9},{2,10},{3,11},{4,12},{5,13},{6,14},{7,15},{8,0},{9,1},... | collective-permute-start | bytes 2312 | tf_op jit(solution)/shard_map/ppermute | solution.py:78
  42.7 5.2 %collective-permute-start.14 = (bf16[8,4096]{1,0:T(8,128)(2,1)S(1)}, bf16[8,4096]{1,0:T(8,128)(2,1)S(1)}, u32[]{:S(2)}, u32[]{:S(2)}) collective-permute-start(bf16[8,4096]{1,0:T(8,128)(2,1)S(1)} %pad_maximum_fusion), channel_id=1, source_target_pairs={{0,8},{1,9},{2,10},{3,11},{4,12},{5,13},{6,14},{7,15},{8,0},{9,1},... | collective-permute-start | bytes 196616 | tf_op jit(solution)/shard_map/ppermute | solution.py:78

commit v5 on v4

--- a/solution.py
+++ b/solution.py
@@ -9,6 +9,10 @@
 
 NEG = -1e30
 f32, bf16, i32 = jnp.float32, jnp.bfloat16, jnp.int32
+
+
+def partners(n, k):
+    return {2: (2, 4), 4: (4, 8), 8: (8, 2)}.get(k, (k, k)) if n >= 16 else (k, k)
 
 
 def prepare(mine, steps, me, table_h, ids_h, language_h, allowed_h, target_h, weight_h,
@@ -32,8 +36,10 @@
     place = lax.broadcasted_iota(i32, (tokens, 1), 0)
     block = lax.div(place, mine)
     source = place - block * mine
+    odd = lax.shift_right_logical(block, steps - 1) & 1
     for i in range(steps):
-        source = source + mine * (n >> (i + 1)) * (lax.shift_right_logical(block, i) & 1)
+        even_k, odd_k = partners(n, n >> (i + 1))
+        source = source + mine * jnp.where(odd == 1, odd_k, even_k) * (lax.shift_right_logical(block, i) & 1)
     here = source == lax.broadcasted_iota(i32, (tokens, tokens), 1)
 
     def column(ref):
@@ -75,10 +81,12 @@
     me = lax.axis_index("vocab")
 
     def swap(x, k):
-        return lax.ppermute(x, "vocab", [(i, i ^ k) for i in range(n)])
+        ks = partners(n, k)
+        return lax.ppermute(x, "vocab", [(i, i ^ ks[i & 1]) for i in range(n)])
 
     def bit(k):
-        return (me & k) != 0
+        even_k, odd_k = partners(n, k)
+        return (me & jnp.where((me & 1) == 1, odd_k, even_k)) != 0
 
     def after(x, *deps):
         return lax.optimization_barrier((x,) + deps)[0]

time: 48.9 us -> 47.1 us (0.963)
  waiting for transfers between devices: 13.6 us -> 11.7 us
    ppermute x19, waiting for transfers between devices: 13.6 us -> 11.7 us  [swap(): return lax.ppermute(x, 'vocab', [(i, i ^ ks[i & 1]) for i in range(n)])]
  transfers between devices with their start and end apart: 19 -> 19, of which waited for: 13 -> 10; matrix products, arithmetic and copies ran while one was open for 16% -> 16% of each run, Pallas kernels for 9% -> 9%
where the time goes in v5:
time: 47.1 us; the launch traced here: 46.9 us
  starting transfers between devices  21.6 us (46%)
  waiting for transfers between devices  11.7 us (25%)
  matrix products  5.44 us (12%)
  Pallas kernels  4.19 us (9%)
  other arithmetic  2.3 us (5%)
  between operations  0.97 us (2%)
  local copies, waits for them, and re-layouts  0.66 us (1%)
    ppermute x19, starting transfers between devices, swap(): return lax.ppermute(x, 'vocab', [(i, i ^ ks[i & 1]) for i in range(n)])  21.6 us
    ppermute x19, waiting for transfers between devices, swap(): return lax.ppermute(x, 'vocab', [(i, i ^ ks[i & 1]) for i in range(n)])  11.7 us
    dot_general x1, matrix products, per_device(): jnp.dot(after(pick, all_hidden), embedding, preferred_element_type=f32)  3.07 us
    pallas_call x1, Pallas kernels, per_device(): pl.pallas_call(functools.partial(table_grad, tiles), out_shape=jax.ShapeD...  2.39 us
    pallas_call x1, Pallas kernels, per_device(): pl.pallas_call(functools.partial(prepare, mine, steps), out_shape=(jax.Sh...  1.8 us
    dot_general x1, matrix products, per_device(): lax.dot_general(all_hidden, embedding, (((1,), (1,)), ((), ())), preferre...  1.49 us
  transfers between devices with their start and end apart: 19, of which 10 were waited for; matrix products, arithmetic and copies ran while one was open for 16% of the time, Pallas kernels for 9%

profile of v5, /device:TPU:0, one launch (start us, length us, event | category | flops | bytes accessed | tf_op | source)
XLA Modules:
  0.0 46.9 jit_solution(3637858962058411828)
XLA Ops:
  0.7 4.1 %collective-permute-start = (bf16[4,4096]{1,0:T(4,128)(2,1)}, bf16[4,4096]{1,0:T(4,128)(2,1)S(1)}, u32[]{:S(2)}, u32[]{:S(2)}) collective-permute-start(bf16[4,4096]{1,0:T(4,128)(2,1)} %param.8), channel_id=1, source_target_pairs={{0,8},{1,3},{2,10},{3,1},{4,12},{5,7},{6,14},{7,5},{8,0},{9,11},{1... | collective-permute-start | bytes 98312 | tf_op jit(solution)/shard_map/ppermute | solution.py:85
  4.8 0.1 collective-permute-start.15
  4.8 1.8 %prepare.1 = (bf16[64,512]{1,0:T(8,128)(2,1)}, bf16[64,512]{1,0:T(8,128)(2,1)}, f32[64,512]{1,0:T(8,128)}, bf16[64,512]{1,0:T(8,128)(2,1)}) custom-call(s32[1,1]{1,0:T(1,128)} %bitcast.me, bf16[512,4096]{1,0:T(8,128)(2,1)} %table_h.1, s32[1,64]{1,0:T(1,128)} %bitcast.88, s32[1,64]{1,0:T(1,128)} %bitcast.89, s32[16,16]{1,0:T(8,128)} %allowed_h.1, ...), custom_call_target="tpu_custom_call" | custom-call | tf_op jit(solution)/shard_map/prepare/pallas_call | solution.py:105
  6.6 0.2 collective-permute-done
  6.9 2.0 %collective-permute-start.1 = (bf16[8,4096]{1,0:T(8,128)(2,1)S(1)}, bf16[8,4096]{1,0:T(8,128)(2,1)S(1)}, u32[]{:S(2)}, u32[]{:S(2)}) collective-permute-start(bf16[8,4096]{1,0:T(8,128)(2,1)S(1)} %maximum_select_fusion.6), channel_id=1, source_target_pairs={{0,4},{1,9},{2,6},{3,11},{4,0},{5,13},{6,2},{7,15},{8,12},{9,1},{1... | collective-permute-start | bytes 196616 | tf_op jit(solution)/shard_map/ppermute | solution.py:85
  8.9 1.0 %collective-permute-done.15 = bf16[4,4096]{1,0:T(4,128)(2,1)S(1)} collective-permute-done((bf16[4,4096]{1,0:T(4,128)(2,1)}, bf16[4,4096]{1,0:T(4,128)(2,1)S(1)}, u32[]{:S(2)}, u32[]{:S(2)}) %collective-permute-start.15) | collective-permute-done | bytes 32800 | tf_op jit(solution)/shard_map/ppermute | solution.py:85
  10.0 1.7 %collective-permute-start.16 = (bf16[8,4096]{1,0:T(8,128)(2,1)S(1)}, bf16[8,4096]{1,0:T(8,128)(2,1)S(1)}, u32[]{:S(2)}, u32[]{:S(2)}) collective-permute-start(bf16[8,4096]{1,0:T(8,128)(2,1)S(1)} %maximum_select_fusion.7), channel_id=1, source_target_pairs={{0,4},{1,9},{2,6},{3,11},{4,0},{5,13},{6,2},{7,15},{8,12},{9,1},{1... | collective-permute-start | bytes 196616 | tf_op jit(solution)/shard_map/ppermute | solution.py:85
  11.7 2.2 %collective-permute-start.2 = (bf16[16,4096]{1,0:T(8,128)(2,1)S(1)}, bf16[16,4096]{1,0:T(8,128)(2,1)S(1)}, u32[]{:S(2)}, u32[]{:S(2)}) collective-permute-start(bf16[16,4096]{1,0:T(8,128)(2,1)S(1)} %maximum_select_fusion.4), channel_id=1, source_target_pairs={{0,2},{1,5},{2,0},{3,7},{4,6},{5,1},{6,4},{7,3},{8,10},{9,13},{10,... | collective-permute-start | bytes 393224 | tf_op jit(solution)/shard_map/ppermute | solution.py:85
  13.9 3.1 %convolution_convert_fusion = bf16[64,4096]{1,0:T(8,128)(2,1)S(1)} fusion(bf16[64,512]{1,0:T(8,128)(2,1)} %get-tuple-element.61, bf16[512,4096]{1,0:T(8,128)(2,1)} %table_h.1), kind=kOutput, calls=%fused_computation | convolution fusion | flops 268697600 | bytes 4784128 | tf_op jit(solution)/shard_map/dot_general | solution.py:141
  17.2 0.5 %collective-permute-start.3 = (bf16[32,4096]{1,0:T(8,128)(2,1)S(1)}, bf16[32,4096]{1,0:T(8,128)(2,1)S(1)}, u32[]{:S(2)}, u32[]{:S(2)}) collective-permute-start(bf16[32,4096]{1,0:T(8,128)(2,1)S(1)} %maximum_select_fusion.2), channel_id=1, source_target_pairs={{0,1},{1,0},{2,3},{3,2},{4,5},{5,4},{6,7},{7,6},{8,9},{9,8},{10,11... | collective-permute-start | bytes 786440 | tf_op jit(solution)/shard_map/ppermute | solution.py:85
  17.7 1.3 %collective-permute-start.17 = (bf16[16,4096]{1,0:T(8,128)(2,1)S(1)}, bf16[16,4096]{1,0:T(8,128)(2,1)S(1)}, u32[]{:S(2)}, u32[]{:S(2)}) collective-permute-start(bf16[16,4096]{1,0:T(8,128)(2,1)S(1)} %maximum_select_fusion.5), channel_id=1, source_target_pairs={{0,2},{1,5},{2,0},{3,7},{4,6},{5,1},{6,4},{7,3},{8,10},{9,13},{10,... | collective-permute-start | bytes 393224 | tf_op jit(solution)/shard_map/ppermute | solution.py:85
  19.1 0.8 %collective-permute-start.11 = (bf16[16,4096]{1,0:T(8,128)(2,1)S(1)}, bf16[16,4096]{1,0:T(8,128)(2,1)S(1)}, u32[]{:S(2)}, u32[]{:S(2)}) collective-permute-start(bf16[16,4096]{1,0:T(8,128)(2,1)S(1)} %broadcast_select_fusion), channel_id=1, source_target_pairs={{0,2},{1,5},{2,0},{3,7},{4,6},{5,1},{6,4},{7,3},{8,10},{9,13},{10,... | collective-permute-start | bytes 393224 | tf_op jit(solution)/shard_map/ppermute | solution.py:85
  19.9 0.1 maximum_select_fusion.hid
  20.0 1.5 %fusion.13 = (f32[64]{0:T(128)S(1)}, f32[64,512]{1,0:T(8,128)S(1)}) fusion(bf16[64,4096]{1,0:T(8,128)(2,1)S(1)} %maximum_select_fusion.hid, bf16[512,4096]{1,0:T(8,128)(2,1)S(1)} %copy-done.1, bf16[64,512]{1,0:T(8,128)(2,1)S(1)} %copy-done.2), kind=kOutput, calls=%fused_computation.68 | convolution fusion | flops 268533696 | bytes 4915456 | tf_op jit(solution)/shard_map/dot_general | solution.py:149
  21.5 0.2 fusion
  21.8 0.9 %fusion.14 = f32[64,4096]{1,0:T(8,128)S(1)} fusion(bf16[64,512]{1,0:T(8,128)(2,1)S(1)} %get-tuple-element.40, bf16[512,4096]{1,0:T(8,128)(2,1)S(1)} %copy-done.1), kind=kOutput, calls=%fused_computation.69 | convolution fusion | flops 268435456 | bytes 5308416 | tf_op jit(solution)/shard_map/dot_general | solution.py:156
  22.8 0.6 %collective-permute-start.5 = (bf16[32,4096]{1,0:T(8,128)(2,1)S(1)}, bf16[32,4096]{1,0:T(8,128)(2,1)S(1)}, u32[]{:S(2)}, u32[]{:S(2)}) collective-permute-start(bf16[32,4096]{1,0:T(8,128)(2,1)S(1)} %select_convert_fusion), channel_id=1, source_target_pairs={{0,1},{1,0},{2,3},{3,2},{4,5},{5,4},{6,7},{7,6},{8,9},{9,8},{10,11... | collective-permute-start | bytes 786440 | tf_op jit(solution)/shard_map/ppermute | solution.py:85
  23.4 0.1 dynamic_slice.36
  23.5 0.1 dynamic_slice.37
  23.6 0.9 %collective-permute-done.5 = bf16[32,4096]{1,0:T(8,128)(2,1)S(1)} collective-permute-done((bf16[32,4096]{1,0:T(8,128)(2,1)S(1)}, bf16[32,4096]{1,0:T(8,128)(2,1)S(1)}, u32[]{:S(2)}, u32[]{:S(2)}) %collective-permute-start.5) | collective-permute-done | bytes 262176 | tf_op jit(solution)/shard_map/ppermute | solution.py:85
  24.5 0.2 multiply_add_fusion
  24.7 1.4 %collective-permute-start.6 = (f32[3,64]{1,0:T(4,128)S(1)}, f32[3,64]{1,0:T(4,128)S(1)}, u32[]{:S(2)}, u32[]{:S(2)}) collective-permute-start(f32[3,64]{1,0:T(4,128)S(1)} %pad_maximum_fusion.2), channel_id=1, source_target_pairs={{0,2},{1,5},{2,0},{3,7},{4,6},{5,1},{6,4},{7,3},{8,10},{9,13},{10,... | collective-permute-start | bytes 2312 | tf_op jit(solution)/shard_map/ppermute | solution.py:85
  26.1 0.8 %collective-permute-start.7 = (bf16[16,4096]{1,0:T(8,128)(2,1)S(1)}, bf16[16,4096]{1,0:T(8,128)(2,1)S(1)}, u32[]{:S(2)}, u32[]{:S(2)}) collective-permute-start(bf16[16,4096]{1,0:T(8,128)(2,1)S(1)} %select_convert_fusion.1), channel_id=1, source_target_pairs={{0,2},{1,5},{2,0},{3,7},{4,6},{5,1},{6,4},{7,3},{8,10},{9,13},{10,... | collective-permute-start | bytes 393224 | tf_op jit(solution)/shard_map/ppermute | solution.py:85
  26.9 1.5 %collective-permute-done.6 = f32[3,64]{1,0:T(4,128)S(1)} collective-permute-done((f32[3,64]{1,0:T(4,128)S(1)}, f32[3,64]{1,0:T(4,128)S(1)}, u32[]{:S(2)}, u32[]{:S(2)}) %collective-permute-start.6) | collective-permute-done | bytes 800 | tf_op jit(solution)/shard_map/ppermute | solution.py:85
  28.4 0.1 dynamic_slice.38
  28.4 0.1 dynamic_slice.39
  28.5 2.6 %collective-permute-done.7 = bf16[16,4096]{1,0:T(8,128)(2,1)S(1)} collective-permute-done((bf16[16,4096]{1,0:T(8,128)(2,1)S(1)}, bf16[16,4096]{1,0:T(8,128)(2,1)S(1)}, u32[]{:S(2)}, u32[]{:S(2)}) %collective-permute-start.7) | collective-permute-done | bytes 131104 | tf_op jit(solution)/shard_map/ppermute | solution.py:85
  31.1 0.1 multiply_add_fusion.1
  31.3 0.9 %collective-permute-start.8 = (f32[3,64]{1,0:T(4,128)S(1)}, f32[3,64]{1,0:T(4,128)S(1)}, u32[]{:S(2)}, u32[]{:S(2)}) collective-permute-start(f32[3,64]{1,0:T(4,128)S(1)} %pad_maximum_fusion.3), channel_id=1, source_target_pairs={{0,4},{1,9},{2,6},{3,11},{4,0},{5,13},{6,2},{7,15},{8,12},{9,1},{1... | collective-permute-start | bytes 2312 | tf_op jit(solution)/shard_map/ppermute | solution.py:85
  32.2 1.2 %collective-permute-start.12 = (bf16[8,4096]{1,0:T(8,128)(2,1)S(1)}, bf16[8,4096]{1,0:T(8,128)(2,1)S(1)}, u32[]{:S(2)}, u32[]{:S(2)}) collective-permute-start(bf16[8,4096]{1,0:T(8,128)(2,1)S(1)} %broadcast_select_fusion.1), channel_id=1, source_target_pairs={{0,4},{1,9},{2,6},{3,11},{4,0},{5,13},{6,2},{7,15},{8,12},{9,1},{1... | collective-permute-start | bytes 196616 | tf_op jit(solution)/shard_map/ppermute | solution.py:85
  33.4 0.9 %collective-permute-start.9 = (bf16[8,4096]{1,0:T(8,128)(2,1)S(1)}, bf16[8,4096]{1,0:T(8,128)(2,1)S(1)}, u32[]{:S(2)}, u32[]{:S(2)}) collective-permute-start(bf16[8,4096]{1,0:T(8,128)(2,1)S(1)} %select_convert_fusion.3), channel_id=1, source_target_pairs={{0,4},{1,9},{2,6},{3,11},{4,0},{5,13},{6,2},{7,15},{8,12},{9,1},{1... | collective-permute-start | bytes 196616 | tf_op jit(solution)/shard_map/ppermute | solution.py:85
  34.3 0.6 %collective-permute-done.8 = f32[3,64]{1,0:T(4,128)S(1)} collective-permute-done((f32[3,64]{1,0:T(4,128)S(1)}, f32[3,64]{1,0:T(4,128)S(1)}, u32[]{:S(2)}, u32[]{:S(2)}) %collective-permute-start.8) | collective-permute-done | bytes 800 | tf_op jit(solution)/shard_map/ppermute | solution.py:85
  34.9 0.1 dynamic_slice.40
  35.0 0.1 dynamic_slice.41
  35.1 1.5 %collective-permute-done.12 = bf16[8,4096]{1,0:T(8,128)(2,1)S(1)} collective-permute-done((bf16[8,4096]{1,0:T(8,128)(2,1)S(1)}, bf16[8,4096]{1,0:T(8,128)(2,1)S(1)}, u32[]{:S(2)}, u32[]{:S(2)}) %collective-permute-start.12) | collective-permute-done | bytes 65568 | tf_op jit(solution)/shard_map/ppermute | solution.py:85
  36.6 1.2 %collective-permute-done.9 = bf16[8,4096]{1,0:T(8,128)(2,1)S(1)} collective-permute-done((bf16[8,4096]{1,0:T(8,128)(2,1)S(1)}, bf16[8,4096]{1,0:T(8,128)(2,1)S(1)}, u32[]{:S(2)}, u32[]{:S(2)}) %collective-permute-start.9) | collective-permute-done | bytes 65568 | tf_op jit(solution)/shard_map/ppermute | solution.py:85
  37.8 0.1 multiply_add_fusion.2
  38.0 2.8 %collective-permute-start.13 = (f32[3,64]{1,0:T(4,128)S(1)}, f32[3,64]{1,0:T(4,128)S(1)}, u32[]{:S(2)}, u32[]{:S(2)}) collective-permute-start(f32[3,64]{1,0:T(4,128)S(1)} %pad_maximum_fusion.4), channel_id=1, source_target_pairs={{0,8},{1,3},{2,10},{3,1},{4,12},{5,7},{6,14},{7,5},{8,0},{9,11},{1... | collective-permute-start | bytes 2312 | tf_op jit(solution)/shard_map/ppermute | solution.py:85
  40.8 0.1 maximum_select_fusion.1.inp
  40.9 0.2 collective-permute-start.14
  41.1 1.4 %collective-permute-done.13 = f32[3,64]{1,0:T(4,128)S(1)} collective-permute-done((f32[3,64]{1,0:T(4,128)S(1)}, f32[3,64]{1,0:T(4,128)S(1)}, u32[]{:S(2)}, u32[]{:S(2)}) %collective-permute-start.13) | collective-permute-done | bytes 800 | tf_op jit(solution)/shard_map/ppermute | solution.py:85
  42.5 0.1 select_convert_fusion.2.dl
  42.7 0.1 dynamic-slice_divide_fusion
  42.8 0.1 dynamic_slice.42
  42.8 0.1 dynamic_slice.43
  42.9 2.4 %table_grad.1 = bf16[512,4096]{1,0:T(8,128)(2,1)} custom-call(bf16[64,512]{1,0:T(8,128)(2,1)S(1)} %select_convert_fusion.2.dl, bf16[64,512]{1,0:T(8,128)(2,1)S(1)} %copy-done, bf16[64,4096]{1,0:T(8,128)(2,1)S(1)} %maximum_select_fusion.hid, bf16[64,4096]{1,0:T(8,128)(2,1)S(1)} %maximum_select_fusion.1.inp), custom_call_target="tpu_custom_call" | custom-call | flops 536870912 | bytes 4194304 | tf_op jit(solution)/shard_map/table_grad/pallas_call | solution.py:203
  45.3 0.8 %collective-permute-done.14 = bf16[8,4096]{1,0:T(8,128)(2,1)S(1)} collective-permute-done((bf16[8,4096]{1,0:T(8,128)(2,1)S(1)}, bf16[8,4096]{1,0:T(8,128)(2,1)S(1)}, u32[]{:S(2)}, u32[]{:S(2)}) %collective-permute-start.14) | collective-permute-done | bytes 65568 | tf_op jit(solution)/shard_map/ppermute | solution.py:85
  46.2 0.7 %add_convert_fusion = bf16[4,4096]{1,0:T(4,128)(2,1)} fusion(f32[8,4096]{1,0:T(8,128)S(1)} %multiply_add_fusion.2, bf16[8,4096]{1,0:T(8,128)(2,1)S(1)} %collective-permute-done.14, f32[4]{0:T(128)S(1)} %get-tuple-element.100, f32[4]{0:T(128)S(1)} %get-tuple-element.99, f32[4]{0:T(128)S(1)} %dynamic_slice.43, f32[4]{0:T(128)S(1)} %dynamic_slice.42, ...), kind=kLoop, calls=%fused_computation.25 | loop fusion | flops 196608 | bytes 294977 | tf_op jit(solution)/shard_map/convert_element_type | solution.py:201
  (52 shorter events, 0.9 us)
Async XLA Ops:
  0.6 6.2 %copy-start.4 = (bf16[4,4096]{1,0:T(4,128)(2,1)S(1)}, bf16[4,4096]{1,0:T(4,128)(2,1)}, u32[]{:S(2)}) copy-start(bf16[4,4096]{1,0:T(4,128)(2,1)} %param.8) | copy-start | bytes 98308
  0.6 9.3 %copy-start.5 = (bf16[4,4096]{1,0:T(4,128)(2,1)S(1)}, bf16[4,4096]{1,0:T(4,128)(2,1)}, u32[]{:S(2)}) copy-start(bf16[4,4096]{1,0:T(4,128)(2,1)} %param.10) | copy-start | bytes 98308
  0.7 6.2 %collective-permute-start = (bf16[4,4096]{1,0:T(4,128)(2,1)}, bf16[4,4096]{1,0:T(4,128)(2,1)S(1)}, u32[]{:S(2)}, u32[]{:S(2)}) collective-permute-start(bf16[4,4096]{1,0:T(4,128)(2,1)} %param.8), channel_id=1, source_target_pairs={{0,8},{1,3},{2,10},{3,1},{4,12},{5,7},{6,14},{7,5},{8,0},{9,11},{1... | collective-permute-start | bytes 98312 | tf_op jit(solution)/shard_map/ppermute | solution.py:85
  4.8 5.2 %collective-permute-start.15 = (bf16[4,4096]{1,0:T(4,128)(2,1)}, bf16[4,4096]{1,0:T(4,128)(2,1)S(1)}, u32[]{:S(2)}, u32[]{:S(2)}) collective-permute-start(bf16[4,4096]{1,0:T(4,128)(2,1)} %param.10), channel_id=1, source_target_pairs={{0,8},{1,3},{2,10},{3,1},{4,12},{5,7},{6,14},{7,5},{8,0},{9,11},{1... | collective-permute-start | bytes 98312 | tf_op jit(solution)/shard_map/ppermute | solution.py:85
  6.9 4.8 %collective-permute-start.1 = (bf16[8,4096]{1,0:T(8,128)(2,1)S(1)}, bf16[8,4096]{1,0:T(8,128)(2,1)S(1)}, u32[]{:S(2)}, u32[]{:S(2)}) collective-permute-start(bf16[8,4096]{1,0:T(8,128)(2,1)S(1)} %maximum_select_fusion.6), channel_id=1, source_target_pairs={{0,4},{1,9},{2,6},{3,11},{4,0},{5,13},{6,2},{7,15},{8,12},{9,1},{1... | collective-permute-start | bytes 196616 | tf_op jit(solution)/shard_map/ppermute | solution.py:85
  10.0 7.1 %collective-permute-start.16 = (bf16[8,4096]{1,0:T(8,128)(2,1)S(1)}, bf16[8,4096]{1,0:T(8,128)(2,1)S(1)}, u32[]{:S(2)}, u32[]{:S(2)}) collective-permute-start(bf16[8,4096]{1,0:T(8,128)(2,1)S(1)} %maximum_select_fusion.7), channel_id=1, source_target_pairs={{0,4},{1,9},{2,6},{3,11},{4,0},{5,13},{6,2},{7,15},{8,12},{9,1},{1... | collective-permute-start | bytes 196616 | tf_op jit(solution)/shard_map/ppermute | solution.py:85
  11.7 8.3 %copy-start.1 = (bf16[512,4096]{1,0:T(8,128)(2,1)S(1)}, bf16[512,4096]{1,0:T(8,128)(2,1)}, u32[]{:S(2)}) copy-start(bf16[512,4096]{1,0:T(8,128)(2,1)} %table_h.1) | copy-start | bytes 12582916
  11.7 8.3 %copy-start.2 = (bf16[64,512]{1,0:T(8,128)(2,1)S(1)}, bf16[64,512]{1,0:T(8,128)(2,1)}, u32[]{:S(2)}) copy-start(bf16[64,512]{1,0:T(8,128)(2,1)} %get-tuple-element.39) | copy-start | bytes 196612
  11.7 5.4 %collective-permute-start.2 = (bf16[16,4096]{1,0:T(8,128)(2,1)S(1)}, bf16[16,4096]{1,0:T(8,128)(2,1)S(1)}, u32[]{:S(2)}, u32[]{:S(2)}) collective-permute-start(bf16[16,4096]{1,0:T(8,128)(2,1)S(1)} %maximum_select_fusion.4), channel_id=1, source_target_pairs={{0,2},{1,5},{2,0},{3,7},{4,6},{5,1},{6,4},{7,3},{8,10},{9,13},{10,... | collective-permute-start | bytes 393224 | tf_op jit(solution)/shard_map/ppermute | solution.py:85
  17.0 2.1 %collective-permute-start.10 = (bf16[32,4096]{1,0:T(8,128)(2,1)S(1)}, bf16[32,4096]{1,0:T(8,128)(2,1)S(1)}, u32[]{:S(2)}, u32[]{:S(2)}) collective-permute-start(bf16[32,4096]{1,0:T(8,128)(2,1)S(1)} %slice.133), channel_id=1, source_target_pairs={{0,1},{1,0},{2,3},{3,2},{4,5},{5,4},{6,7},{7,6},{8,9},{9,8},{10,11... | collective-permute-start | bytes 786440 | tf_op jit(solution)/shard_map/ppermute | solution.py:85
  17.2 2.7 %collective-permute-start.3 = (bf16[32,4096]{1,0:T(8,128)(2,1)S(1)}, bf16[32,4096]{1,0:T(8,128)(2,1)S(1)}, u32[]{:S(2)}, u32[]{:S(2)}) collective-permute-start(bf16[32,4096]{1,0:T(8,128)(2,1)S(1)} %maximum_select_fusion.2), channel_id=1, source_target_pairs={{0,1},{1,0},{2,3},{3,2},{4,5},{5,4},{6,7},{7,6},{8,9},{9,8},{10,11... | collective-permute-start | bytes 786440 | tf_op jit(solution)/shard_map/ppermute | solution.py:85
  17.7 5.6 %collective-permute-start.17 = (bf16[16,4096]{1,0:T(8,128)(2,1)S(1)}, bf16[16,4096]{1,0:T(8,128)(2,1)S(1)}, u32[]{:S(2)}, u32[]{:S(2)}) collective-permute-start(bf16[16,4096]{1,0:T(8,128)(2,1)S(1)} %maximum_select_fusion.5), channel_id=1, source_target_pairs={{0,2},{1,5},{2,0},{3,7},{4,6},{5,1},{6,4},{7,3},{8,10},{9,13},{10,... | collective-permute-start | bytes 393224 | tf_op jit(solution)/shard_map/ppermute | solution.py:85
  19.1 5.6 %collective-permute-start.11 = (bf16[16,4096]{1,0:T(8,128)(2,1)S(1)}, bf16[16,4096]{1,0:T(8,128)(2,1)S(1)}, u32[]{:S(2)}, u32[]{:S(2)}) collective-permute-start(bf16[16,4096]{1,0:T(8,128)(2,1)S(1)} %broadcast_select_fusion), channel_id=1, source_target_pairs={{0,2},{1,5},{2,0},{3,7},{4,6},{5,1},{6,4},{7,3},{8,10},{9,13},{10,... | collective-permute-start | bytes 393224 | tf_op jit(solution)/shard_map/ppermute | solution.py:85
  21.7 1.6 %collective-permute-start.4 = (f32[3,64]{1,0:T(4,128)S(1)}, f32[3,64]{1,0:T(4,128)S(1)}, u32[]{:S(2)}, u32[]{:S(2)}) collective-permute-start(f32[3,64]{1,0:T(4,128)S(1)} %pad_maximum_fusion.1), channel_id=1, source_target_pairs={{0,1},{1,0},{2,3},{3,2},{4,5},{5,4},{6,7},{7,6},{8,9},{9,8},{10,11... | collective-permute-start | bytes 2312 | tf_op jit(solution)/shard_map/ppermute | solution.py:85
  22.7 19.9 %copy-start.3 = (f32[64,512]{1,0:T(8,128)S(1)}, f32[64,512]{1,0:T(8,128)}, u32[]{:S(2)}) copy-start(f32[64,512]{1,0:T(8,128)} %get-tuple-element.72) | copy-start | bytes 393220
  22.7 20.0 %copy-start.6 = (f32[64]{0:T(128)S(1)}, f32[64]{0:T(128)}, u32[]{:S(2)}) copy-start(f32[64]{0:T(128)} %param.15) | copy-start | bytes 772
  22.7 20.2 %copy-start = (bf16[64,512]{1,0:T(8,128)(2,1)S(1)}, bf16[64,512]{1,0:T(8,128)(2,1)}, u32[]{:S(2)}) copy-start(bf16[64,512]{1,0:T(8,128)(2,1)} %get-tuple-element.73.took) | copy-start | bytes 196612
  22.8 1.7 %collective-permute-start.5 = (bf16[32,4096]{1,0:T(8,128)(2,1)S(1)}, bf16[32,4096]{1,0:T(8,128)(2,1)S(1)}, u32[]{:S(2)}, u32[]{:S(2)}) collective-permute-start(bf16[32,4096]{1,0:T(8,128)(2,1)S(1)} %select_convert_fusion), channel_id=1, source_target_pairs={{0,1},{1,0},{2,3},{3,2},{4,5},{5,4},{6,7},{7,6},{8,9},{9,8},{10,11... | collective-permute-start | bytes 786440 | tf_op jit(solution)/shard_map/ppermute | solution.py:85
  23.6 17.3 %collective-permute-start.18 = (bf16[32,4096]{1,0:T(8,128)(2,1)S(1)}, bf16[32,4096]{1,0:T(8,128)(2,1)S(1)}, u32[]{:S(2)}, u32[]{:S(2)}) collective-permute-start(bf16[32,4096]{1,0:T(8,128)(2,1)S(1)} %maximum_select_fusion.3), channel_id=1, source_target_pairs={{0,1},{1,0},{2,3},{3,2},{4,5},{5,4},{6,7},{7,6},{8,9},{9,8},{10,11... | collective-permute-start | bytes 786440 | tf_op jit(solution)/shard_map/ppermute | solution.py:85
  24.7 3.7 %collective-permute-start.6 = (f32[3,64]{1,0:T(4,128)S(1)}, f32[3,64]{1,0:T(4,128)S(1)}, u32[]{:S(2)}, u32[]{:S(2)}) collective-permute-start(f32[3,64]{1,0:T(4,128)S(1)} %pad_maximum_fusion.2), channel_id=1, source_target_pairs={{0,2},{1,5},{2,0},{3,7},{4,6},{5,1},{6,4},{7,3},{8,10},{9,13},{10,... | collective-permute-start | bytes 2312 | tf_op jit(solution)/shard_map/ppermute | solution.py:85
  26.1 5.0 %collective-permute-start.7 = (bf16[16,4096]{1,0:T(8,128)(2,1)S(1)}, bf16[16,4096]{1,0:T(8,128)(2,1)S(1)}, u32[]{:S(2)}, u32[]{:S(2)}) collective-permute-start(bf16[16,4096]{1,0:T(8,128)(2,1)S(1)} %select_convert_fusion.1), channel_id=1, source_target_pairs={{0,2},{1,5},{2,0},{3,7},{4,6},{5,1},{6,4},{7,3},{8,10},{9,13},{10,... | collective-permute-start | bytes 393224 | tf_op jit(solution)/shard_map/ppermute | solution.py:85
  31.3 3.7 %collective-permute-start.8 = (f32[3,64]{1,0:T(4,128)S(1)}, f32[3,64]{1,0:T(4,128)S(1)}, u32[]{:S(2)}, u32[]{:S(2)}) collective-permute-start(f32[3,64]{1,0:T(4,128)S(1)} %pad_maximum_fusion.3), channel_id=1, source_target_pairs={{0,4},{1,9},{2,6},{3,11},{4,0},{5,13},{6,2},{7,15},{8,12},{9,1},{1... | collective-permute-start | bytes 2312 | tf_op jit(solution)/shard_map/ppermute | solution.py:85
  32.2 4.3 %collective-permute-start.12 = (bf16[8,4096]{1,0:T(8,128)(2,1)S(1)}, bf16[8,4096]{1,0:T(8,128)(2,1)S(1)}, u32[]{:S(2)}, u32[]{:S(2)}) collective-permute-start(bf16[8,4096]{1,0:T(8,128)(2,1)S(1)} %broadcast_select_fusion.1), channel_id=1, source_target_pairs={{0,4},{1,9},{2,6},{3,11},{4,0},{5,13},{6,2},{7,15},{8,12},{9,1},{1... | collective-permute-start | bytes 196616 | tf_op jit(solution)/shard_map/ppermute | solution.py:85
  33.4 4.4 %collective-permute-start.9 = (bf16[8,4096]{1,0:T(8,128)(2,1)S(1)}, bf16[8,4096]{1,0:T(8,128)(2,1)S(1)}, u32[]{:S(2)}, u32[]{:S(2)}) collective-permute-start(bf16[8,4096]{1,0:T(8,128)(2,1)S(1)} %select_convert_fusion.3), channel_id=1, source_target_pairs={{0,4},{1,9},{2,6},{3,11},{4,0},{5,13},{6,2},{7,15},{8,12},{9,1},{1... | collective-permute-start | bytes 196616 | tf_op jit(solution)/shard_map/ppermute | solution.py:85
  38.0 4.5 %collective-permute-start.13 = (f32[3,64]{1,0:T(4,128)S(1)}, f32[3,64]{1,0:T(4,128)S(1)}, u32[]{:S(2)}, u32[]{:S(2)}) collective-permute-start(f32[3,64]{1,0:T(4,128)S(1)} %pad_maximum_fusion.4), channel_id=1, source_target_pairs={{0,8},{1,3},{2,10},{3,1},{4,12},{5,7},{6,14},{7,5},{8,0},{9,11},{1... | collective-permute-start | bytes 2312 | tf_op jit(solution)/shard_map/ppermute | solution.py:85
  40.9 5.2 %collective-permute-start.14 = (bf16[8,4096]{1,0:T(8,128)(2,1)S(1)}, bf16[8,4096]{1,0:T(8,128)(2,1)S(1)}, u32[]{:S(2)}, u32[]{:S(2)}) collective-permute-start(bf16[8,4096]{1,0:T(8,128)(2,1)S(1)} %pad_maximum_fusion), channel_id=1, source_target_pairs={{0,8},{1,3},{2,10},{3,1},{4,12},{5,7},{6,14},{7,5},{8,0},{9,11},{1... | collective-permute-start | bytes 196616 | tf_op jit(solution)/shard_map/ppermute | solution.py:85

commit v6 on v5

--- a/solution.py
+++ b/solution.py
@@ -180,15 +180,13 @@
         if k == 1:
             all_input = join(all_input, after(input_got, m), 2)
             all_input = join(all_input, swap(all_input, 1), 1)
-        elif 2 < k < n // 2:
-            rows = rows_keep + after(rows_got, m)
-        if 1 < k < n // 4:
-            rows_keep, rows_send = halves(after(rows, m), 2 * k)
-            rows_got = swap(rows_send, 2 * k)
         lo = lo + jnp.where(bit(k), size, 0)
         part = keep * lax.dynamic_slice_in_dim(a, lo, size)[:, None] + recv[:size].astype(f32) * lax.dynamic_slice_in_dim(b, lo, size)[:, None]
-        if k == 1:
+        if k < n // 4:
             rows = rows_keep + after(rows_got, part)
+        if k < n // 8:
+            rows_keep, rows_send = halves(rows, 4 * k)
+            rows_got = swap(rows_send, 4 * k)
         k *= 2
 
     hot = is_target.astype(f32)

time: 47.1 us -> 46.8 us (level)
  transfers between devices with their start and end apart: 19 -> 19, of which waited for: 10 -> 8; matrix products, arithmetic and copies ran while one was open for 16% -> 16% of each run, Pallas kernels for 9% -> 9%
where the time goes in v6:
time: 46.8 us; the launch traced here: 46.6 us
  starting transfers between devices  21.6 us (46%)
  waiting for transfers between devices  11.4 us (24%)
  matrix products  5.44 us (12%)
  Pallas kernels  4.2 us (9%)
  other arithmetic  2.3 us (5%)
  between operations  0.98 us (2%)
  local copies, waits for them, and re-layouts  0.66 us (1%)
    ppermute x19, starting transfers between devices, swap(): return lax.ppermute(x, 'vocab', [(i, i ^ ks[i & 1]) for i in range(n)])  21.6 us
    ppermute x19, waiting for transfers between devices, swap(): return lax.ppermute(x, 'vocab', [(i, i ^ ks[i & 1]) for i in range(n)])  11.4 us
    dot_general x1, matrix products, per_device(): jnp.dot(after(pick, all_hidden), embedding, preferred_element_type=f32)  3.07 us
    pallas_call x1, Pallas kernels, per_device(): pl.pallas_call(functools.partial(table_grad, tiles), out_shape=jax.ShapeD...  2.4 us
    pallas_call x1, Pallas kernels, per_device(): pl.pallas_call(functools.partial(prepare, mine, steps), out_shape=(jax.Sh...  1.8 us
    dot_general x1, matrix products, per_device(): lax.dot_general(all_hidden, embedding, (((1,), (1,)), ((), ())), preferre...  1.49 us
  transfers between devices with their start and end apart: 19, of which 8 were waited for; matrix products, arithmetic and copies ran while one was open for 16% of the time, Pallas kernels for 9%

profile of v6, /device:TPU:0, one launch (start us, length us, event | category | flops | bytes accessed | tf_op | source)
XLA Modules:
  0.0 46.6 jit_solution(12398224730800641258)
XLA Ops:
  0.7 4.1 %collective-permute-start = (bf16[4,4096]{1,0:T(4,128)(2,1)}, bf16[4,4096]{1,0:T(4,128)(2,1)S(1)}, u32[]{:S(2)}, u32[]{:S(2)}) collective-permute-start(bf16[4,4096]{1,0:T(4,128)(2,1)} %param.8), channel_id=1, source_target_pairs={{0,8},{1,3},{2,10},{3,1},{4,12},{5,7},{6,14},{7,5},{8,0},{9,11},{1... | collective-permute-start | bytes 98312 | tf_op jit(solution)/shard_map/ppermute | solution.py:85
  4.8 0.1 collective-permute-start.15
  4.8 1.8 %prepare.1 = (bf16[64,512]{1,0:T(8,128)(2,1)}, bf16[64,512]{1,0:T(8,128)(2,1)}, f32[64,512]{1,0:T(8,128)}, bf16[64,512]{1,0:T(8,128)(2,1)}) custom-call(s32[1,1]{1,0:T(1,128)} %bitcast.me, bf16[512,4096]{1,0:T(8,128)(2,1)} %table_h.1, s32[1,64]{1,0:T(1,128)} %bitcast.88, s32[1,64]{1,0:T(1,128)} %bitcast.89, s32[16,16]{1,0:T(8,128)} %allowed_h.1, ...), custom_call_target="tpu_custom_call" | custom-call | tf_op jit(solution)/shard_map/prepare/pallas_call | solution.py:105
  6.6 0.2 collective-permute-done
  6.9 2.0 %collective-permute-start.1 = (bf16[8,4096]{1,0:T(8,128)(2,1)S(1)}, bf16[8,4096]{1,0:T(8,128)(2,1)S(1)}, u32[]{:S(2)}, u32[]{:S(2)}) collective-permute-start(bf16[8,4096]{1,0:T(8,128)(2,1)S(1)} %maximum_select_fusion.6), channel_id=1, source_target_pairs={{0,4},{1,9},{2,6},{3,11},{4,0},{5,13},{6,2},{7,15},{8,12},{9,1},{1... | collective-permute-start | bytes 196616 | tf_op jit(solution)/shard_map/ppermute | solution.py:85
  8.9 1.0 %collective-permute-done.15 = bf16[4,4096]{1,0:T(4,128)(2,1)S(1)} collective-permute-done((bf16[4,4096]{1,0:T(4,128)(2,1)}, bf16[4,4096]{1,0:T(4,128)(2,1)S(1)}, u32[]{:S(2)}, u32[]{:S(2)}) %collective-permute-start.15) | collective-permute-done | bytes 32800 | tf_op jit(solution)/shard_map/ppermute | solution.py:85
  10.0 1.7 %collective-permute-start.16 = (bf16[8,4096]{1,0:T(8,128)(2,1)S(1)}, bf16[8,4096]{1,0:T(8,128)(2,1)S(1)}, u32[]{:S(2)}, u32[]{:S(2)}) collective-permute-start(bf16[8,4096]{1,0:T(8,128)(2,1)S(1)} %maximum_select_fusion.7), channel_id=1, source_target_pairs={{0,4},{1,9},{2,6},{3,11},{4,0},{5,13},{6,2},{7,15},{8,12},{9,1},{1... | collective-permute-start | bytes 196616 | tf_op jit(solution)/shard_map/ppermute | solution.py:85
  11.7 2.2 %collective-permute-start.2 = (bf16[16,4096]{1,0:T(8,128)(2,1)S(1)}, bf16[16,4096]{1,0:T(8,128)(2,1)S(1)}, u32[]{:S(2)}, u32[]{:S(2)}) collective-permute-start(bf16[16,4096]{1,0:T(8,128)(2,1)S(1)} %maximum_select_fusion.4), channel_id=1, source_target_pairs={{0,2},{1,5},{2,0},{3,7},{4,6},{5,1},{6,4},{7,3},{8,10},{9,13},{10,... | collective-permute-start | bytes 393224 | tf_op jit(solution)/shard_map/ppermute | solution.py:85
  13.9 3.1 %convolution_convert_fusion = bf16[64,4096]{1,0:T(8,128)(2,1)S(1)} fusion(bf16[64,512]{1,0:T(8,128)(2,1)} %get-tuple-element.60, bf16[512,4096]{1,0:T(8,128)(2,1)} %table_h.1), kind=kOutput, calls=%fused_computation | convolution fusion | flops 268697600 | bytes 4784128 | tf_op jit(solution)/shard_map/dot_general | solution.py:141
  17.0 0.1 collective-permute-start.10
  17.2 0.5 %collective-permute-start.3 = (bf16[32,4096]{1,0:T(8,128)(2,1)S(1)}, bf16[32,4096]{1,0:T(8,128)(2,1)S(1)}, u32[]{:S(2)}, u32[]{:S(2)}) collective-permute-start(bf16[32,4096]{1,0:T(8,128)(2,1)S(1)} %maximum_select_fusion.2), channel_id=1, source_target_pairs={{0,1},{1,0},{2,3},{3,2},{4,5},{5,4},{6,7},{7,6},{8,9},{9,8},{10,11... | collective-permute-start | bytes 786440 | tf_op jit(solution)/shard_map/ppermute | solution.py:85
  17.7 1.3 %collective-permute-start.17 = (bf16[16,4096]{1,0:T(8,128)(2,1)S(1)}, bf16[16,4096]{1,0:T(8,128)(2,1)S(1)}, u32[]{:S(2)}, u32[]{:S(2)}) collective-permute-start(bf16[16,4096]{1,0:T(8,128)(2,1)S(1)} %maximum_select_fusion.5), channel_id=1, source_target_pairs={{0,2},{1,5},{2,0},{3,7},{4,6},{5,1},{6,4},{7,3},{8,10},{9,13},{10,... | collective-permute-start | bytes 393224 | tf_op jit(solution)/shard_map/ppermute | solution.py:85
  19.1 0.8 %collective-permute-start.11 = (bf16[16,4096]{1,0:T(8,128)(2,1)S(1)}, bf16[16,4096]{1,0:T(8,128)(2,1)S(1)}, u32[]{:S(2)}, u32[]{:S(2)}) collective-permute-start(bf16[16,4096]{1,0:T(8,128)(2,1)S(1)} %broadcast_select_fusion), channel_id=1, source_target_pairs={{0,2},{1,5},{2,0},{3,7},{4,6},{5,1},{6,4},{7,3},{8,10},{9,13},{10,... | collective-permute-start | bytes 393224 | tf_op jit(solution)/shard_map/ppermute | solution.py:85
  19.9 0.1 maximum_select_fusion.hid
  20.0 1.5 %fusion.13 = (f32[64]{0:T(128)S(1)}, f32[64,512]{1,0:T(8,128)S(1)}) fusion(bf16[64,4096]{1,0:T(8,128)(2,1)S(1)} %maximum_select_fusion.hid, bf16[512,4096]{1,0:T(8,128)(2,1)S(1)} %copy-done.1, bf16[64,512]{1,0:T(8,128)(2,1)S(1)} %copy-done.2), kind=kOutput, calls=%fused_computation.68 | convolution fusion | flops 268533696 | bytes 4915456 | tf_op jit(solution)/shard_map/dot_general | solution.py:149
  21.5 0.2 fusion
  21.7 0.1 collective-permute-start.4
  21.8 0.9 %fusion.14 = f32[64,4096]{1,0:T(8,128)S(1)} fusion(bf16[64,512]{1,0:T(8,128)(2,1)S(1)} %get-tuple-element.39, bf16[512,4096]{1,0:T(8,128)(2,1)S(1)} %copy-done.1), kind=kOutput, calls=%fused_computation.69 | convolution fusion | flops 268435456 | bytes 5308416 | tf_op jit(solution)/shard_map/dot_general | solution.py:156
  22.8 0.6 %collective-permute-start.5 = (bf16[32,4096]{1,0:T(8,128)(2,1)S(1)}, bf16[32,4096]{1,0:T(8,128)(2,1)S(1)}, u32[]{:S(2)}, u32[]{:S(2)}) collective-permute-start(bf16[32,4096]{1,0:T(8,128)(2,1)S(1)} %select_convert_fusion), channel_id=1, source_target_pairs={{0,1},{1,0},{2,3},{3,2},{4,5},{5,4},{6,7},{7,6},{8,9},{9,8},{10,11... | collective-permute-start | bytes 786440 | tf_op jit(solution)/shard_map/ppermute | solution.py:85
  23.4 0.1 dynamic_slice.36
  23.5 0.1 dynamic_slice.37
  23.6 0.9 %collective-permute-done.5 = bf16[32,4096]{1,0:T(8,128)(2,1)S(1)} collective-permute-done((bf16[32,4096]{1,0:T(8,128)(2,1)S(1)}, bf16[32,4096]{1,0:T(8,128)(2,1)S(1)}, u32[]{:S(2)}, u32[]{:S(2)}) %collective-permute-start.5) | collective-permute-done | bytes 262176 | tf_op jit(solution)/shard_map/ppermute | solution.py:85
  24.5 0.2 multiply_add_fusion
  24.7 1.4 %collective-permute-start.6 = (f32[3,64]{1,0:T(4,128)S(1)}, f32[3,64]{1,0:T(4,128)S(1)}, u32[]{:S(2)}, u32[]{:S(2)}) collective-permute-start(f32[3,64]{1,0:T(4,128)S(1)} %pad_maximum_fusion.2), channel_id=1, source_target_pairs={{0,2},{1,5},{2,0},{3,7},{4,6},{5,1},{6,4},{7,3},{8,10},{9,13},{10,... | collective-permute-start | bytes 2312 | tf_op jit(solution)/shard_map/ppermute | solution.py:85
  26.1 0.9 %collective-permute-start.12 = (bf16[8,4096]{1,0:T(8,128)(2,1)S(1)}, bf16[8,4096]{1,0:T(8,128)(2,1)S(1)}, u32[]{:S(2)}, u32[]{:S(2)}) collective-permute-start(bf16[8,4096]{1,0:T(8,128)(2,1)S(1)} %broadcast_select_fusion.1), channel_id=1, source_target_pairs={{0,4},{1,9},{2,6},{3,11},{4,0},{5,13},{6,2},{7,15},{8,12},{9,1},{1... | collective-permute-start | bytes 196616 | tf_op jit(solution)/shard_map/ppermute | solution.py:85
  27.1 0.7 %collective-permute-start.7 = (bf16[16,4096]{1,0:T(8,128)(2,1)S(1)}, bf16[16,4096]{1,0:T(8,128)(2,1)S(1)}, u32[]{:S(2)}, u32[]{:S(2)}) collective-permute-start(bf16[16,4096]{1,0:T(8,128)(2,1)S(1)} %select_convert_fusion.1), channel_id=1, source_target_pairs={{0,2},{1,5},{2,0},{3,7},{4,6},{5,1},{6,4},{7,3},{8,10},{9,13},{10,... | collective-permute-start | bytes 393224 | tf_op jit(solution)/shard_map/ppermute | solution.py:85
  27.8 0.6 %collective-permute-done.6 = f32[3,64]{1,0:T(4,128)S(1)} collective-permute-done((f32[3,64]{1,0:T(4,128)S(1)}, f32[3,64]{1,0:T(4,128)S(1)}, u32[]{:S(2)}, u32[]{:S(2)}) %collective-permute-start.6) | collective-permute-done | bytes 800 | tf_op jit(solution)/shard_map/ppermute | solution.py:85
  28.4 0.1 dynamic_slice.38
  28.5 0.1 dynamic_slice.39
  28.6 3.5 %collective-permute-done.7 = bf16[16,4096]{1,0:T(8,128)(2,1)S(1)} collective-permute-done((bf16[16,4096]{1,0:T(8,128)(2,1)S(1)}, bf16[16,4096]{1,0:T(8,128)(2,1)S(1)}, u32[]{:S(2)}, u32[]{:S(2)}) %collective-permute-start.7) | collective-permute-done | bytes 131104 | tf_op jit(solution)/shard_map/ppermute | solution.py:85
  32.0 0.1 multiply_add_fusion.1
  32.2 1.2 %collective-permute-start.8 = (f32[3,64]{1,0:T(4,128)S(1)}, f32[3,64]{1,0:T(4,128)S(1)}, u32[]{:S(2)}, u32[]{:S(2)}) collective-permute-start(f32[3,64]{1,0:T(4,128)S(1)} %pad_maximum_fusion.3), channel_id=1, source_target_pairs={{0,4},{1,9},{2,6},{3,11},{4,0},{5,13},{6,2},{7,15},{8,12},{9,1},{1... | collective-permute-start | bytes 2312 | tf_op jit(solution)/shard_map/ppermute | solution.py:85
  33.5 0.9 %collective-permute-start.9 = (bf16[8,4096]{1,0:T(8,128)(2,1)S(1)}, bf16[8,4096]{1,0:T(8,128)(2,1)S(1)}, u32[]{:S(2)}, u32[]{:S(2)}) collective-permute-start(bf16[8,4096]{1,0:T(8,128)(2,1)S(1)} %select_convert_fusion.3), channel_id=1, source_target_pairs={{0,4},{1,9},{2,6},{3,11},{4,0},{5,13},{6,2},{7,15},{8,12},{9,1},{1... | collective-permute-start | bytes 196616 | tf_op jit(solution)/shard_map/ppermute | solution.py:85
  34.4 1.5 %collective-permute-done.8 = f32[3,64]{1,0:T(4,128)S(1)} collective-permute-done((f32[3,64]{1,0:T(4,128)S(1)}, f32[3,64]{1,0:T(4,128)S(1)}, u32[]{:S(2)}, u32[]{:S(2)}) %collective-permute-start.8) | collective-permute-done | bytes 800 | tf_op jit(solution)/shard_map/ppermute | solution.py:85
  35.9 0.1 dynamic_slice.40
  35.9 0.1 dynamic_slice.41
  36.0 2.3 %collective-permute-done.9 = bf16[8,4096]{1,0:T(8,128)(2,1)S(1)} collective-permute-done((bf16[8,4096]{1,0:T(8,128)(2,1)S(1)}, bf16[8,4096]{1,0:T(8,128)(2,1)S(1)}, u32[]{:S(2)}, u32[]{:S(2)}) %collective-permute-start.9) | collective-permute-done | bytes 65568 | tf_op jit(solution)/shard_map/ppermute | solution.py:85
  38.3 0.1 multiply_add_fusion.2
  38.5 1.8 %collective-permute-start.13 = (f32[3,64]{1,0:T(4,128)S(1)}, f32[3,64]{1,0:T(4,128)S(1)}, u32[]{:S(2)}, u32[]{:S(2)}) collective-permute-start(f32[3,64]{1,0:T(4,128)S(1)} %pad_maximum_fusion.4), channel_id=1, source_target_pairs={{0,8},{1,3},{2,10},{3,1},{4,12},{5,7},{6,14},{7,5},{8,0},{9,11},{1... | collective-permute-start | bytes 2312 | tf_op jit(solution)/shard_map/ppermute | solution.py:85
  40.3 0.1 maximum_select_fusion.1.inp
  40.4 1.3 %collective-permute-start.14 = (bf16[8,4096]{1,0:T(8,128)(2,1)S(1)}, bf16[8,4096]{1,0:T(8,128)(2,1)S(1)}, u32[]{:S(2)}, u32[]{:S(2)}) collective-permute-start(bf16[8,4096]{1,0:T(8,128)(2,1)S(1)} %pad_maximum_fusion), channel_id=1, source_target_pairs={{0,8},{1,3},{2,10},{3,1},{4,12},{5,7},{6,14},{7,5},{8,0},{9,11},{1... | collective-permute-start | bytes 196616 | tf_op jit(solution)/shard_map/ppermute | solution.py:85
  41.7 1.4 %collective-permute-done.13 = f32[3,64]{1,0:T(4,128)S(1)} collective-permute-done((f32[3,64]{1,0:T(4,128)S(1)}, f32[3,64]{1,0:T(4,128)S(1)}, u32[]{:S(2)}, u32[]{:S(2)}) %collective-permute-start.13) | collective-permute-done | bytes 800 | tf_op jit(solution)/shard_map/ppermute | solution.py:85
  43.1 0.1 select_convert_fusion.2.dl
  43.2 0.1 dynamic-slice_divide_fusion
  43.3 0.1 dynamic_slice.42
  43.4 0.1 dynamic_slice.43
  43.5 2.4 %table_grad.1 = bf16[512,4096]{1,0:T(8,128)(2,1)} custom-call(bf16[64,512]{1,0:T(8,128)(2,1)S(1)} %select_convert_fusion.2.dl, bf16[64,512]{1,0:T(8,128)(2,1)S(1)} %copy-done, bf16[64,4096]{1,0:T(8,128)(2,1)S(1)} %maximum_select_fusion.hid, bf16[64,4096]{1,0:T(8,128)(2,1)S(1)} %maximum_select_fusion.1.inp), custom_call_target="tpu_custom_call" | custom-call | flops 536870912 | bytes 4194304 | tf_op jit(solution)/shard_map/table_grad/pallas_call | solution.py:201
  45.9 0.7 %add_convert_fusion = bf16[4,4096]{1,0:T(4,128)(2,1)} fusion(f32[8,4096]{1,0:T(8,128)S(1)} %multiply_add_fusion.2, bf16[8,4096]{1,0:T(8,128)(2,1)S(1)} %collective-permute-done.14, f32[4]{0:T(128)S(1)} %get-tuple-element.98, f32[4]{0:T(128)S(1)} %get-tuple-element.97, f32[4]{0:T(128)S(1)} %dynamic_slice.43, f32[4]{0:T(128)S(1)} %dynamic_slice.42, ...), kind=kLoop, calls=%fused_computation.25 | loop fusion | flops 196608 | bytes 294977 | tf_op jit(solution)/shard_map/convert_element_type | solution.py:199
  (52 shorter events, 0.7 us)
Async XLA Ops:
  0.6 6.2 %copy-start.4 = (bf16[4,4096]{1,0:T(4,128)(2,1)S(1)}, bf16[4,4096]{1,0:T(4,128)(2,1)}, u32[]{:S(2)}) copy-start(bf16[4,4096]{1,0:T(4,128)(2,1)} %param.8) | copy-start | bytes 98308
  0.6 9.3 %copy-start.5 = (bf16[4,4096]{1,0:T(4,128)(2,1)S(1)}, bf16[4,4096]{1,0:T(4,128)(2,1)}, u32[]{:S(2)}) copy-start(bf16[4,4096]{1,0:T(4,128)(2,1)} %param.10) | copy-start | bytes 98308
  0.7 6.2 %collective-permute-start = (bf16[4,4096]{1,0:T(4,128)(2,1)}, bf16[4,4096]{1,0:T(4,128)(2,1)S(1)}, u32[]{:S(2)}, u32[]{:S(2)}) collective-permute-start(bf16[4,4096]{1,0:T(4,128)(2,1)} %param.8), channel_id=1, source_target_pairs={{0,8},{1,3},{2,10},{3,1},{4,12},{5,7},{6,14},{7,5},{8,0},{9,11},{1... | collective-permute-start | bytes 98312 | tf_op jit(solution)/shard_map/ppermute | solution.py:85
  4.8 5.2 %collective-permute-start.15 = (bf16[4,4096]{1,0:T(4,128)(2,1)}, bf16[4,4096]{1,0:T(4,128)(2,1)S(1)}, u32[]{:S(2)}, u32[]{:S(2)}) collective-permute-start(bf16[4,4096]{1,0:T(4,128)(2,1)} %param.10), channel_id=1, source_target_pairs={{0,8},{1,3},{2,10},{3,1},{4,12},{5,7},{6,14},{7,5},{8,0},{9,11},{1... | collective-permute-start | bytes 98312 | tf_op jit(solution)/shard_map/ppermute | solution.py:85
  6.9 4.8 %collective-permute-start.1 = (bf16[8,4096]{1,0:T(8,128)(2,1)S(1)}, bf16[8,4096]{1,0:T(8,128)(2,1)S(1)}, u32[]{:S(2)}, u32[]{:S(2)}) collective-permute-start(bf16[8,4096]{1,0:T(8,128)(2,1)S(1)} %maximum_select_fusion.6), channel_id=1, source_target_pairs={{0,4},{1,9},{2,6},{3,11},{4,0},{5,13},{6,2},{7,15},{8,12},{9,1},{1... | collective-permute-start | bytes 196616 | tf_op jit(solution)/shard_map/ppermute | solution.py:85
  10.0 7.1 %collective-permute-start.16 = (bf16[8,4096]{1,0:T(8,128)(2,1)S(1)}, bf16[8,4096]{1,0:T(8,128)(2,1)S(1)}, u32[]{:S(2)}, u32[]{:S(2)}) collective-permute-start(bf16[8,4096]{1,0:T(8,128)(2,1)S(1)} %maximum_select_fusion.7), channel_id=1, source_target_pairs={{0,4},{1,9},{2,6},{3,11},{4,0},{5,13},{6,2},{7,15},{8,12},{9,1},{1... | collective-permute-start | bytes 196616 | tf_op jit(solution)/shard_map/ppermute | solution.py:85
  11.7 8.3 %copy-start.1 = (bf16[512,4096]{1,0:T(8,128)(2,1)S(1)}, bf16[512,4096]{1,0:T(8,128)(2,1)}, u32[]{:S(2)}) copy-start(bf16[512,4096]{1,0:T(8,128)(2,1)} %table_h.1) | copy-start | bytes 12582916
  11.7 8.3 %copy-start.2 = (bf16[64,512]{1,0:T(8,128)(2,1)S(1)}, bf16[64,512]{1,0:T(8,128)(2,1)}, u32[]{:S(2)}) copy-start(bf16[64,512]{1,0:T(8,128)(2,1)} %get-tuple-element.38) | copy-start | bytes 196612
  11.7 5.4 %collective-permute-start.2 = (bf16[16,4096]{1,0:T(8,128)(2,1)S(1)}, bf16[16,4096]{1,0:T(8,128)(2,1)S(1)}, u32[]{:S(2)}, u32[]{:S(2)}) collective-permute-start(bf16[16,4096]{1,0:T(8,128)(2,1)S(1)} %maximum_select_fusion.4), channel_id=1, source_target_pairs={{0,2},{1,5},{2,0},{3,7},{4,6},{5,1},{6,4},{7,3},{8,10},{9,13},{10,... | collective-permute-start | bytes 393224 | tf_op jit(solution)/shard_map/ppermute | solution.py:85
  17.0 2.1 %collective-permute-start.10 = (bf16[32,4096]{1,0:T(8,128)(2,1)S(1)}, bf16[32,4096]{1,0:T(8,128)(2,1)S(1)}, u32[]{:S(2)}, u32[]{:S(2)}) collective-permute-start(bf16[32,4096]{1,0:T(8,128)(2,1)S(1)} %slice.133), channel_id=1, source_target_pairs={{0,1},{1,0},{2,3},{3,2},{4,5},{5,4},{6,7},{7,6},{8,9},{9,8},{10,11... | collective-permute-start | bytes 786440 | tf_op jit(solution)/shard_map/ppermute | solution.py:85
  17.2 2.7 %collective-permute-start.3 = (bf16[32,4096]{1,0:T(8,128)(2,1)S(1)}, bf16[32,4096]{1,0:T(8,128)(2,1)S(1)}, u32[]{:S(2)}, u32[]{:S(2)}) collective-permute-start(bf16[32,4096]{1,0:T(8,128)(2,1)S(1)} %maximum_select_fusion.2), channel_id=1, source_target_pairs={{0,1},{1,0},{2,3},{3,2},{4,5},{5,4},{6,7},{7,6},{8,9},{9,8},{10,11... | collective-permute-start | bytes 786440 | tf_op jit(solution)/shard_map/ppermute | solution.py:85
  17.7 5.6 %collective-permute-start.17 = (bf16[16,4096]{1,0:T(8,128)(2,1)S(1)}, bf16[16,4096]{1,0:T(8,128)(2,1)S(1)}, u32[]{:S(2)}, u32[]{:S(2)}) collective-permute-start(bf16[16,4096]{1,0:T(8,128)(2,1)S(1)} %maximum_select_fusion.5), channel_id=1, source_target_pairs={{0,2},{1,5},{2,0},{3,7},{4,6},{5,1},{6,4},{7,3},{8,10},{9,13},{10,... | collective-permute-start | bytes 393224 | tf_op jit(solution)/shard_map/ppermute | solution.py:85
  19.1 5.6 %collective-permute-start.11 = (bf16[16,4096]{1,0:T(8,128)(2,1)S(1)}, bf16[16,4096]{1,0:T(8,128)(2,1)S(1)}, u32[]{:S(2)}, u32[]{:S(2)}) collective-permute-start(bf16[16,4096]{1,0:T(8,128)(2,1)S(1)} %broadcast_select_fusion), channel_id=1, source_target_pairs={{0,2},{1,5},{2,0},{3,7},{4,6},{5,1},{6,4},{7,3},{8,10},{9,13},{10,... | collective-permute-start | bytes 393224 | tf_op jit(solution)/shard_map/ppermute | solution.py:85
  21.7 1.6 %collective-permute-start.4 = (f32[3,64]{1,0:T(4,128)S(1)}, f32[3,64]{1,0:T(4,128)S(1)}, u32[]{:S(2)}, u32[]{:S(2)}) collective-permute-start(f32[3,64]{1,0:T(4,128)S(1)} %pad_maximum_fusion.1), channel_id=1, source_target_pairs={{0,1},{1,0},{2,3},{3,2},{4,5},{5,4},{6,7},{7,6},{8,9},{9,8},{10,11... | collective-permute-start | bytes 2312 | tf_op jit(solution)/shard_map/ppermute | solution.py:85
  22.7 20.4 %copy-start.3 = (f32[64,512]{1,0:T(8,128)S(1)}, f32[64,512]{1,0:T(8,128)}, u32[]{:S(2)}) copy-start(f32[64,512]{1,0:T(8,128)} %get-tuple-element.70) | copy-start | bytes 393220
  22.7 20.5 %copy-start.6 = (f32[64]{0:T(128)S(1)}, f32[64]{0:T(128)}, u32[]{:S(2)}) copy-start(f32[64]{0:T(128)} %param.15) | copy-start | bytes 772
  22.7 20.8 %copy-start = (bf16[64,512]{1,0:T(8,128)(2,1)S(1)}, bf16[64,512]{1,0:T(8,128)(2,1)}, u32[]{:S(2)}) copy-start(bf16[64,512]{1,0:T(8,128)(2,1)} %get-tuple-element.71.took) | copy-start | bytes 196612
  22.8 1.7 %collective-permute-start.5 = (bf16[32,4096]{1,0:T(8,128)(2,1)S(1)}, bf16[32,4096]{1,0:T(8,128)(2,1)S(1)}, u32[]{:S(2)}, u32[]{:S(2)}) collective-permute-start(bf16[32,4096]{1,0:T(8,128)(2,1)S(1)} %select_convert_fusion), channel_id=1, source_target_pairs={{0,1},{1,0},{2,3},{3,2},{4,5},{5,4},{6,7},{7,6},{8,9},{9,8},{10,11... | collective-permute-start | bytes 786440 | tf_op jit(solution)/shard_map/ppermute | solution.py:85
  23.6 16.7 %collective-permute-start.18 = (bf16[32,4096]{1,0:T(8,128)(2,1)S(1)}, bf16[32,4096]{1,0:T(8,128)(2,1)S(1)}, u32[]{:S(2)}, u32[]{:S(2)}) collective-permute-start(bf16[32,4096]{1,0:T(8,128)(2,1)S(1)} %maximum_select_fusion.3), channel_id=1, source_target_pairs={{0,1},{1,0},{2,3},{3,2},{4,5},{5,4},{6,7},{7,6},{8,9},{9,8},{10,11... | collective-permute-start | bytes 786440 | tf_op jit(solution)/shard_map/ppermute | solution.py:85
  24.7 3.7 %collective-permute-start.6 = (f32[3,64]{1,0:T(4,128)S(1)}, f32[3,64]{1,0:T(4,128)S(1)}, u32[]{:S(2)}, u32[]{:S(2)}) collective-permute-start(f32[3,64]{1,0:T(4,128)S(1)} %pad_maximum_fusion.2), channel_id=1, source_target_pairs={{0,2},{1,5},{2,0},{3,7},{4,6},{5,1},{6,4},{7,3},{8,10},{9,13},{10,... | collective-permute-start | bytes 2312 | tf_op jit(solution)/shard_map/ppermute | solution.py:85
  26.1 6.0 %collective-permute-start.12 = (bf16[8,4096]{1,0:T(8,128)(2,1)S(1)}, bf16[8,4096]{1,0:T(8,128)(2,1)S(1)}, u32[]{:S(2)}, u32[]{:S(2)}) collective-permute-start(bf16[8,4096]{1,0:T(8,128)(2,1)S(1)} %broadcast_select_fusion.1), channel_id=1, source_target_pairs={{0,4},{1,9},{2,6},{3,11},{4,0},{5,13},{6,2},{7,15},{8,12},{9,1},{1... | collective-permute-start | bytes 196616 | tf_op jit(solution)/shard_map/ppermute | solution.py:85
  27.1 5.0 %collective-permute-start.7 = (bf16[16,4096]{1,0:T(8,128)(2,1)S(1)}, bf16[16,4096]{1,0:T(8,128)(2,1)S(1)}, u32[]{:S(2)}, u32[]{:S(2)}) collective-permute-start(bf16[16,4096]{1,0:T(8,128)(2,1)S(1)} %select_convert_fusion.1), channel_id=1, source_target_pairs={{0,2},{1,5},{2,0},{3,7},{4,6},{5,1},{6,4},{7,3},{8,10},{9,13},{10,... | collective-permute-start | bytes 393224 | tf_op jit(solution)/shard_map/ppermute | solution.py:85
  32.2 3.7 %collective-permute-start.8 = (f32[3,64]{1,0:T(4,128)S(1)}, f32[3,64]{1,0:T(4,128)S(1)}, u32[]{:S(2)}, u32[]{:S(2)}) collective-permute-start(f32[3,64]{1,0:T(4,128)S(1)} %pad_maximum_fusion.3), channel_id=1, source_target_pairs={{0,4},{1,9},{2,6},{3,11},{4,0},{5,13},{6,2},{7,15},{8,12},{9,1},{1... | collective-permute-start | bytes 2312 | tf_op jit(solution)/shard_map/ppermute | solution.py:85
  33.5 4.9 %collective-permute-start.9 = (bf16[8,4096]{1,0:T(8,128)(2,1)S(1)}, bf16[8,4096]{1,0:T(8,128)(2,1)S(1)}, u32[]{:S(2)}, u32[]{:S(2)}) collective-permute-start(bf16[8,4096]{1,0:T(8,128)(2,1)S(1)} %select_convert_fusion.3), channel_id=1, source_target_pairs={{0,4},{1,9},{2,6},{3,11},{4,0},{5,13},{6,2},{7,15},{8,12},{9,1},{1... | collective-permute-start | bytes 196616 | tf_op jit(solution)/shard_map/ppermute | solution.py:85
  38.5 4.5 %collective-permute-start.13 = (f32[3,64]{1,0:T(4,128)S(1)}, f32[3,64]{1,0:T(4,128)S(1)}, u32[]{:S(2)}, u32[]{:S(2)}) collective-permute-start(f32[3,64]{1,0:T(4,128)S(1)} %pad_maximum_fusion.4), channel_id=1, source_target_pairs={{0,8},{1,3},{2,10},{3,1},{4,12},{5,7},{6,14},{7,5},{8,0},{9,11},{1... | collective-permute-start | bytes 2312 | tf_op jit(solution)/shard_map/ppermute | solution.py:85
  40.4 5.5 %collective-permute-start.14 = (bf16[8,4096]{1,0:T(8,128)(2,1)S(1)}, bf16[8,4096]{1,0:T(8,128)(2,1)S(1)}, u32[]{:S(2)}, u32[]{:S(2)}) collective-permute-start(bf16[8,4096]{1,0:T(8,128)(2,1)S(1)} %pad_maximum_fusion), channel_id=1, source_target_pairs={{0,8},{1,3},{2,10},{3,1},{4,12},{5,7},{6,14},{7,5},{8,0},{9,11},{1... | collective-permute-start | bytes 196616 | tf_op jit(solution)/shard_map/ppermute | solution.py:85
